TPU v7x, 256 devices: a whole 4x4x8 slice. The times are simulated.
256 devices in a mesh: dp: 4 (over x), psg: 32 (over y, z), tp: 2 (over core).
Axes of the slice: x: 4, y: 4, z: 8, core: 2. Of those that a mesh axis runs over, the one named last changes fastest.
Arguments:
- enc_states: bfloat16 [4, 96, 256, 4096], P('dp', 'psg'), may hold values from -6 to 6
- lengths: int32 [4, 96], P('dp', 'psg'), may hold values from 16 to 256
- enc_gain: bfloat16 [4096], replicated, may hold values from 0.099609375 to 1.8984375
- dec_states: bfloat16 [4, 32, 4096], P('dp'), may hold values from -360 to 360
- w_query: bfloat16 [4096, 2048], P('psg', 'tp'), may hold values from -0.09375 to 0.09375
- w_key: bfloat16 [4096, 2048], P('psg', 'tp'), may hold values from -0.09375 to 0.09375
- w_value: bfloat16 [4096, 2048], P('psg', 'tp'), may hold values from -0.09375 to 0.09375
- w_out: bfloat16 [2048, 4096], P('tp', 'psg'), may hold values from -0.125 to 0.125
Outputs:
- attended: bfloat16 [4, 32, 4096], P('dp', None, 'psg')
- scores: float32 [4, 96], P('dp', 'psg')
All inputs are finite; a program needn't handle non-finite values.
Results may differ from a plain program's by a relative error of at most 0.014.
The roundings to bfloat16 on the way count: a program that leaves them out, or rounds other values in their place, can miss the bound.
Values may be sent and summed in bfloat16 or wider, within the bound.
No kernel may reach another device: no remote copies, remote signals or barrier semaphores. Data moves between devices by JAX's collectives and lax.ppermute only.
A program may use at most 128 MiB of HBM per device.

v0:
```python
import jax
import jax.numpy as jnp
from jax import lax
from jax.sharding import PartitionSpec as P

HEADS = 32
HDIM = 64


def body(enc_states, lengths, enc_gain, dec_states, w_query, w_key, w_value, w_out):
    qdev, pdev, plen, width = enc_states.shape
    answers = dec_states.shape[1]
    columns = w_key.shape[1]
    local_heads = columns // HDIM
    e32 = enc_states.astype(jnp.float32)
    scale = lax.rsqrt(jnp.mean(e32 * e32, axis=-1, keepdims=True) + 1e-06)
    normed = (e32 * scale * enc_gain.astype(jnp.float32)).astype(jnp.bfloat16)
    normed = normed.reshape(qdev * pdev * plen, width)
    dec_flat = dec_states.reshape(qdev * answers, width)

    def add_rows(left, piece):
        return jnp.dot(left, piece, preferred_element_type=jnp.float32)

    keys32 = add_rows(normed, lax.all_gather(w_key, "psg", axis=0, tiled=True))
    values32 = add_rows(normed, lax.all_gather(w_value, "psg", axis=0, tiled=True))
    query32 = add_rows(dec_flat, lax.all_gather(w_query, "psg", axis=0, tiled=True))
    keys = keys32.astype(jnp.bfloat16).reshape(qdev, pdev * plen, local_heads, HDIM)
    values = values32.astype(jnp.bfloat16).reshape(qdev, pdev * plen, local_heads, HDIM)
    queries = query32.astype(jnp.bfloat16).reshape(qdev, answers, local_heads, HDIM)
    logits = jnp.einsum(
        "qahe,qkhe->qhak", queries, keys, preferred_element_type=jnp.float32
    ) * HDIM ** (-0.5)
    valid = (jnp.arange(plen, dtype=jnp.int32)[None, None, :] < lengths[:, :, None]).reshape(
        qdev, 1, 1, pdev * plen
    )
    masked = jnp.where(valid, logits, -1e30)
    local_max = jnp.max(masked, axis=-1)
    values_wide = values.astype(jnp.float32)
    top = lax.pmax(local_max, "psg")
    weights = jnp.where(valid, jnp.exp(masked - top[..., None]), 0.0)
    part_total = jnp.sum(weights, axis=-1)
    part_numer = jnp.einsum("qhak,qkhe->qhae", weights, values_wide)
    total, numer = lax.psum((part_total, part_numer), "psg")
    share = weights / total[..., None]
    mass = jnp.sum(share.reshape(qdev, local_heads, answers, pdev, plen), axis=(1, 2, 4))
    context = numer / total[..., None]
    context = (
        jnp.transpose(context, (0, 2, 1, 3)).reshape(qdev, answers, columns).astype(jnp.bfloat16)
    )
    partial_out = jnp.einsum("qac,cd->qad", context, w_out, preferred_element_type=jnp.float32)
    out_sum, mass_sum = lax.psum((partial_out, mass), "tp")
    passages_all = pdev * lax.axis_size("psg")
    scores = mass_sum * (passages_all / (HEADS * answers))
    return (out_sum.astype(jnp.bfloat16), scores)


def solution(mesh):
    placed = (
        P("dp", "psg", None, None),
        P("dp", "psg"),
        P(),
        P("dp", None, None),
        P("psg", "tp"),
        P("psg", "tp"),
        P("psg", "tp"),
        P("tp", "psg"),
    )
    return jax.shard_map(
        body,
        mesh=mesh,
        in_specs=placed,
        out_specs=(P("dp", None, "psg"), P("dp", "psg")),
        check_vma=False,
    )
```

profile of v0, /device:TPU:1, one launch (start us, length us, event | category | flops | bytes accessed | tf_op | source)
XLA Modules:
  0.0 541.4 jit_solution(13770672056811224082)
XLA Ops:
  7.2 0.7 all-gather.8.cloned.1.call-update
  8.0 0.7 all-gather.6.cloned.1.call-update
  8.7 0.7 all-gather.4.cloned.1.call-update
  9.4 0.0 all-reduce.3.cloned.1.call-start
  9.4 0.7 convert_element_type.36
  10.2 0.7 broadcast_reduce_fusion
  10.9 4.2 fusion
  15.2 0.4 copy-done.1
  15.5 5.4 %fusion.2 = bf16[1,3,256,4096]{3,2,1,0:T(8,128)(2,1)} fusion(bf16[1,3,256,4096]{3,2,1,0:T(8,128)(2,1)S(1)} %copy-done.1, f32[4096]{0:T(1024)S(1)} %convert_element_type.36, f32[3,256]{1,0:T(4,128)S(1)} %add_rsqrt_fusion), kind=kLoop, calls=%fused_computation.4 | loop fusion | flops 12582912 | bytes 12602368 | tf_op jit(solution)/shard_map/convert_element_type | solution.py:17
  20.9 91.6 %all-gather.8.cloned.1.call-done = bf16[4096,1024]{1,0:T(8,128)(2,1)} async-done(((bf16[128,1024]{1,0:T(8,128)(2,1)}), bf16[4096,1024]{1,0:T(8,128)(2,1)}) %all-gather.8.cloned.1.call-update) | async-done | bytes 8388624 | tf_op jit(solution)/shard_map/all_gather | solution.py:25
  112.5 10.9 %convolution_convert_fusion = bf16[768,1024]{1,0:T(8,128)(2,1)S(1)} fusion(bf16[768,4096]{1,0:T(8,128)(2,1)} %bitcast.25, bf16[4096,1024]{1,0:T(8,128)(2,1)} %all-gather.8.cloned.1.call-done), kind=kOutput, calls=%fused_computation.5 | convolution fusion | flops 6443237376 | bytes 16252928 | tf_op jit(solution)/shard_map/dot_general | solution.py:22
  123.5 0.7 copy.19
  124.2 86.6 %all-gather.6.cloned.1.call-done = bf16[4096,1024]{1,0:T(8,128)(2,1)} async-done(((bf16[128,1024]{1,0:T(8,128)(2,1)}), bf16[4096,1024]{1,0:T(8,128)(2,1)}) %all-gather.6.cloned.1.call-update) | async-done | bytes 8388624 | tf_op jit(solution)/shard_map/all_gather | solution.py:24
  210.7 10.9 %convolution_convert_fusion.1 = bf16[768,1024]{1,0:T(8,128)(2,1)S(1)} fusion(bf16[768,4096]{1,0:T(8,128)(2,1)} %bitcast.26, bf16[4096,1024]{1,0:T(8,128)(2,1)} %all-gather.6.cloned.1.call-done), kind=kOutput, calls=%fused_computation.6 | convolution fusion | flops 6443237376 | bytes 16252928 | tf_op jit(solution)/shard_map/dot_general | solution.py:22
  221.7 1.6 copy.17
  223.3 85.7 %all-gather.4.cloned.1.call-done = bf16[4096,1024]{1,0:T(8,128)(2,1)} async-done(((bf16[128,1024]{1,0:T(8,128)(2,1)}), bf16[4096,1024]{1,0:T(8,128)(2,1)}) %all-gather.4.cloned.1.call-update) | async-done | bytes 8388624 | tf_op jit(solution)/shard_map/all_gather | solution.py:26
  309.0 4.9 convolution_convert_fusion.2
  313.9 0.1 reshape.97
  314.1 1.9 fusion.11
  315.9 58.6 %pmax.7 = f32[16,32]{1,0:T(8,128)S(1)} all-reduce(f32[16,32]{1,0:T(8,128)S(1)} %get-tuple-element.4), channel_id=1, replica_groups=mesh['dp'=4,'psg'=32,'tp'=2] {'psg'}, use_global_device_ids=true, to_apply=%region_2.3 | all-reduce | flops 512 | bytes 4096 | tf_op jit(solution)/shard_map/pmax | solution.py:39
  374.6 0.4 fusion.3
  375.0 1.3 convolution_bitcast_fusion
  376.3 57.2 %psum.29 = f32[16,32]{1,0:T(8,128)S(1)} all-reduce(f32[16,32]{1,0:T(8,128)S(1)} %fusion.3), channel_id=1, replica_groups=mesh['dp'=4,'psg'=32,'tp'=2] {'psg'}, use_global_device_ids=true, to_apply=%region_5.6 | all-reduce | flops 512 | bytes 4096 | tf_op jit(solution)/shard_map/psum | solution.py:43
  433.6 0.4 divide_reduce_fusion
  434.0 0.1 reduce_sum.43
  434.1 89.8 %all-reduce.3.cloned.1.call-done = f32[1,16,32,64]{3,2,1,0:T(8,128)} async-done(((f32[1,16,32,64]{3,2,1,0:T(8,128)}), f32[1,16,32,64]{3,2,1,0:T(8,128)}) %all-reduce.3.cloned.1.call-update) | async-done | bytes 131088 | tf_op jit(solution)/shard_map/psum | solution.py:43
  523.9 1.1 fusion.9
  525.0 0.1 copy.20
  525.1 0.1 convert_element_type.42
  525.2 0.2 convolution_bitcast_fusion.1
  525.4 8.9 %all-reduce = (bf16[1,32,128]{2,1,0:T(8,128)(2,1)}, f32[1,3]{1,0:T(1,128)S(1)}) all-reduce(f32[1,32,128]{2,1,0:T(8,128)S(1)} %convolution_bitcast_fusion.1, f32[1,3]{1,0:T(1,128)S(1)} %bitcast.29), channel_id=1, replica_groups=mesh['dp'=4,'psg'=32,'tp'=2] {'tp'}, use_global_device_ids=true, to_apply=%region_6.7 | all-reduce | flops 4099 | bytes 24600 | tf_op jit(solution)/shard_map/psum | solution.py:51
  534.3 0.5 broadcast_multiply_fusion
  (15 shorter events, 0.2 us)
Async XLA Ops:
  7.2 301.8 %copy-start = (bf16[1,32,4096]{2,1,0:T(8,128)(2,1)S(1)}, bf16[1,32,4096]{2,1,0:T(8,128)(2,1)}, u32[]{:S(2)}) copy-start(bf16[1,32,4096]{2,1,0:T(8,128)(2,1)} %param.11) | copy-start | bytes 786436
  7.2 105.4 %all-gather.8.cloned.1.call-start = ((), (), s32[]{:S(2)}) async-start(), calls=%async_computation.2 | async-start | bytes 8650752 | tf_op jit(solution)/shard_map/all_gather | solution.py:25
  7.9 202.8 %all-gather.6.cloned.1.call-start = ((), (), s32[]{:S(2)}) async-start(), calls=%async_computation.1 | async-start | bytes 8650752 | tf_op jit(solution)/shard_map/all_gather | solution.py:24
  8.7 300.3 %all-gather.4.cloned.1.call-start = ((), (), s32[]{:S(2)}) async-start(), calls=%async_computation | async-start | bytes 8650752 | tf_op jit(solution)/shard_map/all_gather | solution.py:26
  9.4 514.5 %all-reduce.3.cloned.1.call-start = ((), (), s32[]{:S(2)}) async-start(), calls=%async_computation.3 | async-start | bytes 524288 | tf_op jit(solution)/shard_map/psum | solution.py:43
  10.9 4.6 copy-start.1
  376.3 148.9 %copy-start.2 = (bf16[1024,128]{1,0:T(8,128)(2,1)S(1)}, bf16[1024,128]{1,0:T(8,128)(2,1)}, u32[]{:S(2)}) copy-start(bf16[1024,128]{1,0:T(8,128)(2,1)} %param.15) | copy-start | bytes 786436
Sparse Core Ops, SparseCore 0:
  10.6 101.8 all-gather.7
  115.1 95.5 all-gather.5
  213.3 95.5 all-gather.3
  376.5 147.4 all-reduce.2
where the time goes:
time: 542 us; the launch traced here: 541 us
  waiting for transfers between devices  356 us (66%)
  blocking collectives  125 us (23%)
  matrix products  30.1 us (6%)
  between operations  13.9 us (3%)
  other arithmetic  12.9 us (2%)
    all_gather x1, waiting for transfers between devices, body(): lax.all_gather(w_value, 'psg', axis=0, tiled=True)  91.6 us
    psum x1, waiting for transfers between devices, body(): total, numer = lax.psum((part_total, part_numer), 'psg')  89.8 us
    all_gather x1, waiting for transfers between devices, body(): keys32 = add_rows(normed, lax.all_gather(w_key, 'psg', axis=0, tiled=True))  86.6 us
    all_gather x1, waiting for transfers between devices, body(): lax.all_gather(w_query, 'psg', axis=0, tiled=True)  85.7 us
    pmax x1, blocking collectives, body(): top = lax.pmax(local_max, 'psg')  58.6 us
    psum x1, blocking collectives, body(): total, numer = lax.psum((part_total, part_numer), 'psg')  57.2 us
    dot_general x3, matrix products, add_rows(): return jnp.dot(left, piece, preferred_element_type=jnp.float32)  26.7 us
  transfers between devices with their start and end apart: 4, of which 4 were waited for; matrix products, arithmetic and copies ran while one was open for 7% of the time, Pallas kernels for 0%

commit v1 on v0

v1 whole, which is shorter than its diff:
```python
import functools

import jax
import jax.numpy as jnp
from jax import lax
from jax.experimental import pallas as pl
from jax.experimental.pallas import tpu as pltpu
from jax.sharding import Mesh, PartitionSpec as P

HEADS = 32
HDIM = 64
NX = 4
NY = 4
NZ = 8
LANES = 128
PSG = ("y", "z")
SIZES = {"dp": NX, "y": NY, "z": NZ}
VMEM = pl.BlockSpec(memory_space=pltpu.VMEM)
SMEM = pl.BlockSpec(memory_space=pltpu.SMEM)
HBM = pl.BlockSpec(memory_space=pltpu.HBM)
f32 = jnp.float32
bf16 = jnp.bfloat16

GROUPS = ((0, 1, 7), (2, 6, 3, 5, 4))
ORDER = [(dy, dz) for group in GROUPS for dz in group for dy in range(NY)]


def shaped(shape, dtype=f32):
    return jax.ShapeDtypeStruct(shape, dtype)


def params(mib):
    return pltpu.CompilerParams(vmem_limit_bytes=mib * 1024 * 1024)


def call(kernel, outs, scratch, *args, mib=16, flops=0, hbm=()):
    specs = [SMEM] + [HBM if i in hbm else VMEM for i in range(1, len(args))]
    return pl.pallas_call(
        kernel,
        out_shape=outs,
        in_specs=specs,
        out_specs=jax.tree.map(lambda _: VMEM, outs),
        scratch_shapes=scratch,
        compiler_params=params(mib),
        cost_estimate=pl.CostEstimate(flops=flops, bytes_accessed=1 << 20, transcendentals=0),
    )(*args)


def recv(a, axis, k):
    n = SIZES[axis]
    return lax.ppermute(a, axis, [((i + k) % n, i) for i in range(n)])


def exchange(a):
    return lax.all_to_all(a, PSG, split_axis=0, concat_axis=0, tiled=True)


def round_x(group):
    half = group.shape[0] // 2
    up, down = recv(group, "dp", 1), recv(group, "dp", -1)
    far = [recv(up[:half], "dp", 1), recv(down[half:], "dp", -1)]
    return [[group], [up], far, [down]]


def gather(shard):
    block = jnp.concatenate(
        [shard, recv(shard, "y", 1), recv(shard, "y", 2), recv(shard, "y", -1)], axis=0
    )
    half = block.shape[0] // 2
    up1, down1 = recv(block, "z", 1), recv(block, "z", -1)
    near = round_x(jnp.concatenate([block, up1, down1], axis=0))
    up2, down2 = recv(up1, "z", 1), recv(down1, "z", -1)
    up3, down3 = recv(up2, "z", 1), recv(down2, "z", -1)
    after = (near[1][0][0, 0] + near[3][0][0, 0]) * 0
    far = (recv(up3[:half] + after, "z", 1), recv(down3[half:] + after, "z", -1))
    rest = round_x(jnp.concatenate([up2, down2, up3, down3, *far], axis=0))
    return [near[dx] + rest[dx] for dx in range(NX)]


def norm_kernel(pos, e_ref, gain_ref, plain_ref, turned_ref):
    e = e_ref[...].astype(f32)
    scale = lax.rsqrt(jnp.mean(e * e, axis=-1, keepdims=True) + 1e-06)
    plain_ref[...] = (e * scale * gain_ref[...].astype(f32)).astype(bf16)
    for i, (dy, dz) in enumerate(ORDER):
        at = lax.rem(pos[0] + dy, NY) * NZ + lax.rem(pos[1] + dz, NZ)
        turned_ref[:, i * LANES : (i + 1) * LANES] = plain_ref[
            :, pl.ds(pl.multiple_of(at * LANES, LANES), LANES)
        ]


def normalise(pos, enc, gain, tile):
    rows, width = enc.shape
    block = pl.BlockSpec((tile, width), lambda i, pos: (i, 0))
    return pl.pallas_call(
        norm_kernel,
        out_shape=[shaped((rows, width), bf16)] * 2,
        grid_spec=pltpu.PrefetchScalarGridSpec(
            num_scalar_prefetch=1,
            grid=(rows // tile,),
            in_specs=[block, pl.BlockSpec((1, width), lambda i, pos: (0, 0))],
            out_specs=[block, block],
        ),
        compiler_params=params(32),
        cost_estimate=pl.CostEstimate(
            flops=6 * rows * width, bytes_accessed=6 * rows * width, transcendentals=0
        ),
    )(pos, enc, gain)


def project_kernel(x_ref, *refs):
    pieces, out_ref = refs[:-1], refs[-1]
    acc, at = None, 0
    for ref in pieces:
        depth = ref.shape[0]
        part = jnp.dot(x_ref[:, at : at + depth], ref[...], preferred_element_type=f32)
        acc = part if acc is None else acc + part
        at += depth
    out_ref[...] = acc.astype(bf16)


def project(x, pieces):
    rows, width = x.shape
    cols = pieces[0].shape[1]
    return pl.pallas_call(
        project_kernel,
        out_shape=shaped((rows, cols), bf16),
        in_specs=[VMEM] * (1 + len(pieces)),
        out_specs=VMEM,
        compiler_params=params(16),
        cost_estimate=pl.CostEstimate(
            flops=2 * rows * width * cols,
            bytes_accessed=2 * (rows * width + width * cols + rows * cols),
            transcendentals=0,
        ),
    )(x, *pieces)


def query_kernel(pos, dec_ref, w_ref, out_ref):
    at = pl.multiple_of((pos[0] * NZ + pos[1]) * LANES, LANES)
    part = jnp.dot(dec_ref[:, pl.ds(at, LANES)], w_ref[...], preferred_element_type=f32)
    for j in range(out_ref.shape[1]):
        out_ref[:, j, :] = part[:, j * LANES : (j + 1) * LANES]


def spread_kernel(pos, got_ref, out_ref):
    total = jnp.sum(got_ref[...], axis=0, keepdims=True)
    out_ref[...] = jnp.broadcast_to(total, out_ref.shape)


def summed(pos, parts):
    return exchange(call(spread_kernel, shaped(parts.shape), [], pos, exchange(parts)))


def same_head(rows, cols, answers):
    row = lax.broadcasted_iota(jnp.int32, (rows, cols), 0) // answers
    col = lax.broadcasted_iota(jnp.int32, (rows, cols), 1) // HDIM
    return row == col


def logits_kernel(plen, pos, q_ref, *refs):
    keys, (high_ref, low_ref, stat_ref, copies_ref, tile_ref) = refs[:NX], refs[NX:]
    answers = q_ref.shape[0]
    for dx, key_ref in enumerate(keys):
        quarter = lax.rem(pos[2] + dx, NX)
        slots, cols = key_ref.shape
        pairs = cols // HDIM * answers
        blocks = cols // LANES
        q = jnp.concatenate(
            [q_ref[:, pl.ds(quarter * blocks + j, 1), :].reshape(answers, LANES) for j in range(blocks)],
            axis=1,
        )
        spread = jnp.where(
            same_head(pairs, cols, answers), jnp.concatenate([q] * (cols // HDIM), axis=0), 0.0
        ).astype(bf16)
        logits = lax.dot_general(
            spread, key_ref[...], (((1,), (1,)), ((), ())), preferred_element_type=f32
        ) * HDIM ** (-0.5)
        token = lax.broadcasted_iota(jnp.int32, (pairs, plen), 1)
        passages = slots // plen
        valid = [token < pos[3 + i] for i in range(passages)]
        masked = [
            jnp.where(valid[i], logits[:, i * plen : (i + 1) * plen], -1e30) for i in range(passages)
        ]
        top = functools.reduce(
            jnp.maximum, [jnp.max(m, axis=1, keepdims=True) for m in masked]
        )
        at = pl.ds(pl.multiple_of(quarter * pairs, pairs), pairs)
        lane = lax.broadcasted_iota(jnp.int32, (pairs, LANES), 1)
        tile = jnp.where(lane == 0, top, 0.0)
        total = jnp.zeros_like(top)
        for i in range(passages):
            p = jnp.where(valid[i], jnp.exp(masked[i] - top), 0.0)
            high = p.astype(bf16)
            high_ref[at, i * plen : (i + 1) * plen] = high
            low_ref[at, i * plen : (i + 1) * plen] = (p - high.astype(f32)).astype(bf16)
            part = jnp.sum(p, axis=1, keepdims=True)
            total = total + part
            tile = jnp.where(lane == 2 + i, part, tile)
        tile_ref[at, :] = jnp.where(lane == 1, total, tile)
    stat_ref[...] = jnp.transpose(tile_ref[...])[0:8, :]
    copies_ref[...] = jnp.broadcast_to(stat_ref[0:2, :][None], copies_ref.shape)


def weigh_kernel(high_ref, low_ref, x_ref, u_ref):
    total = jnp.dot(high_ref[...], x_ref[...], preferred_element_type=f32)
    total += jnp.dot(low_ref[...], x_ref[...], preferred_element_type=f32)
    high = total.astype(bf16)
    low = (total - high.astype(f32)).astype(bf16)
    per = total.shape[0] // NX
    for g in range(NX):
        at = slice(g * per, (g + 1) * per)
        u_ref[2 * g * per : (2 * g + 1) * per, :] = high[at, :]
        u_ref[(2 * g + 1) * per : (2 * g + 2) * per, :] = low[at, :]


def weigh(high, low, x, tile):
    pairs, slots = high.shape
    width = x.shape[1]
    whole = pl.BlockSpec((pairs, slots), lambda i: (0, 0))
    return pl.pallas_call(
        weigh_kernel,
        out_shape=shaped((2 * pairs, width), bf16),
        grid=(width // tile,),
        in_specs=[whole, whole, pl.BlockSpec((slots, tile), lambda i: (0, i))],
        out_specs=pl.BlockSpec((2 * pairs, tile), lambda i: (0, i)),
        compiler_params=params(24),
        cost_estimate=pl.CostEstimate(
            flops=4 * pairs * slots * width, bytes_accessed=1 << 24, transcendentals=0
        ),
    )(high, low, x)


def numer_kernel(pos, own_ref, stats_ref, u_ref, v_hbm, out_ref, mass_ref, buf, acc, sems):
    chunks, depth, columns = buf.shape
    answers = out_ref.shape[0]
    cols = columns // NX
    per = u_ref.shape[0] // NX

    def fetch(i):
        return pltpu.make_async_copy(v_hbm.at[pl.ds(i * depth, depth), :], buf.at[i], sems.at[i])

    for i in range(chunks):
        fetch(i).start()
    tops = stats_ref[:, 0, :]
    top = jnp.max(tops, axis=0, keepdims=True)
    total = jnp.sum(stats_ref[:, 1, :] * jnp.exp(tops - top), axis=0, keepdims=True)
    factor = jnp.exp(own_ref[0:1, :] - top) / total
    for i in range(8):
        part = jnp.sum(own_ref[2 + i : 3 + i, :] * factor, keepdims=True) if i < 6 else 0.0
        mass_ref[i : i + 1, :] = jnp.broadcast_to(part, (1, LANES))
    column = jnp.transpose(jnp.broadcast_to(factor, (LANES, factor.shape[1])))
    for i in range(chunks):
        fetch(i).wait()
        for g in range(NX):
            part = jnp.dot(
                u_ref[g * per : (g + 1) * per, i * depth : (i + 1) * depth],
                buf[i, :, g * cols : (g + 1) * cols],
                preferred_element_type=f32,
            )
            acc[g] = part if i == 0 else acc[g] + part
    pairs = per // 2
    for g in range(NX):
        numer = acc[g, :pairs, :] + acc[g, pairs:, :]
        scaled = column[g * pairs : (g + 1) * pairs, :]
        numer = numer * jnp.concatenate([scaled] * (cols // LANES), axis=1)
        numer = jnp.where(same_head(pairs, cols, answers), numer, 0.0)
        rows = numer[0:answers, :]
        for h in range(1, pairs // answers):
            rows = rows + numer[h * answers : (h + 1) * answers, :]
        for j in range(cols // LANES):
            out_ref[:, g * (cols // LANES) + j, :] = rows[:, j * LANES : (j + 1) * LANES]


def out_kernel(pos, ctx_ref, mass_ref, w_ref, out_ref):
    answers, blocks, _ = ctx_ref.shape
    ctx = jnp.concatenate([ctx_ref[:, j, :] for j in range(blocks)], axis=1).astype(bf16)
    out_ref[0:answers, :] = jnp.dot(ctx, w_ref[...], preferred_element_type=f32)
    out_ref[answers : answers + 8, :] = mass_ref[...]


def body(enc_states, lengths, enc_gain, dec_states, w_query, w_key, w_value, w_out):
    qdev, pdev, plen, width = enc_states.shape
    answers = dec_states.shape[1]
    columns = w_key.shape[1]
    pairs = columns // HDIM * answers
    slots = pdev * plen
    quarter = columns // NX
    blocks = columns // LANES
    members = NY * NZ
    x, y, z = (lax.axis_index(axis).astype(jnp.int32) for axis in ("dp", "y", "z"))
    pos = jnp.concatenate([jnp.stack([y, z, x]), lengths.reshape(pdev)])

    values = lax.all_gather(w_value, PSG, axis=0, tiled=True)
    mine = lax.dynamic_slice(w_key, (0, x * quarter), (w_key.shape[0], quarter))
    key_blocks = gather(mine)

    q_parts = call(
        query_kernel,
        shaped((answers, blocks, LANES)),
        [],
        pos,
        dec_states.reshape(answers, width),
        w_query,
    )
    queries = summed(pos, q_parts)

    plain, turned = normalise(pos, enc_states.reshape(slots, width), enc_gain[None], plen)
    keys = [project(turned, pieces) for pieces in key_blocks]
    high, low, stat, copies = call(
        functools.partial(logits_kernel, plen),
        [
            shaped((pairs, slots), bf16),
            shaped((pairs, slots), bf16),
            shaped((8, pairs)),
            shaped((members, 2, pairs)),
        ],
        [pltpu.VMEM((pairs, LANES), f32)],
        pos,
        queries,
        *keys,
    )
    stats = exchange(copies)
    weighed = weigh(high, low, plain, 512)
    chunks = 8
    parts, mass = call(
        numer_kernel,
        [shaped((answers, blocks, LANES)), shaped((8, LANES))],
        [
            pltpu.VMEM((chunks, width // chunks, columns), bf16),
            pltpu.VMEM((NX, 2 * pairs // NX, quarter), f32),
            pltpu.SemaphoreType.DMA((chunks,)),
        ],
        pos,
        stat,
        stats,
        weighed,
        values,
        mib=46,
        flops=4 * pairs * width * quarter,
        hbm=(4,),
    )
    context = summed(pos, parts)
    part = call(out_kernel, shaped((answers + 8, w_out.shape[1])), [], pos, context, mass, w_out)
    both = part + lax.ppermute(part, "tp", [(0, 1), (1, 0)])
    scores = both[answers : answers + pdev, 0] * (pdev * members / (HEADS * answers))
    return both[:answers].astype(bf16)[None], scores[None]


def solution(mesh):
    fine = Mesh(mesh.devices.reshape(NX, NY, NZ, 2), ("dp", "y", "z", "tp"))
    placed = (
        P("dp", PSG, None, None),
        P("dp", PSG),
        P(),
        P("dp", None, None),
        P(PSG, "tp"),
        P(PSG, "tp"),
        P(PSG, "tp"),
        P("tp", PSG),
    )
    return jax.shard_map(
        body,
        mesh=fine,
        in_specs=placed,
        out_specs=(P("dp", None, PSG), P("dp", PSG)),
        check_vma=False,
    )
```

time: 542 us -> 217 us (0.40)
  waiting for transfers between devices: 356 us -> 41.1 us
  blocking collectives: 125 us -> 30.6 us
  starting transfers between devices: 0.15 us -> 61.4 us
  Pallas kernels: 0 us -> 37.1 us
  matrix products: 30.1 us -> 0 us
  local copies, waits for them, and re-layouts: 3.83 us -> 29.9 us
  other arithmetic: 12.9 us -> 0.75 us
    all_gather x3 -> x1, waiting for transfers between devices: 264 us -> 0.01 us  [body(): values = lax.all_gather(w_value, PSG, axis=0, tiled=True)]
    psum x1 -> x0, waiting for transfers between devices: 89.8 us -> none  [body(): total, numer = lax.psum((part_total, part_numer), 'psg')]
    psum x2 -> x0, blocking collectives: 66.1 us -> none  [the longest x1 57.2 us: body(): total, numer = lax.psum((part_total, part_numer), 'psg')]
    pmax x1 -> x0, blocking collectives: 58.6 us -> none  [body(): top = lax.pmax(local_max, 'psg')]
    ppermute x0 -> x20, waiting for transfers between devices: none -> 40.4 us  [the longest x19 39.6 us: recv(): return lax.ppermute(a, axis, [((i + k) % n, i) for i in range(n)])]
    ppermute x0 -> x20, starting transfers between devices: none -> 38.6 us  [the longest x19 26.9 us: recv(): return lax.ppermute(a, axis, [((i + k) % n, i) for i in range(n)])]
    pallas_call x0 -> x12, Pallas kernels: none -> 37.1 us  [the longest x6 12.5 us: call(): pl.pallas_call(kernel, out_shape=outs, in_specs=specs, out_specs=jax.tree...]
    all_to_all x0 -> x2, blocking collectives: none -> 30.6 us  [exchange(): return lax.all_to_all(a, PSG, split_axis=0, concat_axis=0, tiled=True)]
  transfers between devices with their start and end apart: 4 -> 24, of which waited for: 4 -> 12; matrix products, arithmetic and copies ran while one was open for 7% -> 4% of each run, Pallas kernels for 0% -> 13%
where the time goes in v1:
time: 217 us; the launch traced here: 216 us
  starting transfers between devices  61.4 us (28%)
  waiting for transfers between devices  41.1 us (19%)
  Pallas kernels  37.1 us (17%)
  blocking collectives  30.6 us (14%)
  local copies, waits for them, and re-layouts  29.9 us (14%)
  between operations  15.7 us (7%)
    ppermute x19, waiting for transfers between devices, recv(): return lax.ppermute(a, axis, [((i + k) % n, i) for i in range(n)])  39.6 us
    all_to_all x2, blocking collectives, exchange(): return lax.all_to_all(a, PSG, split_axis=0, concat_axis=0, tiled=True)  30.6 us
    ppermute x19, starting transfers between devices, recv(): return lax.ppermute(a, axis, [((i + k) % n, i) for i in range(n)])  26.9 us
    unnamed x52, local copies, waits for them, and re-layouts  24.7 us
    all_to_all x3, starting transfers between devices, exchange(): return lax.all_to_all(a, PSG, split_axis=0, concat_axis=0, tiled=True)  22.8 us
    pallas_call x6, Pallas kernels, call(): pl.pallas_call(kernel, out_shape=outs, in_specs=specs, out_specs=jax.tree...  12.5 us
    ppermute x1, starting transfers between devices, body(): both = part + lax.ppermute(part, 'tp', [(0, 1), (1, 0)])  11.7 us
    pallas_call x4, Pallas kernels, project(): pl.pallas_call(project_kernel, out_shape=shaped((rows, cols), bf16), in_s...  9.79 us
  transfers between devices with their start and end apart: 24, of which 12 were waited for; matrix products, arithmetic and copies ran while one was open for 4% of the time, Pallas kernels for 13%

profile of v1, /device:TPU:1, one launch (start us, length us, event | category | flops | bytes accessed | tf_op | source)
XLA Modules:
  0.0 216.5 jit_solution(7095824533910366134)
XLA Ops:
  8.8 3.6 %collective-permute-start = (bf16[128,256]{1,0:T(8,128)(2,1)S(1)}, bf16[128,256]{1,0:T(8,128)(2,1)S(1)}, u32[]{:S(2)}, u32[]{:S(2)}) collective-permute-start(bf16[128,256]{1,0:T(8,128)(2,1)S(1)} %get-tuple-element.19), channel_id=1, source_target_pairs={{16,0},{32,16},{48,32},{0,48},{17,1},{33,17},{49,33},{1,49},{18,2}... | collective-permute-start | bytes 196616 | tf_op jit(solution)/shard_map/ppermute | solution.py:51
  13.7 3.4 %collective-permute-done.1 = bf16[128,256]{1,0:T(8,128)(2,1)S(1)} collective-permute-done((bf16[128,256]{1,0:T(8,128)(2,1)S(1)}, bf16[128,256]{1,0:T(8,128)(2,1)S(1)}, u32[]{:S(2)}, u32[]{:S(2)}) %collective-permute-start.1) | collective-permute-done | bytes 65568 | tf_op jit(solution)/shard_map/ppermute | solution.py:51
  17.7 5.7 %collective-permute-start.3 = (bf16[512,256]{1,0:T(8,128)(2,1)S(1)}, bf16[512,256]{1,0:T(8,128)(2,1)S(1)}, u32[]{:S(2)}, u32[]{:S(2)}) collective-permute-start(bf16[512,256]{1,0:T(8,128)(2,1)S(1)} %pad_maximum_fusion), channel_id=1, source_target_pairs={{2,0},{4,2},{6,4},{8,6},{10,8},{12,10},{14,12},{0,14},{3,1},{5,3},... | collective-permute-start | bytes 786440 | tf_op jit(solution)/shard_map/ppermute | solution.py:51
  23.4 3.3 %collective-permute-done.3 = bf16[512,256]{1,0:T(8,128)(2,1)S(1)} collective-permute-done((bf16[512,256]{1,0:T(8,128)(2,1)S(1)}, bf16[512,256]{1,0:T(8,128)(2,1)S(1)}, u32[]{:S(2)}, u32[]{:S(2)}) %collective-permute-start.3) | collective-permute-done | bytes 262176 | tf_op jit(solution)/shard_map/ppermute | solution.py:51
  26.7 3.1 %collective-permute-done.4 = bf16[512,256]{1,0:T(8,128)(2,1)S(1)} collective-permute-done((bf16[512,256]{1,0:T(8,128)(2,1)S(1)}, bf16[512,256]{1,0:T(8,128)(2,1)S(1)}, u32[]{:S(2)}, u32[]{:S(2)}) %collective-permute-start.4) | collective-permute-done | bytes 262176 | tf_op jit(solution)/shard_map/ppermute | solution.py:51
  29.9 2.6 %collective-permute-start.9 = (bf16[1536,256]{1,0:T(8,128)(2,1)S(1)}, bf16[1536,256]{1,0:T(8,128)(2,1)S(1)}, u32[]{:S(2)}, u32[]{:S(2)}) collective-permute-start(bf16[1536,256]{1,0:T(8,128)(2,1)S(1)} %constant_dynamic-update-slice_fusion.refs_0_), channel_id=1, source_target_pairs={{64,0},{128,64},{192,128},{0,192},{65,1},{129,65},{193,129},{1,193... | collective-permute-start | bytes 2359304 | tf_op jit(solution)/shard_map/ppermute | solution.py:51
  33.9 6.2 %collective-permute-done.5 = bf16[512,256]{1,0:T(8,128)(2,1)S(1)} collective-permute-done((bf16[512,256]{1,0:T(8,128)(2,1)S(1)}, bf16[512,256]{1,0:T(8,128)(2,1)S(1)}, u32[]{:S(2)}, u32[]{:S(2)}) %collective-permute-start.5) | collective-permute-done | bytes 262176 | tf_op jit(solution)/shard_map/ppermute | solution.py:51
  43.8 5.7 %collective-permute-done.7 = bf16[512,256]{1,0:T(8,128)(2,1)S(1)} collective-permute-done((bf16[512,256]{1,0:T(8,128)(2,1)S(1)}, bf16[512,256]{1,0:T(8,128)(2,1)S(1)}, u32[]{:S(2)}, u32[]{:S(2)}) %collective-permute-start.7) | collective-permute-done | bytes 262176 | tf_op jit(solution)/shard_map/ppermute | solution.py:51
  52.5 2.5 %collective-permute-start.11 = (bf16[256,256]{1,0:T(8,128)(2,1)S(1)}, bf16[256,256]{1,0:T(8,128)(2,1)S(1)}, u32[]{:S(2)}, u32[]{:S(2)}) collective-permute-start(bf16[256,256]{1,0:T(8,128)(2,1)S(1)} %slice_add_fusion.1), channel_id=1, source_target_pairs={{2,0},{4,2},{6,4},{8,6},{10,8},{12,10},{14,12},{0,14},{3,1},{5,3},... | collective-permute-start | bytes 393224 | tf_op jit(solution)/shard_map/ppermute | solution.py:51
  58.0 2.2 collective-permute-done.12
  60.8 2.8 %collective-permute-start.13 = (bf16[2560,256]{1,0:T(8,128)(2,1)}, bf16[2560,256]{1,0:T(8,128)(2,1)S(1)}, u32[]{:S(2)}, u32[]{:S(2)}) collective-permute-start(bf16[2560,256]{1,0:T(8,128)(2,1)} %constant_dynamic-update-slice_fusion.6.refs_1_), channel_id=1, source_target_pairs={{64,0},{128,64},{192,128},{0,192},{65,1},{129,65},{193,129},{1,193... | collective-permute-start | bytes 3932168 | tf_op jit(solution)/shard_map/ppermute | solution.py:51
  67.0 5.9 %all-to-all-start = ((f32[32,8,128]{2,1,0:T(8,128)}), f32[32,8,128]{2,1,0:T(8,128)S(1)}, u32[]{:S(2)}, u32[]{:S(2)}) async-start(f32[32,8,128]{2,1,0:T(8,128)} %copy-done.13), calls=%async_computation | async-start | bytes 262144 | tf_op jit(solution)/shard_map/all_to_all | solution.py:55
  73.0 12.0 %collective-permute-done.13.refs_1_ = bf16[2560,256]{1,0:T(8,128)(2,1)S(1)} collective-permute-done((bf16[2560,256]{1,0:T(8,128)(2,1)}, bf16[2560,256]{1,0:T(8,128)(2,1)S(1)}, u32[]{:S(2)}, u32[]{:S(2)}) %collective-permute-start.13) | collective-permute-done | bytes 1310752 | tf_op jit(solution)/shard_map/ppermute | solution.py:51
  85.9 3.4 %collective-permute-start.16 = (bf16[1280,256]{1,0:T(8,128)(2,1)}, bf16[1280,256]{1,0:T(8,128)(2,1)}, u32[]{:S(2)}, u32[]{:S(2)}) collective-permute-start(bf16[1280,256]{1,0:T(8,128)(2,1)} %slice.47), channel_id=1, source_target_pairs={{64,0},{128,64},{192,128},{0,192},{65,1},{129,65},{193,129},{1,193... | collective-permute-start | bytes 1966088 | tf_op jit(solution)/shard_map/ppermute | solution.py:51
  90.2 2.9 %copy-done.3 = bf16[1,3,256,4096]{3,2,1,0:T(8,128)(2,1)S(1)} copy-done((bf16[1,3,256,4096]{3,2,1,0:T(8,128)(2,1)S(1)}, bf16[1,3,256,4096]{3,2,1,0:T(8,128)(2,1)}, u32[]{:S(2)}) %copy-start.3) | copy-done | bytes 6291480
  93.1 5.7 %shard_map.97 = (bf16[768,4096]{1,0:T(8,128)(2,1)S(1)}, bf16[768,4096]{1,0:T(8,128)(2,1)S(1)}) custom-call(s32[6]{0:T(128)S(1)} %pad_add_fusion.pos, bf16[768,4096]{1,0:T(8,128)(2,1)S(1)} %bitcast.10, bf16[1,4096]{1,0:T(2,128)(2,1)S(1)} %broadcast_in_dim.7.gain_ref), custom_call_target="tpu_custom_call" | custom-call | flops 18874368 | bytes 18874368 | tf_op jit(solution)/shard_map/pallas_call | solution.py:94
  98.8 2.6 %copy-done = bf16[768,4096]{1,0:T(8,128)(2,1)} copy-done((bf16[768,4096]{1,0:T(8,128)(2,1)}, bf16[768,4096]{1,0:T(8,128)(2,1)S(1)}, u32[]{:S(2)}) %copy-start) | copy-done | bytes 6291480
  101.4 2.7 %copy-done.17 = bf16[768,4096]{1,0:T(8,128)(2,1)} copy-done((bf16[768,4096]{1,0:T(8,128)(2,1)}, bf16[768,4096]{1,0:T(8,128)(2,1)S(1)}, u32[]{:S(2)}) %copy-start.17) | copy-done | bytes 6291480
  105.3 7.7 %all-to-all-start.1 = ((f32[32,8,128]{2,1,0:T(8,128)}), f32[32,8,128]{2,1,0:T(8,128)S(1)}, u32[]{:S(2)}, u32[]{:S(2)}) async-start(f32[32,8,128]{2,1,0:T(8,128)} %copy-done.12), calls=%async_computation.1 | async-start | bytes 262144 | tf_op jit(solution)/shard_map/all_to_all | solution.py:55
  113.1 2.8 %collective-permute-start.14 = (bf16[768,256]{1,0:T(8,128)(2,1)S(1)}, bf16[768,256]{1,0:T(8,128)(2,1)S(1)}, u32[]{:S(2)}, u32[]{:S(2)}) collective-permute-start(bf16[768,256]{1,0:T(8,128)(2,1)S(1)} %slice.45), channel_id=1, source_target_pairs={{64,0},{128,64},{192,128},{0,192},{65,1},{129,65},{193,129},{1,193... | collective-permute-start | bytes 1179656 | tf_op jit(solution)/shard_map/ppermute | solution.py:51
  117.0 2.8 %copy-done.1 = bf16[768,4096]{1,0:T(8,128)(2,1)S(1)} copy-done((bf16[768,4096]{1,0:T(8,128)(2,1)S(1)}, bf16[768,4096]{1,0:T(8,128)(2,1)}, u32[]{:S(2)}) %copy-start.1) | copy-done | bytes 6291480
  119.8 3.1 %shard_map.98.refs_0_ = bf16[768,256]{1,0:T(8,128)(2,1)S(1)} custom-call(bf16[768,4096]{1,0:T(8,128)(2,1)S(1)} %copy-done.1, bf16[1536,256]{1,0:T(8,128)(2,1)S(1)} %copy-done.11, bf16[2560,256]{1,0:T(8,128)(2,1)} %constant_dynamic-update-slice_fusion.6.refs_1_), custom_call_target="tpu_custom_call" | custom-call | flops 1610612736 | bytes 8781824 | tf_op jit(solution)/shard_map/pallas_call | solution.py:124
  126.6 3.1 %shard_map.100.refs_2_ = bf16[768,256]{1,0:T(8,128)(2,1)S(1)} custom-call(bf16[768,4096]{1,0:T(8,128)(2,1)S(1)} %copy-done.1, bf16[768,256]{1,0:T(8,128)(2,1)S(1)} %collective-permute-done.14.refs_0_, bf16[768,256]{1,0:T(8,128)(2,1)S(1)} %collective-permute-done.15.refs_1_, bf16[1280,256]{1,0:T(8,128)(2,1)} %collective-permute-done.16.refs_2_, ...), custom_call_target="tpu_custom_call" | custom-call | flops 1610612736 | bytes 8781824 | tf_op jit(solution)/shard_map/pallas_call | solution.py:124
  129.7 2.4 %shard_map.102 = (bf16[512,768]{1,0:T(8,128)(2,1)S(1)}, bf16[512,768]{1,0:T(8,128)(2,1)S(1)}, f32[8,512]{1,0:T(8,128)S(1)}, f32[32,2,512]{2,1,0:T(2,128)}) custom-call(s32[6]{0:T(128)S(1)} %pad_add_fusion.pos, f32[32,8,128]{2,1,0:T(8,128)S(1)} %all-to-all-done.1.q_ref, bf16[768,256]{1,0:T(8,128)(2,1)S(1)} %copy-done.7, bf16[768,256]{1,0:T(8,128)(2,1)S(1)} %copy-done.9, ...), custom_call_target="tpu_custom_call" | custom-call | bytes 1048576 | tf_op jit(solution)/shard_map/pallas_call | solution.py:38
  132.1 9.2 %all-to-all-start.2 = ((f32[32,2,512]{2,1,0:T(2,128)}), f32[32,2,512]{2,1,0:T(2,128)S(1)}, u32[]{:S(2)}, u32[]{:S(2)}) async-start(f32[32,2,512]{2,1,0:T(2,128)} %get-tuple-element.12), calls=%async_computation.2 | async-start | bytes 262144 | tf_op jit(solution)/shard_map/all_to_all | solution.py:55
  141.3 2.8 %copy-done.18 = bf16[768,4096]{1,0:T(8,128)(2,1)S(1)} copy-done((bf16[768,4096]{1,0:T(8,128)(2,1)S(1)}, bf16[768,4096]{1,0:T(8,128)(2,1)}, u32[]{:S(2)}) %copy-start.18) | copy-done | bytes 6291480
  144.1 9.0 %shard_map.103.u_ref = bf16[1024,4096]{1,0:T(8,128)(2,1)S(1)} custom-call(bf16[512,768]{1,0:T(8,128)(2,1)S(1)} %get-tuple-element.13.high_ref, bf16[512,768]{1,0:T(8,128)(2,1)S(1)} %get-tuple-element.14.low_ref, bf16[768,4096]{1,0:T(8,128)(2,1)S(1)} %copy-done.18), custom_call_target="tpu_custom_call" | custom-call | flops 6442450944 | bytes 16777216 | tf_op jit(solution)/shard_map/pallas_call | solution.py:220
  153.2 3.2 %copy-done.2 = bf16[1024,4096]{1,0:T(8,128)(2,1)} copy-done((bf16[1024,4096]{1,0:T(8,128)(2,1)}, bf16[1024,4096]{1,0:T(8,128)(2,1)S(1)}, u32[]{:S(2)}) %copy-start.2) | copy-done | bytes 8388632
  156.4 7.5 %shard_map.104 = (f32[32,8,128]{2,1,0:T(8,128)S(1)}, f32[8,128]{1,0:T(8,128)S(1)}) custom-call(s32[6]{0:T(128)S(1)} %pad_add_fusion.pos, f32[8,512]{1,0:T(8,128)S(1)} %get-tuple-element.11.own_ref, f32[32,2,512]{2,1,0:T(2,128)S(1)} %all-to-all-done.2.stats_ref, bf16[1024,4096]{1,0:T(8,128)(2,1)} %copy-done.2, ...), custom_call_target="tpu_custom_call" | custom-call | flops 2147483648 | bytes 1048576 | tf_op jit(solution)/shard_map/pallas_call | solution.py:38
  163.9 18.2 %all_to_all.25.got_ref = f32[32,8,128]{2,1,0:T(8,128)S(1)} all-to-all(f32[32,8,128]{2,1,0:T(8,128)S(1)} %get-tuple-element.16), channel_id=1, replica_groups=mesh['dp'=4,'y'=4,'z'=8,'tp'=2] {'y','z'}, dimensions={0} | all-to-all | bytes 262144 | tf_op jit(solution)/shard_map/all_to_all | solution.py:55
  182.7 12.4 %all_to_all.26.ctx_ref = f32[32,8,128]{2,1,0:T(8,128)S(1)} all-to-all(f32[32,8,128]{2,1,0:T(8,128)S(1)} %shard_map.105), channel_id=1, replica_groups=mesh['dp'=4,'y'=4,'z'=8,'tp'=2] {'y','z'}, dimensions={0} | all-to-all | bytes 262144 | tf_op jit(solution)/shard_map/all_to_all | solution.py:55
  195.9 11.7 %collective-permute-start.19 = (f32[40,128]{1,0:T(8,128)S(1)}, f32[40,128]{1,0:T(8,128)S(1)}, u32[]{:S(2)}, u32[]{:S(2)}) collective-permute-start(f32[40,128]{1,0:T(8,128)S(1)} %shard_map.106), channel_id=1, source_target_pairs={{0,1},{1,0},{2,3},{3,2},{4,5},{5,4},{6,7},{7,6},{8,9},{9,8},{10,11... | collective-permute-start | bytes 61448 | tf_op jit(solution)/shard_map/ppermute | solution.py:344
  (99 shorter events, 28.7 us)
Async XLA Ops:
  7.2 149.3 %all-gather.2.cloned.1.call-start = ((), (), s32[]{:S(2)}) async-start(), calls=%async_computation.5 | async-start | bytes 8650752 | tf_op jit(solution)/shard_map/all_gather | solution.py:293
  8.8 5.0 %collective-permute-start = (bf16[128,256]{1,0:T(8,128)(2,1)S(1)}, bf16[128,256]{1,0:T(8,128)(2,1)S(1)}, u32[]{:S(2)}, u32[]{:S(2)}) collective-permute-start(bf16[128,256]{1,0:T(8,128)(2,1)S(1)} %get-tuple-element.19), channel_id=1, source_target_pairs={{16,0},{32,16},{48,32},{0,48},{17,1},{33,17},{49,33},{1,49},{18,2}... | collective-permute-start | bytes 196616 | tf_op jit(solution)/shard_map/ppermute | solution.py:51
  12.4 4.7 %collective-permute-start.1 = (bf16[128,256]{1,0:T(8,128)(2,1)S(1)}, bf16[128,256]{1,0:T(8,128)(2,1)S(1)}, u32[]{:S(2)}, u32[]{:S(2)}) collective-permute-start(bf16[128,256]{1,0:T(8,128)(2,1)S(1)} %get-tuple-element.19), channel_id=1, source_target_pairs={{32,0},{48,16},{0,32},{16,48},{33,1},{49,17},{1,33},{17,49},{34,2}... | collective-permute-start | bytes 196616 | tf_op jit(solution)/shard_map/ppermute | solution.py:51
  12.8 5.0 %collective-permute-start.2 = (bf16[128,256]{1,0:T(8,128)(2,1)S(1)}, bf16[128,256]{1,0:T(8,128)(2,1)S(1)}, u32[]{:S(2)}, u32[]{:S(2)}) collective-permute-start(bf16[128,256]{1,0:T(8,128)(2,1)S(1)} %get-tuple-element.19), channel_id=1, source_target_pairs={{48,0},{0,16},{16,32},{32,48},{49,1},{1,17},{17,33},{33,49},{50,2}... | collective-permute-start | bytes 196616 | tf_op jit(solution)/shard_map/ppermute | solution.py:51
  17.7 9.0 %collective-permute-start.3 = (bf16[512,256]{1,0:T(8,128)(2,1)S(1)}, bf16[512,256]{1,0:T(8,128)(2,1)S(1)}, u32[]{:S(2)}, u32[]{:S(2)}) collective-permute-start(bf16[512,256]{1,0:T(8,128)(2,1)S(1)} %pad_maximum_fusion), channel_id=1, source_target_pairs={{2,0},{4,2},{6,4},{8,6},{10,8},{12,10},{14,12},{0,14},{3,1},{5,3},... | collective-permute-start | bytes 786440 | tf_op jit(solution)/shard_map/ppermute | solution.py:51
  23.4 6.4 %collective-permute-start.4 = (bf16[512,256]{1,0:T(8,128)(2,1)S(1)}, bf16[512,256]{1,0:T(8,128)(2,1)S(1)}, u32[]{:S(2)}, u32[]{:S(2)}) collective-permute-start(bf16[512,256]{1,0:T(8,128)(2,1)S(1)} %pad_maximum_fusion), channel_id=1, source_target_pairs={{14,0},{0,2},{2,4},{4,6},{6,8},{8,10},{10,12},{12,14},{15,1},{1,3}... | collective-permute-start | bytes 786440 | tf_op jit(solution)/shard_map/ppermute | solution.py:51
  29.9 26.0 %copy-start.10 = (bf16[1536,256]{1,0:T(8,128)(2,1)}, bf16[1536,256]{1,0:T(8,128)(2,1)S(1)}, u32[]{:S(2)}) copy-start(bf16[1536,256]{1,0:T(8,128)(2,1)S(1)} %constant_dynamic-update-slice_fusion.refs_0_) | copy-start | bytes 2359300
  29.9 20.3 %collective-permute-start.9 = (bf16[1536,256]{1,0:T(8,128)(2,1)S(1)}, bf16[1536,256]{1,0:T(8,128)(2,1)S(1)}, u32[]{:S(2)}, u32[]{:S(2)}) collective-permute-start(bf16[1536,256]{1,0:T(8,128)(2,1)S(1)} %constant_dynamic-update-slice_fusion.refs_0_), channel_id=1, source_target_pairs={{64,0},{128,64},{192,128},{0,192},{65,1},{129,65},{193,129},{1,193... | collective-permute-start | bytes 2359304 | tf_op jit(solution)/shard_map/ppermute | solution.py:51
  32.4 18.3 %collective-permute-start.10 = (bf16[1536,256]{1,0:T(8,128)(2,1)S(1)}, bf16[1536,256]{1,0:T(8,128)(2,1)S(1)}, u32[]{:S(2)}, u32[]{:S(2)}) collective-permute-start(bf16[1536,256]{1,0:T(8,128)(2,1)S(1)} %constant_dynamic-update-slice_fusion.refs_0_), channel_id=1, source_target_pairs={{192,0},{0,64},{64,128},{128,192},{193,1},{1,65},{65,129},{129,193... | collective-permute-start | bytes 2359304 | tf_op jit(solution)/shard_map/ppermute | solution.py:51
  32.4 7.7 %collective-permute-start.5 = (bf16[512,256]{1,0:T(8,128)(2,1)S(1)}, bf16[512,256]{1,0:T(8,128)(2,1)S(1)}, u32[]{:S(2)}, u32[]{:S(2)}) collective-permute-start(bf16[512,256]{1,0:T(8,128)(2,1)S(1)} %collective-permute-done.3), channel_id=1, source_target_pairs={{2,0},{4,2},{6,4},{8,6},{10,8},{12,10},{14,12},{0,14},{3,1},{5,3},... | collective-permute-start | bytes 786440 | tf_op jit(solution)/shard_map/ppermute | solution.py:51
  32.9 9.4 %collective-permute-start.6 = (bf16[512,256]{1,0:T(8,128)(2,1)S(1)}, bf16[512,256]{1,0:T(8,128)(2,1)S(1)}, u32[]{:S(2)}, u32[]{:S(2)}) collective-permute-start(bf16[512,256]{1,0:T(8,128)(2,1)S(1)} %collective-permute-done.4), channel_id=1, source_target_pairs={{14,0},{0,2},{2,4},{4,6},{6,8},{8,10},{10,12},{12,14},{15,1},{1,3}... | collective-permute-start | bytes 786440 | tf_op jit(solution)/shard_map/ppermute | solution.py:51
  40.1 9.3 %collective-permute-start.7 = (bf16[512,256]{1,0:T(8,128)(2,1)S(1)}, bf16[512,256]{1,0:T(8,128)(2,1)S(1)}, u32[]{:S(2)}, u32[]{:S(2)}) collective-permute-start(bf16[512,256]{1,0:T(8,128)(2,1)S(1)} %collective-permute-done.5), channel_id=1, source_target_pairs={{2,0},{4,2},{6,4},{8,6},{10,8},{12,10},{14,12},{0,14},{3,1},{5,3},... | collective-permute-start | bytes 786440 | tf_op jit(solution)/shard_map/ppermute | solution.py:51
  42.4 12.7 %collective-permute-start.8 = (bf16[512,256]{1,0:T(8,128)(2,1)S(1)}, bf16[512,256]{1,0:T(8,128)(2,1)S(1)}, u32[]{:S(2)}, u32[]{:S(2)}) collective-permute-start(bf16[512,256]{1,0:T(8,128)(2,1)S(1)} %collective-permute-done.6), channel_id=1, source_target_pairs={{14,0},{0,2},{2,4},{4,6},{6,8},{8,10},{10,12},{12,14},{15,1},{1,3}... | collective-permute-start | bytes 786440 | tf_op jit(solution)/shard_map/ppermute | solution.py:51
  43.1 20.6 %copy-start.20 = (s32[1,3]{1,0:T(1,128)S(1)}, s32[1,3]{1,0:T(1,128)}, u32[]{:S(2)}) copy-start(s32[1,3]{1,0:T(1,128)} %param.9) | copy-start | bytes 40
  50.7 10.1 %copy-start.4 = (bf16[1536,256]{1,0:T(8,128)(2,1)}, bf16[1536,256]{1,0:T(8,128)(2,1)S(1)}, u32[]{:S(2)}) copy-start(bf16[1536,256]{1,0:T(8,128)(2,1)S(1)} %collective-permute-done.10.refs_0_) | copy-start | bytes 2359300
  52.5 4.8 %collective-permute-start.11 = (bf16[256,256]{1,0:T(8,128)(2,1)S(1)}, bf16[256,256]{1,0:T(8,128)(2,1)S(1)}, u32[]{:S(2)}, u32[]{:S(2)}) collective-permute-start(bf16[256,256]{1,0:T(8,128)(2,1)S(1)} %slice_add_fusion.1), channel_id=1, source_target_pairs={{2,0},{4,2},{6,4},{8,6},{10,8},{12,10},{14,12},{0,14},{3,1},{5,3},... | collective-permute-start | bytes 393224 | tf_op jit(solution)/shard_map/ppermute | solution.py:51
  55.1 5.1 %collective-permute-start.12 = (bf16[256,256]{1,0:T(8,128)(2,1)S(1)}, bf16[256,256]{1,0:T(8,128)(2,1)S(1)}, u32[]{:S(2)}, u32[]{:S(2)}) collective-permute-start(bf16[256,256]{1,0:T(8,128)(2,1)S(1)} %slice_add_fusion), channel_id=1, source_target_pairs={{14,0},{0,2},{2,4},{4,6},{6,8},{8,10},{10,12},{12,14},{15,1},{1,3}... | collective-permute-start | bytes 393224 | tf_op jit(solution)/shard_map/ppermute | solution.py:51
  60.8 24.1 %collective-permute-start.13 = (bf16[2560,256]{1,0:T(8,128)(2,1)}, bf16[2560,256]{1,0:T(8,128)(2,1)S(1)}, u32[]{:S(2)}, u32[]{:S(2)}) collective-permute-start(bf16[2560,256]{1,0:T(8,128)(2,1)} %constant_dynamic-update-slice_fusion.6.refs_1_), channel_id=1, source_target_pairs={{64,0},{128,64},{192,128},{0,192},{65,1},{129,65},{193,129},{1,193... | collective-permute-start | bytes 3932168 | tf_op jit(solution)/shard_map/ppermute | solution.py:51
  63.7 25.6 %collective-permute-start.17 = (bf16[2560,256]{1,0:T(8,128)(2,1)}, bf16[2560,256]{1,0:T(8,128)(2,1)S(1)}, u32[]{:S(2)}, u32[]{:S(2)}) collective-permute-start(bf16[2560,256]{1,0:T(8,128)(2,1)} %constant_dynamic-update-slice_fusion.6.refs_1_), channel_id=1, source_target_pairs={{192,0},{0,64},{64,128},{128,192},{193,1},{1,65},{65,129},{129,193... | collective-permute-start | bytes 3932168 | tf_op jit(solution)/shard_map/ppermute | solution.py:51
  67.0 37.0 %all-to-all-start = ((f32[32,8,128]{2,1,0:T(8,128)}), f32[32,8,128]{2,1,0:T(8,128)S(1)}, u32[]{:S(2)}, u32[]{:S(2)}) async-start(f32[32,8,128]{2,1,0:T(8,128)} %copy-done.13), calls=%async_computation | async-start | bytes 262144 | tf_op jit(solution)/shard_map/all_to_all | solution.py:55
  73.0 17.2 %copy-start.19 = (bf16[4096]{0:T(1024)(128)(2,1)S(1)}, bf16[4096]{0:T(1024)(128)(2,1)}, u32[]{:S(2)}) copy-start(bf16[4096]{0:T(1024)(128)(2,1)} %param.10) | copy-start | bytes 24580
  85.9 40.7 %collective-permute-start.16 = (bf16[1280,256]{1,0:T(8,128)(2,1)}, bf16[1280,256]{1,0:T(8,128)(2,1)}, u32[]{:S(2)}, u32[]{:S(2)}) collective-permute-start(bf16[1280,256]{1,0:T(8,128)(2,1)} %slice.47), channel_id=1, source_target_pairs={{64,0},{128,64},{192,128},{0,192},{65,1},{129,65},{193,129},{1,193... | collective-permute-start | bytes 1966088 | tf_op jit(solution)/shard_map/ppermute | solution.py:51
  90.2 36.4 %collective-permute-start.18 = (bf16[1280,256]{1,0:T(8,128)(2,1)}, bf16[1280,256]{1,0:T(8,128)(2,1)}, u32[]{:S(2)}, u32[]{:S(2)}) collective-permute-start(bf16[1280,256]{1,0:T(8,128)(2,1)} %slice.48), channel_id=1, source_target_pairs={{192,0},{0,64},{64,128},{128,192},{193,1},{1,65},{65,129},{129,193... | collective-permute-start | bytes 1966088 | tf_op jit(solution)/shard_map/ppermute | solution.py:51
  105.3 24.4 %all-to-all-start.1 = ((f32[32,8,128]{2,1,0:T(8,128)}), f32[32,8,128]{2,1,0:T(8,128)S(1)}, u32[]{:S(2)}, u32[]{:S(2)}) async-start(f32[32,8,128]{2,1,0:T(8,128)} %copy-done.12), calls=%async_computation.1 | async-start | bytes 262144 | tf_op jit(solution)/shard_map/all_to_all | solution.py:55
  113.0 3.9 %copy-start.11 = (bf16[1536,256]{1,0:T(8,128)(2,1)S(1)}, bf16[1536,256]{1,0:T(8,128)(2,1)}, u32[]{:S(2)}) copy-start(bf16[1536,256]{1,0:T(8,128)(2,1)} %copy-done.10) | copy-start | bytes 2359300
  113.1 13.4 %collective-permute-start.14 = (bf16[768,256]{1,0:T(8,128)(2,1)S(1)}, bf16[768,256]{1,0:T(8,128)(2,1)S(1)}, u32[]{:S(2)}, u32[]{:S(2)}) collective-permute-start(bf16[768,256]{1,0:T(8,128)(2,1)S(1)} %slice.45), channel_id=1, source_target_pairs={{64,0},{128,64},{192,128},{0,192},{65,1},{129,65},{193,129},{1,193... | collective-permute-start | bytes 1179656 | tf_op jit(solution)/shard_map/ppermute | solution.py:51
  116.9 9.7 %collective-permute-start.15 = (bf16[768,256]{1,0:T(8,128)(2,1)S(1)}, bf16[768,256]{1,0:T(8,128)(2,1)S(1)}, u32[]{:S(2)}, u32[]{:S(2)}) collective-permute-start(bf16[768,256]{1,0:T(8,128)(2,1)S(1)} %slice.46), channel_id=1, source_target_pairs={{192,0},{0,64},{64,128},{128,192},{193,1},{1,65},{65,129},{129,193... | collective-permute-start | bytes 1179656 | tf_op jit(solution)/shard_map/ppermute | solution.py:51
  126.5 3.2 %copy-start.7 = (bf16[768,256]{1,0:T(8,128)(2,1)S(1)}, bf16[768,256]{1,0:T(8,128)(2,1)}, u32[]{:S(2)}) copy-start(bf16[768,256]{1,0:T(8,128)(2,1)} %copy-done.6) | copy-start | bytes 1179652
  132.1 24.3 %all-to-all-start.2 = ((f32[32,2,512]{2,1,0:T(2,128)}), f32[32,2,512]{2,1,0:T(2,128)S(1)}, u32[]{:S(2)}, u32[]{:S(2)}) async-start(f32[32,2,512]{2,1,0:T(2,128)} %get-tuple-element.12), calls=%async_computation.2 | async-start | bytes 262144 | tf_op jit(solution)/shard_map/all_to_all | solution.py:55
  153.2 3.3 %copy-start.2 = (bf16[1024,4096]{1,0:T(8,128)(2,1)}, bf16[1024,4096]{1,0:T(8,128)(2,1)S(1)}, u32[]{:S(2)}) copy-start(bf16[1024,4096]{1,0:T(8,128)(2,1)S(1)} %shard_map.103.u_ref) | copy-start | bytes 25165828
  156.4 38.7 %copy-start.14 = (bf16[1024,128]{1,0:T(8,128)(2,1)S(1)}, bf16[1024,128]{1,0:T(8,128)(2,1)}, u32[]{:S(2)}) copy-start(bf16[1024,128]{1,0:T(8,128)(2,1)} %w_ref.3) | copy-start | bytes 786436
  195.9 12.5 %collective-permute-start.19 = (f32[40,128]{1,0:T(8,128)S(1)}, f32[40,128]{1,0:T(8,128)S(1)}, u32[]{:S(2)}, u32[]{:S(2)}) collective-permute-start(f32[40,128]{1,0:T(8,128)S(1)} %shard_map.106), channel_id=1, source_target_pairs={{0,1},{1,0},{2,3},{3,2},{4,5},{5,4},{6,7},{7,6},{8,9},{9,8},{10,11... | collective-permute-start | bytes 61448 | tf_op jit(solution)/shard_map/ppermute | solution.py:344
  (13 other events, 25.6 us)
Sparse Core Ops, SparseCore 0:
  10.6 104.7 all-gather.1

commit v2 on v1

v2 whole, which is shorter than its diff:
```python
import functools

import jax
import jax.numpy as jnp
from jax import lax
from jax.experimental import pallas as pl
from jax.experimental.pallas import tpu as pltpu
from jax.sharding import Mesh, PartitionSpec as P

HEADS = 32
HDIM = 64
NX = 4
NY = 4
NZ = 8
LANES = 128
PSG = ("y", "z")
SIZES = {"dp": NX, "y": NY, "z": NZ}
VMEM = pl.BlockSpec(memory_space=pltpu.VMEM)
SMEM = pl.BlockSpec(memory_space=pltpu.SMEM)
f32 = jnp.float32
bf16 = jnp.bfloat16

GROUPS = ((0, 1, 7), (2, 6, 3, 5, 4))
ORDER = [(dy, dz) for group in GROUPS for dz in group for dy in range(NY)]


def shaped(shape, dtype=f32):
    return jax.ShapeDtypeStruct(shape, dtype)


def params(mib):
    return pltpu.CompilerParams(vmem_limit_bytes=mib * 1024 * 1024)


def call(kernel, outs, scratch, *args, mib=16, flops=0):
    specs = [SMEM] + [VMEM] * (len(args) - 1)
    return pl.pallas_call(
        kernel,
        out_shape=outs,
        in_specs=specs,
        out_specs=jax.tree.map(lambda _: VMEM, outs),
        scratch_shapes=scratch,
        compiler_params=params(mib),
        cost_estimate=pl.CostEstimate(flops=flops, bytes_accessed=1 << 20, transcendentals=0),
    )(*args)


def recv(a, axis, k):
    n = SIZES[axis]
    return lax.ppermute(a, axis, [((i + k) % n, i) for i in range(n)])


def exchange(a):
    return lax.all_to_all(a, PSG, split_axis=0, concat_axis=0, tiled=True)


def round_x(group, after):
    half = group.shape[0] // 2
    up, down = recv(group, "dp", 1), recv(group, "dp", -1)
    far = [recv(up[:half] + after, "dp", 1), recv(down[half:] + after, "dp", -1)]
    return [[group], [up], far, [down]]


def first_of(*arrays):
    return sum(a[(0,) * a.ndim].astype(bf16) for a in arrays) * 0


def gather(shard, after):
    block = jnp.concatenate(
        [shard, recv(shard, "y", 1), recv(shard, "y", 2), recv(shard, "y", -1)], axis=0
    )
    half = block.shape[0] // 2
    up1, down1 = recv(block, "z", 1), recv(block, "z", -1)
    near = round_x(jnp.concatenate([block, up1, down1], axis=0), 0)
    up2, down2 = recv(up1, "z", 1), recv(down1, "z", -1)
    up3, down3 = recv(up2, "z", 1), recv(down2, "z", -1)
    last = first_of(*near[2])
    far = (recv(up3[:half], "z", 1) + last, recv(down3[half:], "z", -1) + last)
    rest = round_x(jnp.concatenate([up2, down2, up3, down3, *far], axis=0), after)
    return [near[dx] + rest[dx] for dx in range(NX)]


def norm_kernel(pos, e_ref, gain_ref, plain_ref, turned_ref):
    e = e_ref[...].astype(f32)
    scale = lax.rsqrt(jnp.mean(e * e, axis=-1, keepdims=True) + 1e-06)
    plain_ref[...] = (e * scale * gain_ref[...].astype(f32)).astype(bf16)
    for i, (dy, dz) in enumerate(ORDER):
        at = lax.rem(pos[0] + dy, NY) * NZ + lax.rem(pos[1] + dz, NZ)
        turned_ref[:, i * LANES : (i + 1) * LANES] = plain_ref[
            :, pl.ds(pl.multiple_of(at * LANES, LANES), LANES)
        ]


def normalise(pos, enc, gain, tile):
    rows, width = enc.shape
    block = pl.BlockSpec((tile, width), lambda i, pos: (i, 0))
    return pl.pallas_call(
        norm_kernel,
        out_shape=[shaped((rows, width), bf16)] * 2,
        grid_spec=pltpu.PrefetchScalarGridSpec(
            num_scalar_prefetch=1,
            grid=(rows // tile,),
            in_specs=[block, pl.BlockSpec((1, width), lambda i, pos: (0, 0))],
            out_specs=[block, block],
        ),
        compiler_params=params(32),
        cost_estimate=pl.CostEstimate(
            flops=6 * rows * width, bytes_accessed=6 * rows * width, transcendentals=0
        ),
    )(pos, enc, gain)


def project_kernel(x_ref, *refs):
    pieces, out_ref = refs[:-1], refs[-1]
    tile = min(out_ref.shape[1], 256)
    for col in range(0, out_ref.shape[1], tile):
        acc, at = None, 0
        for ref in pieces:
            depth = ref.shape[0]
            part = jnp.dot(
                x_ref[:, at : at + depth], ref[:, col : col + tile], preferred_element_type=f32
            )
            acc = part if acc is None else acc + part
            at += depth
        out_ref[:, col : col + tile] = acc.astype(bf16)


def project(x, pieces):
    rows, width = x.shape
    cols = pieces[0].shape[1]
    return pl.pallas_call(
        project_kernel,
        out_shape=shaped((rows, cols), bf16),
        in_specs=[VMEM] * (1 + len(pieces)),
        out_specs=VMEM,
        compiler_params=params(16),
        cost_estimate=pl.CostEstimate(
            flops=2 * rows * width * cols,
            bytes_accessed=2 * (rows * width + width * cols + rows * cols),
            transcendentals=0,
        ),
    )(x, *pieces)


def query_kernel(pos, dec_ref, w_ref, out_ref):
    at = pl.multiple_of((pos[0] * NZ + pos[1]) * LANES, LANES)
    part = jnp.dot(dec_ref[:, pl.ds(at, LANES)], w_ref[...], preferred_element_type=f32)
    for j in range(out_ref.shape[1]):
        out_ref[:, j, :] = part[:, j * LANES : (j + 1) * LANES]


def spread_kernel(pos, got_ref, out_ref):
    total = jnp.sum(got_ref[...], axis=0, keepdims=True)
    out_ref[...] = jnp.broadcast_to(total, out_ref.shape)


def same_head(rows, cols, answers):
    row = lax.broadcasted_iota(jnp.int32, (rows, cols), 0) // answers
    col = lax.broadcasted_iota(jnp.int32, (rows, cols), 1) // HDIM
    return row == col


def attend_kernel(plen, pos, q_ref, v_ref, *refs):
    keys, (out_ref, mass_ref) = refs[:NX], refs[NX:]
    answers = q_ref.shape[0]
    lane = lax.broadcasted_iota(jnp.int32, (answers, LANES), 1)
    last = out_ref.shape[1] - 1
    stats = jnp.zeros((answers, LANES), f32)
    passages = v_ref.shape[0] // plen
    masses = [stats] * passages
    for dx, key_ref in enumerate(keys):
        quarter = lax.rem(pos[2] + dx, NX)
        slots, cols = key_ref.shape
        heads = cols // HDIM
        pairs = heads * answers
        blocks = cols // LANES
        q = jnp.concatenate(
            [q_ref[:, pl.ds(quarter * blocks + j, 1), :].reshape(answers, LANES) for j in range(blocks)],
            axis=1,
        )
        own = same_head(pairs, cols, answers)
        spread = jnp.where(own, jnp.concatenate([q] * heads, axis=0), 0.0).astype(bf16)
        logits = lax.dot_general(
            spread, key_ref[...], (((1,), (1,)), ((), ())), preferred_element_type=f32
        ) * HDIM ** (-0.5)
        token = lax.broadcasted_iota(jnp.int32, (pairs, plen), 1)
        valid = [token < pos[3 + i] for i in range(passages)]
        masked = [
            jnp.where(valid[i], logits[:, i * plen : (i + 1) * plen], -1e30) for i in range(passages)
        ]
        top = functools.reduce(jnp.maximum, [jnp.max(m, axis=1, keepdims=True) for m in masked])
        p = [jnp.where(valid[i], jnp.exp(masked[i] - top), 0.0) for i in range(passages)]
        sums = [jnp.sum(part, axis=1, keepdims=True) for part in p]
        total = functools.reduce(jnp.add, sums)
        for h in range(heads):
            at = slice(h * answers, (h + 1) * answers)
            head = quarter * heads + h
            stats = jnp.where(lane == head, top[at, :], stats)
            stats = jnp.where(lane == head + LANES // 2, total[at, :], stats)
            masses = [jnp.where(lane == head, s[at, :], m) for s, m in zip(sums, masses)]
        whole = jnp.concatenate(p, axis=1)
        high = whole.astype(bf16)
        low = (whole - high.astype(f32)).astype(bf16)
        v = v_ref[:, pl.ds(pl.multiple_of(quarter * cols, cols), cols)]
        numer = jnp.dot(high, v, preferred_element_type=f32)
        numer += jnp.dot(low, v, preferred_element_type=f32)
        numer = jnp.where(own, numer, 0.0)
        rows = numer[0:answers, :]
        for h in range(1, heads):
            rows = rows + numer[h * answers : (h + 1) * answers, :]
        for j in range(blocks):
            out_ref[:, pl.ds(quarter * blocks + j, 1), :] = rows[
                :, j * LANES : (j + 1) * LANES
            ].reshape(answers, 1, LANES)
    out_ref[:, last, :] = stats
    for i, mass in enumerate(masses):
        mass_ref[i] = mass


def by_head(lane, row, j):
    return jnp.where(lane < HDIM, row[:, 2 * j : 2 * j + 1], row[:, 2 * j + 1 : 2 * j + 2])


def merge_kernel(pos, got_ref, out_ref):
    last = got_ref.shape[1] - 1
    stats = got_ref[:, last, :]
    top = jnp.max(stats, axis=0, keepdims=True)
    scale = jnp.exp(stats - top)
    total = jnp.sum(pltpu.roll(stats, LANES // 2, 1) * scale, axis=0, keepdims=True)
    lane = lax.broadcasted_iota(jnp.int32, scale.shape, 1)
    first = lane[0:1, :]
    for j in range(last):
        numer = jnp.sum(got_ref[:, j, :] * by_head(lane, scale, j), axis=0, keepdims=True)
        row = numer / by_head(first, total, j)
        out_ref[:, j, :] = jnp.broadcast_to(row, scale.shape)
    row = jnp.where(first < LANES // 2, top, pltpu.roll(total, LANES // 2, 1))
    out_ref[:, last, :] = jnp.broadcast_to(row, scale.shape)


def out_kernel(pos, ctx_ref, parts_ref, mass_ref, w_ref, out_ref):
    answers, rows, _ = ctx_ref.shape
    last = rows - 1
    ctx = jnp.concatenate([ctx_ref[:, j, :] for j in range(last)], axis=1).astype(bf16)
    out_ref[0:answers, :] = jnp.dot(ctx, w_ref[...], preferred_element_type=f32)
    merged = ctx_ref[:, last, :]
    lane = lax.broadcasted_iota(jnp.int32, merged.shape, 1)
    heads = last * LANES // HDIM
    total = jnp.where(lane < heads, pltpu.roll(merged, LANES // 2, 1), 1.0)
    gap = jnp.where(lane < heads, parts_ref[:, last, :] - merged, 0.0)
    factor = jnp.exp(gap) / total
    for i in range(8):
        part = jnp.sum(mass_ref[i] * factor, keepdims=True) if i < mass_ref.shape[0] else 0.0
        out_ref[answers + i : answers + i + 1, :] = jnp.broadcast_to(part, (1, LANES))


def body(enc_states, lengths, enc_gain, dec_states, w_query, w_key, w_value, w_out):
    qdev, pdev, plen, width = enc_states.shape
    answers = dec_states.shape[1]
    columns = w_key.shape[1]
    pairs = columns // HDIM * answers
    slots = pdev * plen
    quarter = columns // NX
    blocks = columns // LANES
    members = NY * NZ
    x, y, z = (lax.axis_index(axis).astype(jnp.int32) for axis in ("dp", "y", "z"))
    pos = jnp.concatenate([jnp.stack([y, z, x]), lengths.reshape(pdev)])

    w_values = lax.all_gather(w_value, PSG, axis=0, tiled=True)
    plain, turned = normalise(pos, enc_states.reshape(slots, width), enc_gain[None], plen)
    q_parts = call(
        query_kernel,
        shaped((answers, blocks, LANES)),
        [],
        pos,
        dec_states.reshape(answers, width),
        w_query,
    )
    q_sum = call(spread_kernel, shaped(q_parts.shape), [], pos, exchange(q_parts))
    queries = exchange(q_sum)

    mine = lax.dynamic_slice(w_key, (0, x * quarter), (w_key.shape[0], quarter))
    keys = [project(turned, pieces) for pieces in gather(mine, first_of(plain))]
    values = project(plain, [w_values])
    parts, mass = call(
        functools.partial(attend_kernel, plen),
        [shaped((answers, blocks + 1, LANES)), shaped((pdev, answers, LANES))],
        [],
        pos,
        queries,
        values,
        *keys,
        flops=4 * pairs * slots * quarter * 2,
    )
    merged = call(merge_kernel, shaped(parts.shape), [], pos, exchange(parts))
    context = exchange(merged)
    part = call(
        out_kernel, shaped((answers + 8, w_out.shape[1])), [], pos, context, parts, mass, w_out
    )
    both = part + lax.ppermute(part, "tp", [(0, 1), (1, 0)])
    scores = both[answers : answers + pdev, 0] * (pdev * members / (HEADS * answers))
    return both[:answers].astype(bf16)[None], scores[None]


def solution(mesh):
    fine = Mesh(mesh.devices.reshape(NX, NY, NZ, 2), ("dp", "y", "z", "tp"))
    placed = (
        P("dp", PSG, None, None),
        P("dp", PSG),
        P(),
        P("dp", None, None),
        P(PSG, "tp"),
        P(PSG, "tp"),
        P(PSG, "tp"),
        P("tp", PSG),
    )
    return jax.shard_map(
        body,
        mesh=fine,
        in_specs=placed,
        out_specs=(P("dp", None, PSG), P("dp", PSG)),
        check_vma=False,
    )
```

time: 217 us -> 187 us (0.86)
  waiting for transfers between devices: 41.1 us -> 25.2 us
  Pallas kernels: 37.1 us -> 27.3 us
  starting transfers between devices: 61.4 us -> 52 us
  other arithmetic: 0.75 us -> 3.86 us
    ppermute x19, waiting for transfers between devices: 39.6 us -> 23.6 us  [recv(): return lax.ppermute(a, axis, [((i + k) % n, i) for i in range(n)])]
    pallas_call x1 -> x0, Pallas kernels: 9.04 us -> none  [weigh(): pl.pallas_call(weigh_kernel, out_shape=shaped((2 * pairs, width), bf16),...]
    pallas_call x6 -> x5, Pallas kernels: 12.5 us -> 5.12 us  [call(): pl.pallas_call(kernel, out_shape=outs, in_specs=specs, out_specs=jax.tree...]
    all_to_all x3 -> x2, starting transfers between devices: 22.8 us -> 15.7 us  [exchange(): return lax.all_to_all(a, PSG, split_axis=0, concat_axis=0, tiled=True)]
    pallas_call x4 -> x5, Pallas kernels: 9.79 us -> 16.5 us  [project(): pl.pallas_call(project_kernel, out_shape=shaped((rows, cols), bf16), in_s...]
    unnamed x52 -> x59, local copies, waits for them, and re-layouts: 24.7 us -> 27 us
    slice x6 -> x7, local copies, waits for them, and re-layouts: 3.89 us -> 1.7 us  [the longest x3 1.63 us: first_of(): return sum((a[(0,) * a.ndim].astype(bf16) for a in arrays)) * 0]
  transfers between devices with their start and end apart: 24 -> 23, of which waited for: 12 -> 11; matrix products, arithmetic and copies ran while one was open for 4% -> 5% of each run, Pallas kernels for 13% -> 13%
where the time goes in v2:
time: 187 us
  starting transfers between devices  52 us (28%)
  blocking collectives  32.5 us (17%)
  local copies, waits for them, and re-layouts  29.3 us (16%)
  Pallas kernels  27.3 us (15%)
  waiting for transfers between devices  25.2 us (13%)
  between operations  16.5 us (9%)
  other arithmetic  3.86 us (2%)
    all_to_all x2, blocking collectives, exchange(): return lax.all_to_all(a, PSG, split_axis=0, concat_axis=0, tiled=True)  32.5 us
    unnamed x59, local copies, waits for them, and re-layouts  27 us
    ppermute x19, starting transfers between devices, recv(): return lax.ppermute(a, axis, [((i + k) % n, i) for i in range(n)])  26.7 us
    ppermute x19, waiting for transfers between devices, recv(): return lax.ppermute(a, axis, [((i + k) % n, i) for i in range(n)])  23.6 us
    pallas_call x5, Pallas kernels, project(): pl.pallas_call(project_kernel, out_shape=shaped((rows, cols), bf16), in_s...  16.5 us
    all_to_all x2, starting transfers between devices, exchange(): return lax.all_to_all(a, PSG, split_axis=0, concat_axis=0, tiled=True)  15.7 us
    ppermute x1, starting transfers between devices, body(): both = part + lax.ppermute(part, 'tp', [(0, 1), (1, 0)])  9.58 us
    pallas_call x1, Pallas kernels, normalise(): pl.pallas_call(norm_kernel, out_shape=[shaped((rows, width), bf16)] * 2,...  5.69 us
  transfers between devices with their start and end apart: 23, of which 11 were waited for; matrix products, arithmetic and copies ran while one was open for 5% of the time, Pallas kernels for 13%

profile of v2, /device:TPU:1, one launch (start us, length us, event | category | flops | bytes accessed | tf_op | source)
XLA Modules:
  0.0 186.6 jit_solution(3497570971448658925)
XLA Ops:
  8.8 3.6 %collective-permute-start = (bf16[128,256]{1,0:T(8,128)(2,1)S(1)}, bf16[128,256]{1,0:T(8,128)(2,1)S(1)}, u32[]{:S(2)}, u32[]{:S(2)}) collective-permute-start(bf16[128,256]{1,0:T(8,128)(2,1)S(1)} %get-tuple-element.11), channel_id=1, source_target_pairs={{16,0},{32,16},{48,32},{0,48},{17,1},{33,17},{49,33},{1,49},{18,2}... | collective-permute-start | bytes 196616 | tf_op jit(solution)/shard_map/ppermute | solution.py:50
  13.7 3.4 %collective-permute-done.1 = bf16[128,256]{1,0:T(8,128)(2,1)S(1)} collective-permute-done((bf16[128,256]{1,0:T(8,128)(2,1)S(1)}, bf16[128,256]{1,0:T(8,128)(2,1)S(1)}, u32[]{:S(2)}, u32[]{:S(2)}) %collective-permute-start.1) | collective-permute-done | bytes 65568 | tf_op jit(solution)/shard_map/ppermute | solution.py:50
  17.7 5.7 %collective-permute-start.3 = (bf16[512,256]{1,0:T(8,128)(2,1)S(1)}, bf16[512,256]{1,0:T(8,128)(2,1)S(1)}, u32[]{:S(2)}, u32[]{:S(2)}) collective-permute-start(bf16[512,256]{1,0:T(8,128)(2,1)S(1)} %pad_maximum_fusion), channel_id=1, source_target_pairs={{2,0},{4,2},{6,4},{8,6},{10,8},{12,10},{14,12},{0,14},{3,1},{5,3},... | collective-permute-start | bytes 786440 | tf_op jit(solution)/shard_map/ppermute | solution.py:50
  23.4 3.3 %collective-permute-done.3 = bf16[512,256]{1,0:T(8,128)(2,1)S(1)} collective-permute-done((bf16[512,256]{1,0:T(8,128)(2,1)S(1)}, bf16[512,256]{1,0:T(8,128)(2,1)S(1)}, u32[]{:S(2)}, u32[]{:S(2)}) %collective-permute-start.3) | collective-permute-done | bytes 262176 | tf_op jit(solution)/shard_map/ppermute | solution.py:50
  26.7 3.1 %collective-permute-done.4 = bf16[512,256]{1,0:T(8,128)(2,1)S(1)} collective-permute-done((bf16[512,256]{1,0:T(8,128)(2,1)S(1)}, bf16[512,256]{1,0:T(8,128)(2,1)S(1)}, u32[]{:S(2)}, u32[]{:S(2)}) %collective-permute-start.4) | collective-permute-done | bytes 262176 | tf_op jit(solution)/shard_map/ppermute | solution.py:50
  29.9 2.6 %collective-permute-start.10 = (bf16[1536,256]{1,0:T(8,128)(2,1)S(1)}, bf16[1536,256]{1,0:T(8,128)(2,1)S(1)}, u32[]{:S(2)}, u32[]{:S(2)}) collective-permute-start(bf16[1536,256]{1,0:T(8,128)(2,1)S(1)} %constant_dynamic-update-slice_fusion.refs_0_), channel_id=1, source_target_pairs={{64,0},{128,64},{192,128},{0,192},{65,1},{129,65},{193,129},{1,193... | collective-permute-start | bytes 2359304 | tf_op jit(solution)/shard_map/ppermute | solution.py:50
  33.9 6.2 %collective-permute-done.5 = bf16[512,256]{1,0:T(8,128)(2,1)S(1)} collective-permute-done((bf16[512,256]{1,0:T(8,128)(2,1)S(1)}, bf16[512,256]{1,0:T(8,128)(2,1)S(1)}, u32[]{:S(2)}, u32[]{:S(2)}) %collective-permute-start.5) | collective-permute-done | bytes 262176 | tf_op jit(solution)/shard_map/ppermute | solution.py:50
  41.0 1.4 collective-permute-done.6
  42.4 1.9 %collective-permute-done.10.refs_0_ = bf16[1536,256]{1,0:T(8,128)(2,1)S(1)} collective-permute-done((bf16[1536,256]{1,0:T(8,128)(2,1)S(1)}, bf16[1536,256]{1,0:T(8,128)(2,1)S(1)}, u32[]{:S(2)}, u32[]{:S(2)}) %collective-permute-start.10) | collective-permute-done | bytes 786464 | tf_op jit(solution)/shard_map/ppermute | solution.py:50
  44.3 3.6 %collective-permute-start.11 = (bf16[768,256]{1,0:T(8,128)(2,1)S(1)}, bf16[768,256]{1,0:T(8,128)(2,1)S(1)}, u32[]{:S(2)}, u32[]{:S(2)}) collective-permute-start(bf16[768,256]{1,0:T(8,128)(2,1)S(1)} %slice.46), channel_id=1, source_target_pairs={{64,0},{128,64},{192,128},{0,192},{65,1},{129,65},{193,129},{1,193... | collective-permute-start | bytes 1179656 | tf_op jit(solution)/shard_map/ppermute | solution.py:50
  49.7 2.3 %collective-permute-start.9 = (bf16[256,256]{1,0:T(8,128)(2,1)S(1)}, bf16[256,256]{1,0:T(8,128)(2,1)S(1)}, u32[]{:S(2)}, u32[]{:S(2)}) collective-permute-start(bf16[256,256]{1,0:T(8,128)(2,1)S(1)} %slice.45), channel_id=1, source_target_pairs={{2,0},{4,2},{6,4},{8,6},{10,8},{12,10},{14,12},{0,14},{3,1},{5,3},... | collective-permute-start | bytes 393224 | tf_op jit(solution)/shard_map/ppermute | solution.py:50
  54.5 3.0 %collective-permute-done.13.refs_1_ = bf16[768,256]{1,0:T(8,128)(2,1)S(1)} collective-permute-done((bf16[768,256]{1,0:T(8,128)(2,1)S(1)}, bf16[768,256]{1,0:T(8,128)(2,1)S(1)}, u32[]{:S(2)}, u32[]{:S(2)}) %collective-permute-start.13) | collective-permute-done | bytes 393248 | tf_op jit(solution)/shard_map/ppermute | solution.py:50
  61.6 2.7 %collective-permute-start.15 = (bf16[2560,256]{1,0:T(8,128)(2,1)}, bf16[2560,256]{1,0:T(8,128)(2,1)S(1)}, u32[]{:S(2)}, u32[]{:S(2)}) collective-permute-start(bf16[2560,256]{1,0:T(8,128)(2,1)} %add_dynamic-update-slice_fusion.refs_1_), channel_id=1, source_target_pairs={{64,0},{128,64},{192,128},{0,192},{65,1},{129,65},{193,129},{1,193... | collective-permute-start | bytes 3932168 | tf_op jit(solution)/shard_map/ppermute | solution.py:50
  67.6 6.1 %all-to-all-start = ((f32[32,8,128]{2,1,0:T(8,128)}), f32[32,8,128]{2,1,0:T(8,128)S(1)}, u32[]{:S(2)}, u32[]{:S(2)}) async-start(f32[32,8,128]{2,1,0:T(8,128)} %copy-done.12), calls=%async_computation | async-start | bytes 262144 | tf_op jit(solution)/shard_map/all_to_all | solution.py:54
  73.8 2.9 %copy-done.2 = bf16[1,3,256,4096]{3,2,1,0:T(8,128)(2,1)S(1)} copy-done((bf16[1,3,256,4096]{3,2,1,0:T(8,128)(2,1)S(1)}, bf16[1,3,256,4096]{3,2,1,0:T(8,128)(2,1)}, u32[]{:S(2)}) %copy-start.2) | copy-done | bytes 6291480
  76.7 5.7 %shard_map.97 = (bf16[768,4096]{1,0:T(8,128)(2,1)S(1)}, bf16[768,4096]{1,0:T(8,128)(2,1)S(1)}) custom-call(s32[6]{0:T(128)S(1)} %pad_add_fusion.pos, bf16[768,4096]{1,0:T(8,128)(2,1)S(1)} %bitcast.11, bf16[1,4096]{1,0:T(2,128)(2,1)S(1)} %broadcast_in_dim.7.gain_ref), custom_call_target="tpu_custom_call" | custom-call | flops 18874368 | bytes 18874368 | tf_op jit(solution)/shard_map/pallas_call | solution.py:97
  82.4 2.6 %copy-done = bf16[768,4096]{1,0:T(8,128)(2,1)} copy-done((bf16[768,4096]{1,0:T(8,128)(2,1)}, bf16[768,4096]{1,0:T(8,128)(2,1)S(1)}, u32[]{:S(2)}) %copy-start) | copy-done | bytes 6291480
  85.5 2.7 %copy-done.21 = bf16[768,4096]{1,0:T(8,128)(2,1)} copy-done((bf16[768,4096]{1,0:T(8,128)(2,1)}, bf16[768,4096]{1,0:T(8,128)(2,1)S(1)}, u32[]{:S(2)}) %copy-start.21) | copy-done | bytes 6291480
  90.7 2.7 %collective-permute-start.16 = (bf16[1280,256]{1,0:T(8,128)(2,1)}, bf16[1280,256]{1,0:T(8,128)(2,1)}, u32[]{:S(2)}, u32[]{:S(2)}) collective-permute-start(bf16[1280,256]{1,0:T(8,128)(2,1)} %slice_add_fusion.1), channel_id=1, source_target_pairs={{64,0},{128,64},{192,128},{0,192},{65,1},{129,65},{193,129},{1,193... | collective-permute-start | bytes 1966088 | tf_op jit(solution)/shard_map/ppermute | solution.py:50
  94.6 9.5 %all-to-all-start.1 = ((f32[32,8,128]{2,1,0:T(8,128)}), f32[32,8,128]{2,1,0:T(8,128)S(1)}, u32[]{:S(2)}, u32[]{:S(2)}) async-start(f32[32,8,128]{2,1,0:T(8,128)} %copy-done.11), calls=%async_computation.1 | async-start | bytes 262144 | tf_op jit(solution)/shard_map/all_to_all | solution.py:54
  104.1 2.8 %copy-done.1 = bf16[768,4096]{1,0:T(8,128)(2,1)S(1)} copy-done((bf16[768,4096]{1,0:T(8,128)(2,1)S(1)}, bf16[768,4096]{1,0:T(8,128)(2,1)}, u32[]{:S(2)}) %copy-start.1) | copy-done | bytes 6291480
  108.1 3.2 %shard_map.99.refs_0_ = bf16[768,256]{1,0:T(8,128)(2,1)S(1)} custom-call(bf16[768,4096]{1,0:T(8,128)(2,1)S(1)} %copy-done.1, bf16[1536,256]{1,0:T(8,128)(2,1)S(1)} %copy-done.10, bf16[2560,256]{1,0:T(8,128)(2,1)} %add_dynamic-update-slice_fusion.refs_1_), custom_call_target="tpu_custom_call" | custom-call | flops 1610612736 | bytes 8781824 | tf_op jit(solution)/shard_map/pallas_call | solution.py:131
  112.0 1.8 shard_map.102.refs_3_
  113.9 1.8 shard_map.100.refs_1_
  115.7 3.1 %shard_map.101.refs_2_ = bf16[768,256]{1,0:T(8,128)(2,1)S(1)} custom-call(bf16[768,4096]{1,0:T(8,128)(2,1)S(1)} %copy-done.1, bf16[768,256]{1,0:T(8,128)(2,1)S(1)} %copy-done.14, bf16[768,256]{1,0:T(8,128)(2,1)S(1)} %copy-done.16, bf16[1280,256]{1,0:T(8,128)(2,1)} %collective-permute-done.16.refs_2_, bf16[1280,256]{1,0:T(8,128)(2,1)} %collective-permute-done.18.refs_3_), custom_call_target="tpu_custom_call" | custom-call | flops 1610612736 | bytes 8781824 | tf_op jit(solution)/shard_map/pallas_call | solution.py:131
  118.8 3.4 %copy-done.20 = bf16[4096,1024]{1,0:T(8,128)(2,1)S(1)} copy-done((bf16[4096,1024]{1,0:T(8,128)(2,1)S(1)}, bf16[4096,1024]{1,0:T(8,128)(2,1)}, u32[]{:S(2)}) %copy-start.20) | copy-done | bytes 8388632
  122.3 2.8 %copy-done.22 = bf16[768,4096]{1,0:T(8,128)(2,1)S(1)} copy-done((bf16[768,4096]{1,0:T(8,128)(2,1)S(1)}, bf16[768,4096]{1,0:T(8,128)(2,1)}, u32[]{:S(2)}) %copy-start.22) | copy-done | bytes 6291480
  125.1 6.7 %shard_map.98.v_ref = bf16[768,1024]{1,0:T(8,128)(2,1)S(1)} custom-call(bf16[768,4096]{1,0:T(8,128)(2,1)S(1)} %copy-done.22, bf16[4096,1024]{1,0:T(8,128)(2,1)S(1)} %copy-done.20), custom_call_target="tpu_custom_call" | custom-call | flops 6442450944 | bytes 16252928 | tf_op jit(solution)/shard_map/pallas_call | solution.py:131
  131.7 2.2 %shard_map.103 = (f32[32,9,128]{2,1,0:T(8,128)S(1)}, f32[3,32,128]{2,1,0:T(8,128)S(1)}) custom-call(s32[6]{0:T(128)S(1)} %pad_add_fusion.pos, f32[32,8,128]{2,1,0:T(8,128)S(1)} %all-to-all-done.1.q_ref, bf16[768,1024]{1,0:T(8,128)(2,1)S(1)} %shard_map.98.v_ref, bf16[768,256]{1,0:T(8,128)(2,1)S(1)} %copy-done.6, bf16[768,256]{1,0:T(8,128)(2,1)S(1)} %shard_map.100.refs_1_, ...), custom_call_target="tpu_custom_call" | custom-call | flops 805306368 | bytes 1048576 | tf_op jit(solution)/shard_map/pallas_call | solution.py:37
  134.0 18.7 %all_to_all.20.got_ref = f32[32,9,128]{2,1,0:T(8,128)S(1)} all-to-all(f32[32,9,128]{2,1,0:T(8,128)S(1)} %get-tuple-element.8.parts_ref), channel_id=1, replica_groups=mesh['dp'=4,'y'=4,'z'=8,'tp'=2] {'y','z'}, dimensions={0} | all-to-all | bytes 294912 | tf_op jit(solution)/shard_map/all_to_all | solution.py:54
  153.5 13.8 %all_to_all.21.ctx_ref = f32[32,9,128]{2,1,0:T(8,128)S(1)} all-to-all(f32[32,9,128]{2,1,0:T(8,128)S(1)} %shard_map.104), channel_id=1, replica_groups=mesh['dp'=4,'y'=4,'z'=8,'tp'=2] {'y','z'}, dimensions={0} | all-to-all | bytes 294912 | tf_op jit(solution)/shard_map/all_to_all | solution.py:54
  168.1 9.6 %collective-permute-start.19 = (f32[40,128]{1,0:T(8,128)S(1)}, f32[40,128]{1,0:T(8,128)S(1)}, u32[]{:S(2)}, u32[]{:S(2)}) collective-permute-start(f32[40,128]{1,0:T(8,128)S(1)} %shard_map.105), channel_id=1, source_target_pairs={{0,1},{1,0},{2,3},{3,2},{4,5},{5,4},{6,7},{7,6},{8,9},{9,8},{10,11... | collective-permute-start | bytes 61448 | tf_op jit(solution)/shard_map/ppermute | solution.py:299
  (105 shorter events, 25.4 us)
Async XLA Ops:
  7.2 111.6 %all-gather.2.cloned.1.call-start = ((), (), s32[]{:S(2)}) async-start(), calls=%async_computation.4 | async-start | bytes 8650752 | tf_op jit(solution)/shard_map/all_gather | solution.py:268
  8.8 5.0 %collective-permute-start = (bf16[128,256]{1,0:T(8,128)(2,1)S(1)}, bf16[128,256]{1,0:T(8,128)(2,1)S(1)}, u32[]{:S(2)}, u32[]{:S(2)}) collective-permute-start(bf16[128,256]{1,0:T(8,128)(2,1)S(1)} %get-tuple-element.11), channel_id=1, source_target_pairs={{16,0},{32,16},{48,32},{0,48},{17,1},{33,17},{49,33},{1,49},{18,2}... | collective-permute-start | bytes 196616 | tf_op jit(solution)/shard_map/ppermute | solution.py:50
  12.4 4.7 %collective-permute-start.1 = (bf16[128,256]{1,0:T(8,128)(2,1)S(1)}, bf16[128,256]{1,0:T(8,128)(2,1)S(1)}, u32[]{:S(2)}, u32[]{:S(2)}) collective-permute-start(bf16[128,256]{1,0:T(8,128)(2,1)S(1)} %get-tuple-element.11), channel_id=1, source_target_pairs={{32,0},{48,16},{0,32},{16,48},{33,1},{49,17},{1,33},{17,49},{34,2}... | collective-permute-start | bytes 196616 | tf_op jit(solution)/shard_map/ppermute | solution.py:50
  12.8 5.0 %collective-permute-start.2 = (bf16[128,256]{1,0:T(8,128)(2,1)S(1)}, bf16[128,256]{1,0:T(8,128)(2,1)S(1)}, u32[]{:S(2)}, u32[]{:S(2)}) collective-permute-start(bf16[128,256]{1,0:T(8,128)(2,1)S(1)} %get-tuple-element.11), channel_id=1, source_target_pairs={{48,0},{0,16},{16,32},{32,48},{49,1},{1,17},{17,33},{33,49},{50,2}... | collective-permute-start | bytes 196616 | tf_op jit(solution)/shard_map/ppermute | solution.py:50
  17.7 9.0 %collective-permute-start.3 = (bf16[512,256]{1,0:T(8,128)(2,1)S(1)}, bf16[512,256]{1,0:T(8,128)(2,1)S(1)}, u32[]{:S(2)}, u32[]{:S(2)}) collective-permute-start(bf16[512,256]{1,0:T(8,128)(2,1)S(1)} %pad_maximum_fusion), channel_id=1, source_target_pairs={{2,0},{4,2},{6,4},{8,6},{10,8},{12,10},{14,12},{0,14},{3,1},{5,3},... | collective-permute-start | bytes 786440 | tf_op jit(solution)/shard_map/ppermute | solution.py:50
  23.4 6.4 %collective-permute-start.4 = (bf16[512,256]{1,0:T(8,128)(2,1)S(1)}, bf16[512,256]{1,0:T(8,128)(2,1)S(1)}, u32[]{:S(2)}, u32[]{:S(2)}) collective-permute-start(bf16[512,256]{1,0:T(8,128)(2,1)S(1)} %pad_maximum_fusion), channel_id=1, source_target_pairs={{14,0},{0,2},{2,4},{4,6},{6,8},{8,10},{10,12},{12,14},{15,1},{1,3}... | collective-permute-start | bytes 786440 | tf_op jit(solution)/shard_map/ppermute | solution.py:50
  29.9 19.8 %copy-start.9 = (bf16[1536,256]{1,0:T(8,128)(2,1)}, bf16[1536,256]{1,0:T(8,128)(2,1)S(1)}, u32[]{:S(2)}) copy-start(bf16[1536,256]{1,0:T(8,128)(2,1)S(1)} %constant_dynamic-update-slice_fusion.refs_0_) | copy-start | bytes 2359300
  29.9 14.4 %collective-permute-start.10 = (bf16[1536,256]{1,0:T(8,128)(2,1)S(1)}, bf16[1536,256]{1,0:T(8,128)(2,1)S(1)}, u32[]{:S(2)}, u32[]{:S(2)}) collective-permute-start(bf16[1536,256]{1,0:T(8,128)(2,1)S(1)} %constant_dynamic-update-slice_fusion.refs_0_), channel_id=1, source_target_pairs={{64,0},{128,64},{192,128},{0,192},{65,1},{129,65},{193,129},{1,193... | collective-permute-start | bytes 2359304 | tf_op jit(solution)/shard_map/ppermute | solution.py:50
  32.4 15.5 %collective-permute-start.12 = (bf16[1536,256]{1,0:T(8,128)(2,1)S(1)}, bf16[1536,256]{1,0:T(8,128)(2,1)S(1)}, u32[]{:S(2)}, u32[]{:S(2)}) collective-permute-start(bf16[1536,256]{1,0:T(8,128)(2,1)S(1)} %constant_dynamic-update-slice_fusion.refs_0_), channel_id=1, source_target_pairs={{192,0},{0,64},{64,128},{128,192},{193,1},{1,65},{65,129},{129,193... | collective-permute-start | bytes 2359304 | tf_op jit(solution)/shard_map/ppermute | solution.py:50
  32.4 7.7 %collective-permute-start.5 = (bf16[512,256]{1,0:T(8,128)(2,1)S(1)}, bf16[512,256]{1,0:T(8,128)(2,1)S(1)}, u32[]{:S(2)}, u32[]{:S(2)}) collective-permute-start(bf16[512,256]{1,0:T(8,128)(2,1)S(1)} %collective-permute-done.3), channel_id=1, source_target_pairs={{2,0},{4,2},{6,4},{8,6},{10,8},{12,10},{14,12},{0,14},{3,1},{5,3},... | collective-permute-start | bytes 786440 | tf_op jit(solution)/shard_map/ppermute | solution.py:50
  32.9 9.4 %collective-permute-start.6 = (bf16[512,256]{1,0:T(8,128)(2,1)S(1)}, bf16[512,256]{1,0:T(8,128)(2,1)S(1)}, u32[]{:S(2)}, u32[]{:S(2)}) collective-permute-start(bf16[512,256]{1,0:T(8,128)(2,1)S(1)} %collective-permute-done.4), channel_id=1, source_target_pairs={{14,0},{0,2},{2,4},{4,6},{6,8},{8,10},{10,12},{12,14},{15,1},{1,3}... | collective-permute-start | bytes 786440 | tf_op jit(solution)/shard_map/ppermute | solution.py:50
  40.1 9.5 %collective-permute-start.7 = (bf16[512,256]{1,0:T(8,128)(2,1)S(1)}, bf16[512,256]{1,0:T(8,128)(2,1)S(1)}, u32[]{:S(2)}, u32[]{:S(2)}) collective-permute-start(bf16[512,256]{1,0:T(8,128)(2,1)S(1)} %collective-permute-done.5), channel_id=1, source_target_pairs={{2,0},{4,2},{6,4},{8,6},{10,8},{12,10},{14,12},{0,14},{3,1},{5,3},... | collective-permute-start | bytes 786440 | tf_op jit(solution)/shard_map/ppermute | solution.py:50
  42.4 9.6 %collective-permute-start.8 = (bf16[512,256]{1,0:T(8,128)(2,1)S(1)}, bf16[512,256]{1,0:T(8,128)(2,1)S(1)}, u32[]{:S(2)}, u32[]{:S(2)}) collective-permute-start(bf16[512,256]{1,0:T(8,128)(2,1)S(1)} %collective-permute-done.6), channel_id=1, source_target_pairs={{14,0},{0,2},{2,4},{4,6},{6,8},{8,10},{10,12},{12,14},{15,1},{1,3}... | collective-permute-start | bytes 786440 | tf_op jit(solution)/shard_map/ppermute | solution.py:50
  44.3 9.7 %collective-permute-start.11 = (bf16[768,256]{1,0:T(8,128)(2,1)S(1)}, bf16[768,256]{1,0:T(8,128)(2,1)S(1)}, u32[]{:S(2)}, u32[]{:S(2)}) collective-permute-start(bf16[768,256]{1,0:T(8,128)(2,1)S(1)} %slice.46), channel_id=1, source_target_pairs={{64,0},{128,64},{192,128},{0,192},{65,1},{129,65},{193,129},{1,193... | collective-permute-start | bytes 1179656 | tf_op jit(solution)/shard_map/ppermute | solution.py:50
  47.9 4.9 %copy-start.3 = (bf16[1536,256]{1,0:T(8,128)(2,1)}, bf16[1536,256]{1,0:T(8,128)(2,1)S(1)}, u32[]{:S(2)}) copy-start(bf16[1536,256]{1,0:T(8,128)(2,1)S(1)} %collective-permute-done.12.refs_0_) | copy-start | bytes 2359300
  48.0 9.5 %collective-permute-start.13 = (bf16[768,256]{1,0:T(8,128)(2,1)S(1)}, bf16[768,256]{1,0:T(8,128)(2,1)S(1)}, u32[]{:S(2)}, u32[]{:S(2)}) collective-permute-start(bf16[768,256]{1,0:T(8,128)(2,1)S(1)} %slice.48), channel_id=1, source_target_pairs={{192,0},{0,64},{64,128},{128,192},{193,1},{1,65},{65,129},{129,193... | collective-permute-start | bytes 1179656 | tf_op jit(solution)/shard_map/ppermute | solution.py:50
  48.9 15.3 %copy-start.24 = (s32[1,3]{1,0:T(1,128)S(1)}, s32[1,3]{1,0:T(1,128)}, u32[]{:S(2)}) copy-start(s32[1,3]{1,0:T(1,128)} %param.9) | copy-start | bytes 40
  49.7 10.5 %collective-permute-start.9 = (bf16[256,256]{1,0:T(8,128)(2,1)S(1)}, bf16[256,256]{1,0:T(8,128)(2,1)S(1)}, u32[]{:S(2)}, u32[]{:S(2)}) collective-permute-start(bf16[256,256]{1,0:T(8,128)(2,1)S(1)} %slice.45), channel_id=1, source_target_pairs={{2,0},{4,2},{6,4},{8,6},{10,8},{12,10},{14,12},{0,14},{3,1},{5,3},... | collective-permute-start | bytes 393224 | tf_op jit(solution)/shard_map/ppermute | solution.py:50
  52.0 21.8 %copy-start.23 = (bf16[4096]{0:T(1024)(128)(2,1)S(1)}, bf16[4096]{0:T(1024)(128)(2,1)}, u32[]{:S(2)}) copy-start(bf16[4096]{0:T(1024)(128)(2,1)} %param.10) | copy-start | bytes 24580
  52.0 8.9 %collective-permute-start.14 = (bf16[256,256]{1,0:T(8,128)(2,1)S(1)}, bf16[256,256]{1,0:T(8,128)(2,1)S(1)}, u32[]{:S(2)}, u32[]{:S(2)}) collective-permute-start(bf16[256,256]{1,0:T(8,128)(2,1)S(1)} %slice.50), channel_id=1, source_target_pairs={{14,0},{0,2},{2,4},{4,6},{6,8},{8,10},{10,12},{12,14},{15,1},{1,3}... | collective-permute-start | bytes 393224 | tf_op jit(solution)/shard_map/ppermute | solution.py:50
  54.0 7.6 %copy-start.13 = (bf16[768,256]{1,0:T(8,128)(2,1)}, bf16[768,256]{1,0:T(8,128)(2,1)S(1)}, u32[]{:S(2)}) copy-start(bf16[768,256]{1,0:T(8,128)(2,1)S(1)} %collective-permute-done.11.refs_0_) | copy-start | bytes 1179652
  61.6 27.3 %collective-permute-start.17 = (bf16[2560,256]{1,0:T(8,128)(2,1)}, bf16[2560,256]{1,0:T(8,128)(2,1)S(1)}, u32[]{:S(2)}, u32[]{:S(2)}) collective-permute-start(bf16[2560,256]{1,0:T(8,128)(2,1)} %add_dynamic-update-slice_fusion.refs_1_), channel_id=1, source_target_pairs={{192,0},{0,64},{64,128},{128,192},{193,1},{1,65},{65,129},{129,193... | collective-permute-start | bytes 3932168 | tf_op jit(solution)/shard_map/ppermute | solution.py:50
  61.6 28.2 %collective-permute-start.15 = (bf16[2560,256]{1,0:T(8,128)(2,1)}, bf16[2560,256]{1,0:T(8,128)(2,1)S(1)}, u32[]{:S(2)}, u32[]{:S(2)}) collective-permute-start(bf16[2560,256]{1,0:T(8,128)(2,1)} %add_dynamic-update-slice_fusion.refs_1_), channel_id=1, source_target_pairs={{64,0},{128,64},{192,128},{0,192},{65,1},{129,65},{193,129},{1,193... | collective-permute-start | bytes 3932168 | tf_op jit(solution)/shard_map/ppermute | solution.py:50
  67.6 25.7 %all-to-all-start = ((f32[32,8,128]{2,1,0:T(8,128)}), f32[32,8,128]{2,1,0:T(8,128)S(1)}, u32[]{:S(2)}, u32[]{:S(2)}) async-start(f32[32,8,128]{2,1,0:T(8,128)} %copy-done.12), calls=%async_computation | async-start | bytes 262144 | tf_op jit(solution)/shard_map/all_to_all | solution.py:54
  89.8 25.9 %collective-permute-start.18 = (bf16[1280,256]{1,0:T(8,128)(2,1)}, bf16[1280,256]{1,0:T(8,128)(2,1)}, u32[]{:S(2)}, u32[]{:S(2)}) collective-permute-start(bf16[1280,256]{1,0:T(8,128)(2,1)} %slice_add_fusion), channel_id=1, source_target_pairs={{192,0},{0,64},{64,128},{128,192},{193,1},{1,65},{65,129},{129,193... | collective-permute-start | bytes 1966088 | tf_op jit(solution)/shard_map/ppermute | solution.py:50
  90.7 25.0 %collective-permute-start.16 = (bf16[1280,256]{1,0:T(8,128)(2,1)}, bf16[1280,256]{1,0:T(8,128)(2,1)}, u32[]{:S(2)}, u32[]{:S(2)}) collective-permute-start(bf16[1280,256]{1,0:T(8,128)(2,1)} %slice_add_fusion.1), channel_id=1, source_target_pairs={{64,0},{128,64},{192,128},{0,192},{65,1},{129,65},{193,129},{1,193... | collective-permute-start | bytes 1966088 | tf_op jit(solution)/shard_map/ppermute | solution.py:50
  94.6 37.1 %all-to-all-start.1 = ((f32[32,8,128]{2,1,0:T(8,128)}), f32[32,8,128]{2,1,0:T(8,128)S(1)}, u32[]{:S(2)}, u32[]{:S(2)}) async-start(f32[32,8,128]{2,1,0:T(8,128)} %copy-done.11), calls=%async_computation.1 | async-start | bytes 262144 | tf_op jit(solution)/shard_map/all_to_all | solution.py:54
  108.1 3.9 %copy-start.4 = (bf16[1536,256]{1,0:T(8,128)(2,1)S(1)}, bf16[1536,256]{1,0:T(8,128)(2,1)}, u32[]{:S(2)}) copy-start(bf16[1536,256]{1,0:T(8,128)(2,1)} %copy-done.3) | copy-start | bytes 2359300
  118.8 13.0 %copy-start.6 = (bf16[768,256]{1,0:T(8,128)(2,1)S(1)}, bf16[768,256]{1,0:T(8,128)(2,1)}, u32[]{:S(2)}) copy-start(bf16[768,256]{1,0:T(8,128)(2,1)} %copy-done.5) | copy-start | bytes 1179652
  118.8 13.0 %copy-start.8 = (bf16[768,256]{1,0:T(8,128)(2,1)S(1)}, bf16[768,256]{1,0:T(8,128)(2,1)}, u32[]{:S(2)}) copy-start(bf16[768,256]{1,0:T(8,128)(2,1)} %copy-done.7) | copy-start | bytes 1179652
  134.0 33.4 %copy-start.17 = (bf16[1024,128]{1,0:T(8,128)(2,1)S(1)}, bf16[1024,128]{1,0:T(8,128)(2,1)}, u32[]{:S(2)}) copy-start(bf16[1024,128]{1,0:T(8,128)(2,1)} %w_ref.3) | copy-start | bytes 786436
  168.1 10.4 %collective-permute-start.19 = (f32[40,128]{1,0:T(8,128)S(1)}, f32[40,128]{1,0:T(8,128)S(1)}, u32[]{:S(2)}, u32[]{:S(2)}) collective-permute-start(f32[40,128]{1,0:T(8,128)S(1)} %shard_map.105), channel_id=1, source_target_pairs={{0,1},{1,0},{2,3},{3,2},{4,5},{5,4},{6,7},{7,6},{8,9},{9,8},{10,11... | collective-permute-start | bytes 61448 | tf_op jit(solution)/shard_map/ppermute | solution.py:299
  (16 other events, 28.6 us)
Sparse Core Ops, SparseCore 0:
  10.6 106.7 all-gather.1

commit v3 on v2

--- a/solution.py
+++ b/solution.py
@@ -17,6 +17,7 @@
 SIZES = {"dp": NX, "y": NY, "z": NZ}
 VMEM = pl.BlockSpec(memory_space=pltpu.VMEM)
 SMEM = pl.BlockSpec(memory_space=pltpu.SMEM)
+HBM = pl.BlockSpec(memory_space=pltpu.HBM)
 f32 = jnp.float32
 bf16 = jnp.bfloat16
 
@@ -32,8 +33,8 @@
     return pltpu.CompilerParams(vmem_limit_bytes=mib * 1024 * 1024)
 
 
-def call(kernel, outs, scratch, *args, mib=16, flops=0):
-    specs = [SMEM] + [VMEM] * (len(args) - 1)
+def call(kernel, outs, scratch, *args, mib=8, flops=0, hbm=()):
+    specs = [SMEM] + [HBM if i in hbm else VMEM for i in range(1, len(args))]
     return pl.pallas_call(
         kernel,
         out_shape=outs,
@@ -65,7 +66,7 @@
     return sum(a[(0,) * a.ndim].astype(bf16) for a in arrays) * 0
 
 
-def gather(shard, after):
+def gather(shard, use, early):
     block = jnp.concatenate(
         [shard, recv(shard, "y", 1), recv(shard, "y", 2), recv(shard, "y", -1)], axis=0
     )
@@ -74,21 +75,26 @@
     near = round_x(jnp.concatenate([block, up1, down1], axis=0), 0)
     up2, down2 = recv(up1, "z", 1), recv(down1, "z", -1)
     up3, down3 = recv(up2, "z", 1), recv(down2, "z", -1)
-    last = first_of(*near[2])
+    last = first_of(*near[2], *early)
     far = (recv(up3[:half], "z", 1) + last, recv(down3[half:], "z", -1) + last)
-    rest = round_x(jnp.concatenate([up2, down2, up3, down3, *far], axis=0), after)
-    return [near[dx] + rest[dx] for dx in range(NX)]
-
-
-def norm_kernel(pos, e_ref, gain_ref, plain_ref, turned_ref):
+    group = jnp.concatenate([up2, down2, up3, down3, *far], axis=0)
+    own = use(near[0] + [group])
+    rest = round_x(group, first_of(own))
+    return [own] + [use(near[dx] + rest[dx]) for dx in range(1, NX)]
+
+
+def place(pos, i):
+    dy, dz = ORDER[i]
+    at = lax.rem(pos[0] + dy, NY) * NZ + lax.rem(pos[1] + dz, NZ)
+    return pl.multiple_of(at * LANES, LANES)
+
+
+def norm_kernel(pos, e_ref, gain_ref, out_ref, rows):
     e = e_ref[...].astype(f32)
     scale = lax.rsqrt(jnp.mean(e * e, axis=-1, keepdims=True) + 1e-06)
-    plain_ref[...] = (e * scale * gain_ref[...].astype(f32)).astype(bf16)
-    for i, (dy, dz) in enumerate(ORDER):
-        at = lax.rem(pos[0] + dy, NY) * NZ + lax.rem(pos[1] + dz, NZ)
-        turned_ref[:, i * LANES : (i + 1) * LANES] = plain_ref[
-            :, pl.ds(pl.multiple_of(at * LANES, LANES), LANES)
-        ]
+    rows[...] = (e * scale * gain_ref[...].astype(f32)).astype(bf16)
+    for i in range(len(ORDER)):
+        out_ref[:, i * LANES : (i + 1) * LANES] = rows[:, pl.ds(place(pos, i), LANES)]
 
 
 def normalise(pos, enc, gain, tile):
@@ -96,16 +102,17 @@
     block = pl.BlockSpec((tile, width), lambda i, pos: (i, 0))
     return pl.pallas_call(
         norm_kernel,
-        out_shape=[shaped((rows, width), bf16)] * 2,
+        out_shape=shaped((rows, width), bf16),
         grid_spec=pltpu.PrefetchScalarGridSpec(
             num_scalar_prefetch=1,
             grid=(rows // tile,),
             in_specs=[block, pl.BlockSpec((1, width), lambda i, pos: (0, 0))],
-            out_specs=[block, block],
+            out_specs=block,
+            scratch_shapes=[pltpu.VMEM((tile, width), bf16)],
         ),
-        compiler_params=params(32),
+        compiler_params=params(12),
         cost_estimate=pl.CostEstimate(
-            flops=6 * rows * width, bytes_accessed=6 * rows * width, transcendentals=0
+            flops=6 * rows * width, bytes_accessed=4 * rows * width, transcendentals=0
         ),
     )(pos, enc, gain)
 
@@ -133,7 +140,7 @@
         out_shape=shaped((rows, cols), bf16),
         in_specs=[VMEM] * (1 + len(pieces)),
         out_specs=VMEM,
-        compiler_params=params(16),
+        compiler_params=params(8),
         cost_estimate=pl.CostEstimate(
             flops=2 * rows * width * cols,
             bytes_accessed=2 * (rows * width + width * cols + rows * cols),
@@ -160,17 +167,16 @@
     return row == col
 
 
-def attend_kernel(plen, pos, q_ref, v_ref, *refs):
-    keys, (out_ref, mass_ref) = refs[:NX], refs[NX:]
+def softmax_kernel(plen, pos, q_ref, *refs):
+    keys, (high_ref, low_ref, stat_ref, mass_ref) = refs[:NX], refs[NX:]
     answers = q_ref.shape[0]
     lane = lax.broadcasted_iota(jnp.int32, (answers, LANES), 1)
-    last = out_ref.shape[1] - 1
     stats = jnp.zeros((answers, LANES), f32)
-    passages = v_ref.shape[0] // plen
-    masses = [stats] * passages
+    masses = [stats] * mass_ref.shape[0]
     for dx, key_ref in enumerate(keys):
         quarter = lax.rem(pos[2] + dx, NX)
         slots, cols = key_ref.shape
+        passages = slots // plen
         heads = cols // HDIM
         pairs = heads * answers
         blocks = cols // LANES
@@ -178,8 +184,9 @@
             [q_ref[:, pl.ds(quarter * blocks + j, 1), :].reshape(answers, LANES) for j in range(blocks)],
             axis=1,
         )
-        own = same_head(pairs, cols, answers)
-        spread = jnp.where(own, jnp.concatenate([q] * heads, axis=0), 0.0).astype(bf16)
+        spread = jnp.where(
+            same_head(pairs, cols, answers), jnp.concatenate([q] * heads, axis=0), 0.0
+        ).astype(bf16)
         logits = lax.dot_general(
             spread, key_ref[...], (((1,), (1,)), ((), ())), preferred_element_type=f32
         ) * HDIM ** (-0.5)
@@ -200,21 +207,53 @@
             masses = [jnp.where(lane == head, s[at, :], m) for s, m in zip(sums, masses)]
         whole = jnp.concatenate(p, axis=1)
         high = whole.astype(bf16)
-        low = (whole - high.astype(f32)).astype(bf16)
-        v = v_ref[:, pl.ds(pl.multiple_of(quarter * cols, cols), cols)]
-        numer = jnp.dot(high, v, preferred_element_type=f32)
-        numer += jnp.dot(low, v, preferred_element_type=f32)
-        numer = jnp.where(own, numer, 0.0)
-        rows = numer[0:answers, :]
-        for h in range(1, heads):
-            rows = rows + numer[h * answers : (h + 1) * answers, :]
+        at = slice(dx * pairs, (dx + 1) * pairs)
+        high_ref[at, :] = high
+        low_ref[at, :] = (whole - high.astype(f32)).astype(bf16)
+    stat_ref[...] = stats
+    for i, mass in enumerate(masses):
+        mass_ref[i] = mass
+
+
+def value_kernel(pos, x_ref, high_ref, low_ref, stat_ref, v_hbm, out_ref, buf, acc, sems):
+    answers, rows, _ = out_ref.shape
+    pairs = high_ref.shape[0] // NX
+    cols = buf.shape[1] // NX
+    blocks = cols // LANES
+    half = len(ORDER) // 2
+
+    def fetch(i):
+        return pltpu.make_async_copy(
+            v_hbm.at[pl.ds(place(pos, i), LANES), :],
+            buf.at[pl.ds(i * LANES, LANES), :],
+            sems.at[i],
+        )
+
+    for i in range(len(ORDER)):
+        fetch(i).start()
+    for part in range(2):
+        for i in range(part * half, (part + 1) * half):
+            fetch(i).wait()
+        at = slice(part * half * LANES, (part + 1) * half * LANES)
+        for g in range(NX):
+            col = slice(g * cols, (g + 1) * cols)
+            v = jnp.dot(x_ref[:, at], buf[at, col], preferred_element_type=f32)
+            acc[:, col] = v if part == 0 else acc[:, col] + v
+    for dx in range(NX):
+        quarter = lax.rem(pos[2] + dx, NX)
+        v = acc[:, pl.ds(pl.multiple_of(quarter * cols, cols), cols)].astype(bf16)
+        at = slice(dx * pairs, (dx + 1) * pairs)
+        numer = jnp.dot(high_ref[at, :], v, preferred_element_type=f32)
+        numer += jnp.dot(low_ref[at, :], v, preferred_element_type=f32)
+        numer = jnp.where(same_head(pairs, cols, answers), numer, 0.0)
+        total = numer[0:answers, :]
+        for h in range(1, pairs // answers):
+            total = total + numer[h * answers : (h + 1) * answers, :]
         for j in range(blocks):
-            out_ref[:, pl.ds(quarter * blocks + j, 1), :] = rows[
+            out_ref[:, pl.ds(quarter * blocks + j, 1), :] = total[
                 :, j * LANES : (j + 1) * LANES
             ].reshape(answers, 1, LANES)
-    out_ref[:, last, :] = stats
-    for i, mass in enumerate(masses):
-        mass_ref[i] = mass
+    out_ref[:, rows - 1, :] = stat_ref[...]
 
 
 def by_head(lane, row, j):
@@ -237,7 +276,7 @@
     out_ref[:, last, :] = jnp.broadcast_to(row, scale.shape)
 
 
-def out_kernel(pos, ctx_ref, parts_ref, mass_ref, w_ref, out_ref):
+def out_kernel(pos, ctx_ref, stat_ref, mass_ref, w_ref, out_ref):
     answers, rows, _ = ctx_ref.shape
     last = rows - 1
     ctx = jnp.concatenate([ctx_ref[:, j, :] for j in range(last)], axis=1).astype(bf16)
@@ -246,11 +285,20 @@
     lane = lax.broadcasted_iota(jnp.int32, merged.shape, 1)
     heads = last * LANES // HDIM
     total = jnp.where(lane < heads, pltpu.roll(merged, LANES // 2, 1), 1.0)
-    gap = jnp.where(lane < heads, parts_ref[:, last, :] - merged, 0.0)
+    gap = jnp.where(lane < heads, stat_ref[...] - merged, 0.0)
     factor = jnp.exp(gap) / total
-    for i in range(8):
-        part = jnp.sum(mass_ref[i] * factor, keepdims=True) if i < mass_ref.shape[0] else 0.0
-        out_ref[answers + i : answers + i + 1, :] = jnp.broadcast_to(part, (1, LANES))
+    first = lax.broadcasted_iota(jnp.int32, (8, LANES), 1)
+    scores = jnp.zeros((8, LANES), f32)
+    for i in range(mass_ref.shape[0]):
+        scores = jnp.where(first == i, jnp.sum(mass_ref[i] * factor, keepdims=True), scores)
+    out_ref[answers : answers + 8, :] = scores
+
+
+def last_kernel(scale, pos, own_ref, other_ref, out_ref, scores_ref):
+    both = own_ref[...] + other_ref[...]
+    answers = out_ref.shape[0]
+    out_ref[...] = both[:answers].astype(bf16)
+    scores_ref[...] = both[answers : answers + 1, : scores_ref.shape[1]] * scale
 
 
 def body(enc_states, lengths, enc_gain, dec_states, w_query, w_key, w_value, w_out):
@@ -266,7 +314,9 @@
     pos = jnp.concatenate([jnp.stack([y, z, x]), lengths.reshape(pdev)])
 
     w_values = lax.all_gather(w_value, PSG, axis=0, tiled=True)
-    plain, turned = normalise(pos, enc_states.reshape(slots, width), enc_gain[None], plen)
+    normed = normalise(
+        pos, enc_states.reshape(slots, width), enc_gain[None], min(slots, 128)
+    )
     q_parts = call(
         query_kernel,
         shaped((answers, blocks, LANES)),
@@ -279,26 +329,60 @@
     queries = exchange(q_sum)
 
     mine = lax.dynamic_slice(w_key, (0, x * quarter), (w_key.shape[0], quarter))
-    keys = [project(turned, pieces) for pieces in gather(mine, first_of(plain))]
-    values = project(plain, [w_values])
-    parts, mass = call(
-        functools.partial(attend_kernel, plen),
-        [shaped((answers, blocks + 1, LANES)), shaped((pdev, answers, LANES))],
+    keys = gather(mine, functools.partial(project, normed), [q_sum])
+    high, low, stat, mass = call(
+        functools.partial(softmax_kernel, plen),
+        [
+            shaped((pairs, slots), bf16),
+            shaped((pairs, slots), bf16),
+            shaped((answers, LANES)),
+            shaped((pdev, answers, LANES)),
+        ],
         [],
         pos,
         queries,
-        values,
         *keys,
-        flops=4 * pairs * slots * quarter * 2,
+        flops=2 * pairs * slots * quarter,
+    )
+    parts = call(
+        value_kernel,
+        shaped((answers, blocks + 1, LANES)),
+        [
+            pltpu.VMEM((width, columns), bf16),
+            pltpu.VMEM((slots, columns), f32),
+            pltpu.SemaphoreType.DMA((len(ORDER),)),
+        ],
+        pos,
+        normed,
+        high,
+        low,
+        stat,
+        w_values,
+        mib=46,
+        flops=2 * slots * width * columns,
+        hbm=(5,),
     )
     merged = call(merge_kernel, shaped(parts.shape), [], pos, exchange(parts))
-    context = exchange(merged)
     part = call(
-        out_kernel, shaped((answers + 8, w_out.shape[1])), [], pos, context, parts, mass, w_out
-    )
-    both = part + lax.ppermute(part, "tp", [(0, 1), (1, 0)])
-    scores = both[answers : answers + pdev, 0] * (pdev * members / (HEADS * answers))
-    return both[:answers].astype(bf16)[None], scores[None]
+        out_kernel,
+        shaped((answers + 8, w_out.shape[1])),
+        [],
+        pos,
+        exchange(merged),
+        stat,
+        mass,
+        w_out,
+    )
+    other = lax.ppermute(part, "tp", [(0, 1), (1, 0)])
+    attended, scores = call(
+        functools.partial(last_kernel, pdev * members / (HEADS * answers)),
+        [shaped((answers, w_out.shape[1]), bf16), shaped((1, pdev))],
+        [],
+        pos,
+        part,
+        other,
+    )
+    return attended[None], scores
 
 
 def solution(mesh):

time: 187 us -> 189 us (1.011)
  local copies, waits for them, and re-layouts: 29.3 us -> 20.3 us
  Pallas kernels: 27.3 us -> 33.7 us
  waiting for transfers between devices: 25.2 us -> 27.8 us
    pallas_call x5 -> x7, Pallas kernels: 5.12 us -> 17 us  [call(): pl.pallas_call(kernel, out_shape=outs, in_specs=specs, out_specs=jax.tree...]
    unnamed x59 -> x53, local copies, waits for them, and re-layouts: 27 us -> 17.1 us
    all_to_all x2, waiting for transfers between devices: 0.01 us -> 7.06 us  [exchange(): return lax.all_to_all(a, PSG, split_axis=0, concat_axis=0, tiled=True)]
    ppermute x1, starting transfers between devices: 9.58 us -> 15.5 us  [body(): other = lax.ppermute(part, 'tp', [(0, 1), (1, 0)])]
    pallas_call x5 -> x4, Pallas kernels: 16.5 us -> 10.8 us  [project(): pl.pallas_call(project_kernel, out_shape=shaped((rows, cols), bf16), in_s...]
    all_to_all x2, starting transfers between devices: 15.7 us -> 10.2 us  [exchange(): return lax.all_to_all(a, PSG, split_axis=0, concat_axis=0, tiled=True)]
    ppermute x19, waiting for transfers between devices: 23.6 us -> 18.4 us  [recv(): return lax.ppermute(a, axis, [((i + k) % n, i) for i in range(n)])]
  transfers between devices with their start and end apart: 23 -> 23, of which waited for: 11 -> 9; matrix products, arithmetic and copies ran while one was open for 5% -> 7% of each run, Pallas kernels for 13% -> 11%
where the time goes in v3:
time: 189 us; the launch traced here: 188 us
  starting transfers between devices  52.9 us (28%)
  Pallas kernels  33.7 us (18%)
  blocking collectives  33.3 us (18%)
  waiting for transfers between devices  27.8 us (15%)
  local copies, waits for them, and re-layouts  20.3 us (11%)
  between operations  17 us (9%)
  other arithmetic  3.24 us (2%)
    all_to_all x2, blocking collectives, exchange(): return lax.all_to_all(a, PSG, split_axis=0, concat_axis=0, tiled=True)  33.3 us
    ppermute x19, starting transfers between devices, recv(): return lax.ppermute(a, axis, [((i + k) % n, i) for i in range(n)])  27.2 us
    ppermute x19, waiting for transfers between devices, recv(): return lax.ppermute(a, axis, [((i + k) % n, i) for i in range(n)])  18.4 us
    unnamed x53, local copies, waits for them, and re-layouts  17.1 us
    pallas_call x7, Pallas kernels, call(): pl.pallas_call(kernel, out_shape=outs, in_specs=specs, out_specs=jax.tree...  17 us
    ppermute x1, starting transfers between devices, body(): other = lax.ppermute(part, 'tp', [(0, 1), (1, 0)])  15.5 us
    pallas_call x4, Pallas kernels, project(): pl.pallas_call(project_kernel, out_shape=shaped((rows, cols), bf16), in_s...  10.8 us
    all_to_all x2, starting transfers between devices, exchange(): return lax.all_to_all(a, PSG, split_axis=0, concat_axis=0, tiled=True)  10.2 us
  transfers between devices with their start and end apart: 23, of which 9 were waited for; matrix products, arithmetic and copies ran while one was open for 7% of the time, Pallas kernels for 11%

profile of v3, /device:TPU:1, one launch (start us, length us, event | category | flops | bytes accessed | tf_op | source)
XLA Modules:
  0.0 188.3 jit_solution(13627530356825936002)
XLA Ops:
  8.8 3.6 %collective-permute-start = (bf16[128,256]{1,0:T(8,128)(2,1)S(1)}, bf16[128,256]{1,0:T(8,128)(2,1)S(1)}, u32[]{:S(2)}, u32[]{:S(2)}) collective-permute-start(bf16[128,256]{1,0:T(8,128)(2,1)S(1)} %get-tuple-element.15), channel_id=1, source_target_pairs={{16,0},{32,16},{48,32},{0,48},{17,1},{33,17},{49,33},{1,49},{18,2}... | collective-permute-start | bytes 196616 | tf_op jit(solution)/shard_map/ppermute | solution.py:51
  13.8 3.4 %collective-permute-done.1 = bf16[128,256]{1,0:T(8,128)(2,1)S(1)} collective-permute-done((bf16[128,256]{1,0:T(8,128)(2,1)S(1)}, bf16[128,256]{1,0:T(8,128)(2,1)S(1)}, u32[]{:S(2)}, u32[]{:S(2)}) %collective-permute-start.1) | collective-permute-done | bytes 65568 | tf_op jit(solution)/shard_map/ppermute | solution.py:51
  17.8 5.7 %collective-permute-start.3 = (bf16[512,256]{1,0:T(8,128)(2,1)S(1)}, bf16[512,256]{1,0:T(8,128)(2,1)S(1)}, u32[]{:S(2)}, u32[]{:S(2)}) collective-permute-start(bf16[512,256]{1,0:T(8,128)(2,1)S(1)} %pad_maximum_fusion), channel_id=1, source_target_pairs={{2,0},{4,2},{6,4},{8,6},{10,8},{12,10},{14,12},{0,14},{3,1},{5,3},... | collective-permute-start | bytes 786440 | tf_op jit(solution)/shard_map/ppermute | solution.py:51
  23.5 3.3 %collective-permute-done.3 = bf16[512,256]{1,0:T(8,128)(2,1)S(1)} collective-permute-done((bf16[512,256]{1,0:T(8,128)(2,1)S(1)}, bf16[512,256]{1,0:T(8,128)(2,1)S(1)}, u32[]{:S(2)}, u32[]{:S(2)}) %collective-permute-start.3) | collective-permute-done | bytes 262176 | tf_op jit(solution)/shard_map/ppermute | solution.py:51
  26.8 3.1 %collective-permute-done.4 = bf16[512,256]{1,0:T(8,128)(2,1)S(1)} collective-permute-done((bf16[512,256]{1,0:T(8,128)(2,1)S(1)}, bf16[512,256]{1,0:T(8,128)(2,1)S(1)}, u32[]{:S(2)}, u32[]{:S(2)}) %collective-permute-start.4) | collective-permute-done | bytes 262176 | tf_op jit(solution)/shard_map/ppermute | solution.py:51
  29.9 2.6 %collective-permute-start.10 = (bf16[1536,256]{1,0:T(8,128)(2,1)S(1)}, bf16[1536,256]{1,0:T(8,128)(2,1)S(1)}, u32[]{:S(2)}, u32[]{:S(2)}) collective-permute-start(bf16[1536,256]{1,0:T(8,128)(2,1)S(1)} %constant_dynamic-update-slice_fusion.refs_0_), channel_id=1, source_target_pairs={{64,0},{128,64},{192,128},{0,192},{65,1},{129,65},{193,129},{1,193... | collective-permute-start | bytes 2359304 | tf_op jit(solution)/shard_map/ppermute | solution.py:51
  34.0 1.4 shard_map.96
  35.4 5.2 %all-to-all-start = ((f32[32,8,128]{2,1,0:T(8,128)}), f32[32,8,128]{2,1,0:T(8,128)S(1)}, u32[]{:S(2)}, u32[]{:S(2)}) async-start(f32[32,8,128]{2,1,0:T(8,128)} %shard_map.96), calls=%async_computation | async-start | bytes 262144 | tf_op jit(solution)/shard_map/all_to_all | solution.py:55
  40.6 2.5 %collective-permute-start.7 = (bf16[512,256]{1,0:T(8,128)(2,1)}, bf16[512,256]{1,0:T(8,128)(2,1)S(1)}, u32[]{:S(2)}, u32[]{:S(2)}) collective-permute-start(bf16[512,256]{1,0:T(8,128)(2,1)} %collective-permute-done.5), channel_id=1, source_target_pairs={{2,0},{4,2},{6,4},{8,6},{10,8},{12,10},{14,12},{0,14},{3,1},{5,3},... | collective-permute-start | bytes 786440 | tf_op jit(solution)/shard_map/ppermute | solution.py:51
  43.1 7.1 %all-to-all-done.got_ref = f32[32,8,128]{2,1,0:T(8,128)S(1)} async-done(((f32[32,8,128]{2,1,0:T(8,128)}), f32[32,8,128]{2,1,0:T(8,128)S(1)}, u32[]{:S(2)}, u32[]{:S(2)}) %all-to-all-start) | async-done | bytes 131104 | tf_op jit(solution)/shard_map/all_to_all | solution.py:55
  51.3 3.1 %collective-permute-start.11 = (bf16[768,256]{1,0:T(8,128)(2,1)S(1)}, bf16[768,256]{1,0:T(8,128)(2,1)S(1)}, u32[]{:S(2)}, u32[]{:S(2)}) collective-permute-start(bf16[768,256]{1,0:T(8,128)(2,1)S(1)} %slice.42), channel_id=1, source_target_pairs={{64,0},{128,64},{192,128},{0,192},{65,1},{129,65},{193,129},{1,193... | collective-permute-start | bytes 1179656 | tf_op jit(solution)/shard_map/ppermute | solution.py:51
  54.5 1.8 constant_dynamic-update-slice_fusion.9
  56.4 1.7 constant_dynamic-update-slice_fusion.8
  59.1 1.7 collective-permute-start.14
  61.5 1.7 constant_dynamic-update-slice_fusion.6
  68.2 2.7 %collective-permute-start.15 = (bf16[2560,256]{1,0:T(8,128)(2,1)}, bf16[2560,256]{1,0:T(8,128)(2,1)S(1)}, u32[]{:S(2)}, u32[]{:S(2)}) collective-permute-start(bf16[2560,256]{1,0:T(8,128)(2,1)} %add_dynamic-update-slice_fusion.refs_1_), channel_id=1, source_target_pairs={{64,0},{128,64},{192,128},{0,192},{65,1},{129,65},{193,129},{1,193... | collective-permute-start | bytes 3932168 | tf_op jit(solution)/shard_map/ppermute | solution.py:51
  70.9 2.8 %copy-done.3 = bf16[1,3,256,4096]{3,2,1,0:T(8,128)(2,1)S(1)} copy-done((bf16[1,3,256,4096]{3,2,1,0:T(8,128)(2,1)S(1)}, bf16[1,3,256,4096]{3,2,1,0:T(8,128)(2,1)}, u32[]{:S(2)}) %copy-start.3) | copy-done | bytes 6291480
  73.7 5.8 %shard_map.95.x_ref = bf16[768,4096]{1,0:T(8,128)(2,1)S(1)} custom-call(s32[6]{0:T(128)S(1)} %pad_add_fusion.pos, bf16[768,4096]{1,0:T(8,128)(2,1)S(1)} %bitcast.10, bf16[1,4096]{1,0:T(2,128)(2,1)S(1)} %broadcast_in_dim.6.gain_ref), custom_call_target="tpu_custom_call" | custom-call | flops 18874368 | bytes 12582912 | tf_op jit(solution)/shard_map/pallas_call | solution.py:103
  79.6 4.1 %shard_map.98.refs_0_ = bf16[768,256]{1,0:T(8,128)(2,1)S(1)} custom-call(bf16[768,4096]{1,0:T(8,128)(2,1)S(1)} %shard_map.95.x_ref, bf16[1536,256]{1,0:T(8,128)(2,1)S(1)} %copy-done.11, bf16[2560,256]{1,0:T(8,128)(2,1)} %add_dynamic-update-slice_fusion.refs_1_), custom_call_target="tpu_custom_call" | custom-call | flops 1610612736 | bytes 8781824 | tf_op jit(solution)/shard_map/pallas_call | solution.py:138
  85.0 7.7 %collective-permute-done.17.refs_1_ = bf16[2560,256]{1,0:T(8,128)(2,1)S(1)} collective-permute-done((bf16[2560,256]{1,0:T(8,128)(2,1)}, bf16[2560,256]{1,0:T(8,128)(2,1)S(1)}, u32[]{:S(2)}, u32[]{:S(2)}) %collective-permute-start.17) | collective-permute-done | bytes 1310752 | tf_op jit(solution)/shard_map/ppermute | solution.py:51
  94.5 2.7 %collective-permute-start.16 = (bf16[1280,256]{1,0:T(8,128)(2,1)}, bf16[1280,256]{1,0:T(8,128)(2,1)}, u32[]{:S(2)}, u32[]{:S(2)}) collective-permute-start(bf16[1280,256]{1,0:T(8,128)(2,1)} %slice_add_fusion.1), channel_id=1, source_target_pairs={{64,0},{128,64},{192,128},{0,192},{65,1},{129,65},{193,129},{1,193... | collective-permute-start | bytes 1966088 | tf_op jit(solution)/shard_map/ppermute | solution.py:51
  97.2 5.1 %all-to-all-start.1 = ((f32[32,8,128]{2,1,0:T(8,128)}), f32[32,8,128]{2,1,0:T(8,128)S(1)}, u32[]{:S(2)}, u32[]{:S(2)}) async-start(f32[32,8,128]{2,1,0:T(8,128)} %copy-done.12), calls=%async_computation.1 | async-start | bytes 262144 | tf_op jit(solution)/shard_map/all_to_all | solution.py:55
  102.3 2.8 %copy-done.1 = bf16[768,4096]{1,0:T(8,128)(2,1)S(1)} copy-done((bf16[768,4096]{1,0:T(8,128)(2,1)S(1)}, bf16[768,4096]{1,0:T(8,128)(2,1)}, u32[]{:S(2)}) %copy-start.1) | copy-done | bytes 6291480
  106.2 1.8 shard_map.101.refs_3_
  108.0 1.8 shard_map.99.refs_1_
  109.9 3.1 %shard_map.100.refs_2_ = bf16[768,256]{1,0:T(8,128)(2,1)S(1)} custom-call(bf16[768,4096]{1,0:T(8,128)(2,1)S(1)} %copy-done.1, bf16[768,256]{1,0:T(8,128)(2,1)S(1)} %copy-done.14, bf16[768,256]{1,0:T(8,128)(2,1)S(1)} %copy-done.16, bf16[1280,256]{1,0:T(8,128)(2,1)} %collective-permute-done.16.refs_2_, bf16[1280,256]{1,0:T(8,128)(2,1)} %collective-permute-done.18.refs_3_), custom_call_target="tpu_custom_call" | custom-call | flops 1610612736 | bytes 8781824 | tf_op jit(solution)/shard_map/pallas_call | solution.py:138
  113.1 1.6 shard_map.102
  115.6 2.8 %copy-done.2 = bf16[768,4096]{1,0:T(8,128)(2,1)S(1)} copy-done((bf16[768,4096]{1,0:T(8,128)(2,1)S(1)}, bf16[768,4096]{1,0:T(8,128)(2,1)}, u32[]{:S(2)}) %copy-start.2) | copy-done | bytes 6291480
  118.4 10.7 %shard_map.103 = f32[32,9,128]{2,1,0:T(8,128)S(1)} custom-call(s32[6]{0:T(128)S(1)} %pad_add_fusion.pos, bf16[768,4096]{1,0:T(8,128)(2,1)S(1)} %copy-done.2, bf16[512,768]{1,0:T(8,128)(2,1)S(1)} %get-tuple-element.8.high_ref, bf16[512,768]{1,0:T(8,128)(2,1)S(1)} %get-tuple-element.9.low_ref, f32[32,128]{1,0:T(8,128)S(1)} %get-tuple-element.10.stat_ref, ...), custom_call_target="tpu_custom_call" | custom-call | flops 6442450944 | bytes 1048576 | tf_op jit(solution)/shard_map/pallas_call | solution.py:38
  129.0 17.9 %all_to_all.20.got_ref = f32[32,9,128]{2,1,0:T(8,128)S(1)} all-to-all(f32[32,9,128]{2,1,0:T(8,128)S(1)} %shard_map.103), channel_id=1, replica_groups=mesh['dp'=4,'y'=4,'z'=8,'tp'=2] {'y','z'}, dimensions={0} | all-to-all | bytes 294912 | tf_op jit(solution)/shard_map/all_to_all | solution.py:55
  147.7 15.5 %all_to_all.21.ctx_ref = f32[32,9,128]{2,1,0:T(8,128)S(1)} all-to-all(f32[32,9,128]{2,1,0:T(8,128)S(1)} %shard_map.104), channel_id=1, replica_groups=mesh['dp'=4,'y'=4,'z'=8,'tp'=2] {'y','z'}, dimensions={0} | all-to-all | bytes 294912 | tf_op jit(solution)/shard_map/all_to_all | solution.py:55
  164.0 15.5 %collective-permute-start.19 = (f32[40,128]{1,0:T(8,128)S(1)}, f32[40,128]{1,0:T(8,128)S(1)}, u32[]{:S(2)}, u32[]{:S(2)}) collective-permute-start(f32[40,128]{1,0:T(8,128)S(1)} %shard_map.105.own_ref), channel_id=1, source_target_pairs={{0,1},{1,0},{2,3},{3,2},{4,5},{5,4},{6,7},{7,6},{8,9},{9,8},{10,11... | collective-permute-start | bytes 61448 | tf_op jit(solution)/shard_map/ppermute | solution.py:376
  (98 shorter events, 19.3 us)
Async XLA Ops:
  7.2 26.8 %copy-start.21 = (s32[1,3]{1,0:T(1,128)S(1)}, s32[1,3]{1,0:T(1,128)}, u32[]{:S(2)}) copy-start(s32[1,3]{1,0:T(1,128)} %param.9) | copy-start | bytes 40
  7.2 26.8 %copy-start.17 = (bf16[1,32,4096]{2,1,0:T(8,128)(2,1)S(1)}, bf16[1,32,4096]{2,1,0:T(8,128)(2,1)}, u32[]{:S(2)}) copy-start(bf16[1,32,4096]{2,1,0:T(8,128)(2,1)} %param.11) | copy-start | bytes 786436
  7.2 26.8 %copy-start.18 = (bf16[128,1024]{1,0:T(8,128)(2,1)S(1)}, bf16[128,1024]{1,0:T(8,128)(2,1)}, u32[]{:S(2)}) copy-start(bf16[128,1024]{1,0:T(8,128)(2,1)} %w_ref.2) | copy-start | bytes 786436
  7.2 108.4 %all-gather.2.cloned.1.call-start = ((), (), s32[]{:S(2)}) async-start(), calls=%async_computation.4 | async-start | bytes 8650752 | tf_op jit(solution)/shard_map/all_gather | solution.py:316
  8.8 5.0 %collective-permute-start = (bf16[128,256]{1,0:T(8,128)(2,1)S(1)}, bf16[128,256]{1,0:T(8,128)(2,1)S(1)}, u32[]{:S(2)}, u32[]{:S(2)}) collective-permute-start(bf16[128,256]{1,0:T(8,128)(2,1)S(1)} %get-tuple-element.15), channel_id=1, source_target_pairs={{16,0},{32,16},{48,32},{0,48},{17,1},{33,17},{49,33},{1,49},{18,2}... | collective-permute-start | bytes 196616 | tf_op jit(solution)/shard_map/ppermute | solution.py:51
  12.4 4.7 %collective-permute-start.1 = (bf16[128,256]{1,0:T(8,128)(2,1)S(1)}, bf16[128,256]{1,0:T(8,128)(2,1)S(1)}, u32[]{:S(2)}, u32[]{:S(2)}) collective-permute-start(bf16[128,256]{1,0:T(8,128)(2,1)S(1)} %get-tuple-element.15), channel_id=1, source_target_pairs={{32,0},{48,16},{0,32},{16,48},{33,1},{49,17},{1,33},{17,49},{34,2}... | collective-permute-start | bytes 196616 | tf_op jit(solution)/shard_map/ppermute | solution.py:51
  12.8 5.0 %collective-permute-start.2 = (bf16[128,256]{1,0:T(8,128)(2,1)S(1)}, bf16[128,256]{1,0:T(8,128)(2,1)S(1)}, u32[]{:S(2)}, u32[]{:S(2)}) collective-permute-start(bf16[128,256]{1,0:T(8,128)(2,1)S(1)} %get-tuple-element.15), channel_id=1, source_target_pairs={{48,0},{0,16},{16,32},{32,48},{49,1},{1,17},{17,33},{33,49},{50,2}... | collective-permute-start | bytes 196616 | tf_op jit(solution)/shard_map/ppermute | solution.py:51
  17.8 9.0 %collective-permute-start.3 = (bf16[512,256]{1,0:T(8,128)(2,1)S(1)}, bf16[512,256]{1,0:T(8,128)(2,1)S(1)}, u32[]{:S(2)}, u32[]{:S(2)}) collective-permute-start(bf16[512,256]{1,0:T(8,128)(2,1)S(1)} %pad_maximum_fusion), channel_id=1, source_target_pairs={{2,0},{4,2},{6,4},{8,6},{10,8},{12,10},{14,12},{0,14},{3,1},{5,3},... | collective-permute-start | bytes 786440 | tf_op jit(solution)/shard_map/ppermute | solution.py:51
  23.4 6.4 %collective-permute-start.4 = (bf16[512,256]{1,0:T(8,128)(2,1)S(1)}, bf16[512,256]{1,0:T(8,128)(2,1)S(1)}, u32[]{:S(2)}, u32[]{:S(2)}) collective-permute-start(bf16[512,256]{1,0:T(8,128)(2,1)S(1)} %pad_maximum_fusion), channel_id=1, source_target_pairs={{14,0},{0,2},{2,4},{4,6},{6,8},{8,10},{10,12},{12,14},{15,1},{1,3}... | collective-permute-start | bytes 786440 | tf_op jit(solution)/shard_map/ppermute | solution.py:51
  29.9 24.5 %copy-start.10 = (bf16[1536,256]{1,0:T(8,128)(2,1)}, bf16[1536,256]{1,0:T(8,128)(2,1)S(1)}, u32[]{:S(2)}) copy-start(bf16[1536,256]{1,0:T(8,128)(2,1)S(1)} %constant_dynamic-update-slice_fusion.refs_0_) | copy-start | bytes 2359300
  29.9 21.4 %collective-permute-start.10 = (bf16[1536,256]{1,0:T(8,128)(2,1)S(1)}, bf16[1536,256]{1,0:T(8,128)(2,1)S(1)}, u32[]{:S(2)}, u32[]{:S(2)}) collective-permute-start(bf16[1536,256]{1,0:T(8,128)(2,1)S(1)} %constant_dynamic-update-slice_fusion.refs_0_), channel_id=1, source_target_pairs={{64,0},{128,64},{192,128},{0,192},{65,1},{129,65},{193,129},{1,193... | collective-permute-start | bytes 2359304 | tf_op jit(solution)/shard_map/ppermute | solution.py:51
  32.5 21.9 %collective-permute-start.12 = (bf16[1536,256]{1,0:T(8,128)(2,1)S(1)}, bf16[1536,256]{1,0:T(8,128)(2,1)S(1)}, u32[]{:S(2)}, u32[]{:S(2)}) collective-permute-start(bf16[1536,256]{1,0:T(8,128)(2,1)S(1)} %constant_dynamic-update-slice_fusion.refs_0_), channel_id=1, source_target_pairs={{192,0},{0,64},{64,128},{128,192},{193,1},{1,65},{65,129},{129,193... | collective-permute-start | bytes 2359304 | tf_op jit(solution)/shard_map/ppermute | solution.py:51
  32.5 8.1 %collective-permute-start.5 = (bf16[512,256]{1,0:T(8,128)(2,1)S(1)}, bf16[512,256]{1,0:T(8,128)(2,1)}, u32[]{:S(2)}, u32[]{:S(2)}) collective-permute-start(bf16[512,256]{1,0:T(8,128)(2,1)S(1)} %collective-permute-done.3), channel_id=1, source_target_pairs={{2,0},{4,2},{6,4},{8,6},{10,8},{12,10},{14,12},{0,14},{3,1},{5,3},... | collective-permute-start | bytes 786440 | tf_op jit(solution)/shard_map/ppermute | solution.py:51
  33.0 10.1 %collective-permute-start.6 = (bf16[512,256]{1,0:T(8,128)(2,1)S(1)}, bf16[512,256]{1,0:T(8,128)(2,1)}, u32[]{:S(2)}, u32[]{:S(2)}) collective-permute-start(bf16[512,256]{1,0:T(8,128)(2,1)S(1)} %collective-permute-done.4), channel_id=1, source_target_pairs={{14,0},{0,2},{2,4},{4,6},{6,8},{8,10},{10,12},{12,14},{15,1},{1,3}... | collective-permute-start | bytes 786440 | tf_op jit(solution)/shard_map/ppermute | solution.py:51
  35.4 14.8 %all-to-all-start = ((f32[32,8,128]{2,1,0:T(8,128)}), f32[32,8,128]{2,1,0:T(8,128)S(1)}, u32[]{:S(2)}, u32[]{:S(2)}) async-start(f32[32,8,128]{2,1,0:T(8,128)} %shard_map.96), calls=%async_computation | async-start | bytes 262144 | tf_op jit(solution)/shard_map/all_to_all | solution.py:55
  40.6 17.5 %collective-permute-start.7 = (bf16[512,256]{1,0:T(8,128)(2,1)}, bf16[512,256]{1,0:T(8,128)(2,1)S(1)}, u32[]{:S(2)}, u32[]{:S(2)}) collective-permute-start(bf16[512,256]{1,0:T(8,128)(2,1)} %collective-permute-done.5), channel_id=1, source_target_pairs={{2,0},{4,2},{6,4},{8,6},{10,8},{12,10},{14,12},{0,14},{3,1},{5,3},... | collective-permute-start | bytes 786440 | tf_op jit(solution)/shard_map/ppermute | solution.py:51
  43.1 15.1 %collective-permute-start.8 = (bf16[512,256]{1,0:T(8,128)(2,1)}, bf16[512,256]{1,0:T(8,128)(2,1)}, u32[]{:S(2)}, u32[]{:S(2)}) collective-permute-start(bf16[512,256]{1,0:T(8,128)(2,1)} %collective-permute-done.6), channel_id=1, source_target_pairs={{14,0},{0,2},{2,4},{4,6},{6,8},{8,10},{10,12},{12,14},{15,1},{1,3}... | collective-permute-start | bytes 786440 | tf_op jit(solution)/shard_map/ppermute | solution.py:51
  50.7 7.3 %copy-start.12 = (f32[32,8,128]{2,1,0:T(8,128)}, f32[32,8,128]{2,1,0:T(8,128)S(1)}, u32[]{:S(2)}) copy-start(f32[32,8,128]{2,1,0:T(8,128)S(1)} %shard_map.97) | copy-start | bytes 393220
  51.3 11.9 %collective-permute-start.11 = (bf16[768,256]{1,0:T(8,128)(2,1)S(1)}, bf16[768,256]{1,0:T(8,128)(2,1)S(1)}, u32[]{:S(2)}, u32[]{:S(2)}) collective-permute-start(bf16[768,256]{1,0:T(8,128)(2,1)S(1)} %slice.42), channel_id=1, source_target_pairs={{64,0},{128,64},{192,128},{0,192},{65,1},{129,65},{193,129},{1,193... | collective-permute-start | bytes 1179656 | tf_op jit(solution)/shard_map/ppermute | solution.py:51
  54.4 7.1 %copy-start.4 = (bf16[1536,256]{1,0:T(8,128)(2,1)}, bf16[1536,256]{1,0:T(8,128)(2,1)S(1)}, u32[]{:S(2)}) copy-start(bf16[1536,256]{1,0:T(8,128)(2,1)S(1)} %collective-permute-done.12.refs_0_) | copy-start | bytes 2359300
  54.4 9.3 %collective-permute-start.13 = (bf16[768,256]{1,0:T(8,128)(2,1)S(1)}, bf16[768,256]{1,0:T(8,128)(2,1)S(1)}, u32[]{:S(2)}, u32[]{:S(2)}) collective-permute-start(bf16[768,256]{1,0:T(8,128)(2,1)S(1)} %slice.44), channel_id=1, source_target_pairs={{192,0},{0,64},{64,128},{128,192},{193,1},{1,65},{65,129},{129,193... | collective-permute-start | bytes 1179656 | tf_op jit(solution)/shard_map/ppermute | solution.py:51
  56.4 14.5 %copy-start.20 = (bf16[4096]{0:T(1024)(128)(2,1)S(1)}, bf16[4096]{0:T(1024)(128)(2,1)}, u32[]{:S(2)}) copy-start(bf16[4096]{0:T(1024)(128)(2,1)} %param.10) | copy-start | bytes 24580
  58.1 8.8 %collective-permute-start.9 = (bf16[256,256]{1,0:T(8,128)(2,1)S(1)}, bf16[256,256]{1,0:T(8,128)(2,1)S(1)}, u32[]{:S(2)}, u32[]{:S(2)}) collective-permute-start(bf16[256,256]{1,0:T(8,128)(2,1)S(1)} %slice.41), channel_id=1, source_target_pairs={{2,0},{4,2},{6,4},{8,6},{10,8},{12,10},{14,12},{0,14},{3,1},{5,3},... | collective-permute-start | bytes 393224 | tf_op jit(solution)/shard_map/ppermute | solution.py:51
  59.1 8.5 %collective-permute-start.14 = (bf16[256,256]{1,0:T(8,128)(2,1)S(1)}, bf16[256,256]{1,0:T(8,128)(2,1)S(1)}, u32[]{:S(2)}, u32[]{:S(2)}) collective-permute-start(bf16[256,256]{1,0:T(8,128)(2,1)S(1)} %slice.47), channel_id=1, source_target_pairs={{14,0},{0,2},{2,4},{4,6},{6,8},{8,10},{10,12},{12,14},{15,1},{1,3}... | collective-permute-start | bytes 393224 | tf_op jit(solution)/shard_map/ppermute | solution.py:51
  68.2 24.5 %collective-permute-start.17 = (bf16[2560,256]{1,0:T(8,128)(2,1)}, bf16[2560,256]{1,0:T(8,128)(2,1)S(1)}, u32[]{:S(2)}, u32[]{:S(2)}) collective-permute-start(bf16[2560,256]{1,0:T(8,128)(2,1)} %add_dynamic-update-slice_fusion.refs_1_), channel_id=1, source_target_pairs={{192,0},{0,64},{64,128},{128,192},{193,1},{1,65},{65,129},{129,193... | collective-permute-start | bytes 3932168 | tf_op jit(solution)/shard_map/ppermute | solution.py:51
  68.2 25.3 %collective-permute-start.15 = (bf16[2560,256]{1,0:T(8,128)(2,1)}, bf16[2560,256]{1,0:T(8,128)(2,1)S(1)}, u32[]{:S(2)}, u32[]{:S(2)}) collective-permute-start(bf16[2560,256]{1,0:T(8,128)(2,1)} %add_dynamic-update-slice_fusion.refs_1_), channel_id=1, source_target_pairs={{64,0},{128,64},{192,128},{0,192},{65,1},{129,65},{193,129},{1,193... | collective-permute-start | bytes 3932168 | tf_op jit(solution)/shard_map/ppermute | solution.py:51
  83.7 10.8 %copy-start.6 = (bf16[768,256]{1,0:T(8,128)(2,1)}, bf16[768,256]{1,0:T(8,128)(2,1)S(1)}, u32[]{:S(2)}) copy-start(bf16[768,256]{1,0:T(8,128)(2,1)S(1)} %shard_map.98.refs_0_) | copy-start | bytes 1179652
  93.6 16.3 %collective-permute-start.18 = (bf16[1280,256]{1,0:T(8,128)(2,1)}, bf16[1280,256]{1,0:T(8,128)(2,1)}, u32[]{:S(2)}, u32[]{:S(2)}) collective-permute-start(bf16[1280,256]{1,0:T(8,128)(2,1)} %slice_add_fusion), channel_id=1, source_target_pairs={{192,0},{0,64},{64,128},{128,192},{193,1},{1,65},{65,129},{129,193... | collective-permute-start | bytes 1966088 | tf_op jit(solution)/shard_map/ppermute | solution.py:51
  94.5 15.4 %collective-permute-start.16 = (bf16[1280,256]{1,0:T(8,128)(2,1)}, bf16[1280,256]{1,0:T(8,128)(2,1)}, u32[]{:S(2)}, u32[]{:S(2)}) collective-permute-start(bf16[1280,256]{1,0:T(8,128)(2,1)} %slice_add_fusion.1), channel_id=1, source_target_pairs={{64,0},{128,64},{192,128},{0,192},{65,1},{129,65},{193,129},{1,193... | collective-permute-start | bytes 1966088 | tf_op jit(solution)/shard_map/ppermute | solution.py:51
  97.2 15.9 %all-to-all-start.1 = ((f32[32,8,128]{2,1,0:T(8,128)}), f32[32,8,128]{2,1,0:T(8,128)S(1)}, u32[]{:S(2)}, u32[]{:S(2)}) async-start(f32[32,8,128]{2,1,0:T(8,128)} %copy-done.12), calls=%async_computation.1 | async-start | bytes 262144 | tf_op jit(solution)/shard_map/all_to_all | solution.py:55
  129.0 34.2 %copy-start.19 = (bf16[1024,128]{1,0:T(8,128)(2,1)S(1)}, bf16[1024,128]{1,0:T(8,128)(2,1)}, u32[]{:S(2)}) copy-start(bf16[1024,128]{1,0:T(8,128)(2,1)} %w_ref.3) | copy-start | bytes 786436
  164.0 16.3 %collective-permute-start.19 = (f32[40,128]{1,0:T(8,128)S(1)}, f32[40,128]{1,0:T(8,128)S(1)}, u32[]{:S(2)}, u32[]{:S(2)}) collective-permute-start(f32[40,128]{1,0:T(8,128)S(1)} %shard_map.105.own_ref), channel_id=1, source_target_pairs={{0,1},{1,0},{2,3},{3,2},{4,5},{5,4},{6,7},{7,6},{8,9},{9,8},{10,11... | collective-permute-start | bytes 61448 | tf_op jit(solution)/shard_map/ppermute | solution.py:376
  (13 other events, 37.3 us)
Sparse Core Ops, SparseCore 0:
  10.6 104.9 all-gather.1

commit v4 on v3

--- a/solution.py
+++ b/solution.py
@@ -55,32 +55,58 @@
     return lax.all_to_all(a, PSG, split_axis=0, concat_axis=0, tiled=True)
 
 
-def round_x(group, after):
-    half = group.shape[0] // 2
-    up, down = recv(group, "dp", 1), recv(group, "dp", -1)
-    far = [recv(up[:half] + after, "dp", 1), recv(down[half:] + after, "dp", -1)]
-    return [[group], [up], far, [down]]
-
-
-def first_of(*arrays):
-    return sum(a[(0,) * a.ndim].astype(bf16) for a in arrays) * 0
-
-
-def gather(shard, use, early):
-    block = jnp.concatenate(
-        [shard, recv(shard, "y", 1), recv(shard, "y", 2), recv(shard, "y", -1)], axis=0
-    )
+def pack_kernel(cuts, *refs):
+    out_ref, at = refs[-1], 0
+    for ref, (start, rows) in zip(refs, cuts):
+        out_ref[at : at + rows, :] = ref[start : start + rows, :]
+        at += rows
+
+
+def pack(pieces, after=()):
+    cuts = [(start, rows) for _, start, rows in pieces]
+    first = pieces[0][0]
+    return pl.pallas_call(
+        functools.partial(pack_kernel, cuts),
+        out_shape=shaped((sum(rows for _, rows in cuts), first.shape[1]), first.dtype),
+        in_specs=[VMEM] * len(pieces) + [pl.BlockSpec(memory_space=pl.ANY)] * len(after),
+        out_specs=VMEM,
+        compiler_params=params(4),
+        cost_estimate=pl.CostEstimate(flops=0, bytes_accessed=1 << 20, transcendentals=0),
+    )(*[array for array, _, _ in pieces], *after)
+
+
+def join(pieces, after=()):
+    return pack([(piece, 0, piece.shape[0]) for piece in pieces], after)
+
+
+def far_x(up, down, after=()):
+    half = up.shape[0] // 2
+    return [
+        recv(pack([(up, 0, half)], after), "dp", 1),
+        recv(pack([(down, half, half)], after), "dp", -1),
+    ]
+
+
+def gather(shard, use, q_sum, queries):
+    block = join([shard, recv(shard, "y", 1), recv(shard, "y", 2), recv(shard, "y", -1)])
     half = block.shape[0] // 2
     up1, down1 = recv(block, "z", 1), recv(block, "z", -1)
-    near = round_x(jnp.concatenate([block, up1, down1], axis=0), 0)
+    near = join([block, up1, down1], [q_sum])
+    near_up, near_down = recv(near, "dp", 1), recv(near, "dp", -1)
     up2, down2 = recv(up1, "z", 1), recv(down1, "z", -1)
     up3, down3 = recv(up2, "z", 1), recv(down2, "z", -1)
-    last = first_of(*near[2], *early)
-    far = (recv(up3[:half], "z", 1) + last, recv(down3[half:], "z", -1) + last)
-    group = jnp.concatenate([up2, down2, up3, down3, *far], axis=0)
-    own = use(near[0] + [group])
-    rest = round_x(group, first_of(own))
-    return [own] + [use(near[dx] + rest[dx]) for dx in range(1, NX)]
+    near_far = far_x(near_up, near_down)
+    far = [
+        recv(pack([(up3, 0, half)]), "z", 1),
+        recv(pack([(down3, half, half)]), "z", -1),
+    ]
+    rest = join([up2, down2, up3, down3, *far], [queries, *near_far])
+    rest_up, rest_down = recv(rest, "dp", 1), recv(rest, "dp", -1)
+    (own,) = use([[near, rest]])
+    rest_far = far_x(rest_up, rest_down, [own])
+    key_up, key_down = use([[near_up, rest_up], [near_down, rest_down]])
+    (key_far,) = use([near_far + rest_far])
+    return [own, key_up, key_far, key_down]
 
 
 def place(pos, i):
@@ -117,32 +143,31 @@
     )(pos, enc, gain)
 
 
-def project_kernel(x_ref, *refs):
-    pieces, out_ref = refs[:-1], refs[-1]
-    tile = min(out_ref.shape[1], 256)
-    for col in range(0, out_ref.shape[1], tile):
+def project_kernel(counts, x_ref, *refs):
+    at_piece = 0
+    for count, out_ref in zip(counts, refs[sum(counts) :]):
         acc, at = None, 0
-        for ref in pieces:
+        for ref in refs[at_piece : at_piece + count]:
             depth = ref.shape[0]
-            part = jnp.dot(
-                x_ref[:, at : at + depth], ref[:, col : col + tile], preferred_element_type=f32
-            )
+            part = jnp.dot(x_ref[:, at : at + depth], ref[...], preferred_element_type=f32)
             acc = part if acc is None else acc + part
             at += depth
-        out_ref[:, col : col + tile] = acc.astype(bf16)
-
-
-def project(x, pieces):
+        out_ref[...] = acc.astype(bf16)
+        at_piece += count
+
+
+def project(x, lists):
     rows, width = x.shape
-    cols = pieces[0].shape[1]
+    cols = lists[0][0].shape[1]
+    pieces = [piece for pieces in lists for piece in pieces]
     return pl.pallas_call(
-        project_kernel,
-        out_shape=shaped((rows, cols), bf16),
+        functools.partial(project_kernel, [len(pieces) for pieces in lists]),
+        out_shape=[shaped((rows, cols), bf16)] * len(lists),
         in_specs=[VMEM] * (1 + len(pieces)),
-        out_specs=VMEM,
+        out_specs=[VMEM] * len(lists),
         compiler_params=params(8),
         cost_estimate=pl.CostEstimate(
-            flops=2 * rows * width * cols,
+            flops=2 * rows * width * cols * len(lists),
             bytes_accessed=2 * (rows * width + width * cols + rows * cols),
             transcendentals=0,
         ),
@@ -168,11 +193,11 @@
 
 
 def softmax_kernel(plen, pos, q_ref, *refs):
-    keys, (high_ref, low_ref, stat_ref, mass_ref) = refs[:NX], refs[NX:]
+    keys, (high_ref, low_ref, stat_ref) = refs[:NX], refs[NX:]
     answers = q_ref.shape[0]
     lane = lax.broadcasted_iota(jnp.int32, (answers, LANES), 1)
     stats = jnp.zeros((answers, LANES), f32)
-    masses = [stats] * mass_ref.shape[0]
+    heads_all = q_ref.shape[1] * LANES // HDIM
     for dx, key_ref in enumerate(keys):
         quarter = lax.rem(pos[2] + dx, NX)
         slots, cols = key_ref.shape
@@ -204,18 +229,17 @@
             head = quarter * heads + h
             stats = jnp.where(lane == head, top[at, :], stats)
             stats = jnp.where(lane == head + LANES // 2, total[at, :], stats)
-            masses = [jnp.where(lane == head, s[at, :], m) for s, m in zip(sums, masses)]
+            for i, part in enumerate(sums):
+                stats = jnp.where(lane == head + (i + 1) * heads_all, part[at, :], stats)
         whole = jnp.concatenate(p, axis=1)
         high = whole.astype(bf16)
         at = slice(dx * pairs, (dx + 1) * pairs)
         high_ref[at, :] = high
         low_ref[at, :] = (whole - high.astype(f32)).astype(bf16)
     stat_ref[...] = stats
-    for i, mass in enumerate(masses):
-        mass_ref[i] = mass
-
-
-def value_kernel(pos, x_ref, high_ref, low_ref, stat_ref, v_hbm, out_ref, buf, acc, sems):
+
+
+def value_kernel(pos, x_hbm, high_ref, low_ref, stat_ref, v_hbm, out_ref, x_buf, buf, acc, x_sems, sems):
     answers, rows, _ = out_ref.shape
     pairs = high_ref.shape[0] // NX
     cols = buf.shape[1] // NX
@@ -229,15 +253,22 @@
             sems.at[i],
         )
 
-    for i in range(len(ORDER)):
-        fetch(i).start()
+    def fetch_x(part):
+        at = pl.ds(part * half * LANES, half * LANES)
+        return pltpu.make_async_copy(x_hbm.at[:, at], x_buf.at[:, at], x_sems.at[part])
+
     for part in range(2):
+        fetch_x(part).start()
+        for i in range(part * half, (part + 1) * half):
+            fetch(i).start()
+    for part in range(2):
+        fetch_x(part).wait()
         for i in range(part * half, (part + 1) * half):
             fetch(i).wait()
         at = slice(part * half * LANES, (part + 1) * half * LANES)
         for g in range(NX):
             col = slice(g * cols, (g + 1) * cols)
-            v = jnp.dot(x_ref[:, at], buf[at, col], preferred_element_type=f32)
+            v = jnp.dot(x_buf[:, at], buf[at, col], preferred_element_type=f32)
             acc[:, col] = v if part == 0 else acc[:, col] + v
     for dx in range(NX):
         quarter = lax.rem(pos[2] + dx, NX)
@@ -260,38 +291,44 @@
     return jnp.where(lane < HDIM, row[:, 2 * j : 2 * j + 1], row[:, 2 * j + 1 : 2 * j + 2])
 
 
-def merge_kernel(pos, got_ref, out_ref):
+def merge_kernel(passages, pos, got_ref, out_ref, rows):
     last = got_ref.shape[1] - 1
+    heads = last * LANES // HDIM
     stats = got_ref[:, last, :]
     top = jnp.max(stats, axis=0, keepdims=True)
     scale = jnp.exp(stats - top)
     total = jnp.sum(pltpu.roll(stats, LANES // 2, 1) * scale, axis=0, keepdims=True)
     lane = lax.broadcasted_iota(jnp.int32, scale.shape, 1)
     first = lane[0:1, :]
+    rows[...] = jnp.zeros_like(rows)
     for j in range(last):
         numer = jnp.sum(got_ref[:, j, :] * by_head(lane, scale, j), axis=0, keepdims=True)
         row = numer / by_head(first, total, j)
-        out_ref[:, j, :] = jnp.broadcast_to(row, scale.shape)
-    row = jnp.where(first < LANES // 2, top, pltpu.roll(total, LANES // 2, 1))
-    out_ref[:, last, :] = jnp.broadcast_to(row, scale.shape)
-
-
-def out_kernel(pos, ctx_ref, stat_ref, mass_ref, w_ref, out_ref):
-    answers, rows, _ = ctx_ref.shape
-    last = rows - 1
-    ctx = jnp.concatenate([ctx_ref[:, j, :] for j in range(last)], axis=1).astype(bf16)
+        rows[:, j, :] = jnp.broadcast_to(row, scale.shape)
+    factor = jnp.where(lane < heads, scale / jnp.where(first < heads, total, 1.0), 0.0)
+    parts = jnp.zeros_like(scale)
+    for i in range(passages):
+        own = pltpu.roll(stats, LANES - (i + 1) * heads, 1) * factor
+        rest = jnp.sum(own, axis=1, keepdims=True)
+        for term in range(3):
+            piece = rest.astype(bf16).astype(f32)
+            parts = jnp.where(lane == term * 8 + i, piece, parts)
+            rest = rest - piece
+    rows[:, last, :] = parts
+    out_ref[...] = rows[...].astype(bf16)
+
+
+def out_kernel(pos, ctx_ref, w_ref, out_ref, rows):
+    answers = ctx_ref.shape[0]
+    last = w_ref.shape[0] // LANES
+    rows[...] = ctx_ref[...].astype(f32)
+    ctx = jnp.concatenate([rows[:, j, :] for j in range(last)], axis=1).astype(bf16)
     out_ref[0:answers, :] = jnp.dot(ctx, w_ref[...], preferred_element_type=f32)
-    merged = ctx_ref[:, last, :]
-    lane = lax.broadcasted_iota(jnp.int32, merged.shape, 1)
-    heads = last * LANES // HDIM
-    total = jnp.where(lane < heads, pltpu.roll(merged, LANES // 2, 1), 1.0)
-    gap = jnp.where(lane < heads, stat_ref[...] - merged, 0.0)
-    factor = jnp.exp(gap) / total
-    first = lax.broadcasted_iota(jnp.int32, (8, LANES), 1)
-    scores = jnp.zeros((8, LANES), f32)
-    for i in range(mass_ref.shape[0]):
-        scores = jnp.where(first == i, jnp.sum(mass_ref[i] * factor, keepdims=True), scores)
-    out_ref[answers : answers + 8, :] = scores
+    parts = rows[:, last, :]
+    scores = parts + pltpu.roll(parts, LANES - 8, 1) + pltpu.roll(parts, LANES - 16, 1)
+    out_ref[answers : answers + 8, :] = jnp.broadcast_to(
+        jnp.sum(scores, axis=0, keepdims=True), (8, LANES)
+    )
 
 
 def last_kernel(scale, pos, own_ref, other_ref, out_ref, scores_ref):
@@ -329,14 +366,13 @@
     queries = exchange(q_sum)
 
     mine = lax.dynamic_slice(w_key, (0, x * quarter), (w_key.shape[0], quarter))
-    keys = gather(mine, functools.partial(project, normed), [q_sum])
-    high, low, stat, mass = call(
+    keys = gather(mine, functools.partial(project, normed), q_sum, queries)
+    high, low, stat = call(
         functools.partial(softmax_kernel, plen),
         [
             shaped((pairs, slots), bf16),
             shaped((pairs, slots), bf16),
             shaped((answers, LANES)),
-            shaped((pdev, answers, LANES)),
         ],
         [],
         pos,
@@ -348,8 +384,10 @@
         value_kernel,
         shaped((answers, blocks + 1, LANES)),
         [
+            pltpu.VMEM((slots, width), bf16),
             pltpu.VMEM((width, columns), bf16),
             pltpu.VMEM((slots, columns), f32),
+            pltpu.SemaphoreType.DMA((2,)),
             pltpu.SemaphoreType.DMA((len(ORDER),)),
         ],
         pos,
@@ -358,19 +396,24 @@
         low,
         stat,
         w_values,
-        mib=46,
+        mib=52,
         flops=2 * slots * width * columns,
-        hbm=(5,),
-    )
-    merged = call(merge_kernel, shaped(parts.shape), [], pos, exchange(parts))
+        hbm=(1, 5),
+    )
+    rows = 2 * blocks
+    merged = call(
+        functools.partial(merge_kernel, pdev),
+        shaped((members, rows, LANES), bf16),
+        [pltpu.VMEM((members, rows, LANES), f32)],
+        pos,
+        exchange(parts),
+    )
     part = call(
         out_kernel,
         shaped((answers + 8, w_out.shape[1])),
-        [],
+        [pltpu.VMEM((answers, rows, LANES), f32)],
         pos,
         exchange(merged),
-        stat,
-        mass,
         w_out,
     )
     other = lax.ppermute(part, "tp", [(0, 1), (1, 0)])

time: 189 us -> 190 us (level)
  blocking collectives: 33.3 us -> 47.8 us
  local copies, waits for them, and re-layouts: 20.3 us -> 5.86 us
  waiting for transfers between devices: 27.8 us -> 41.4 us
  starting transfers between devices: 52.9 us -> 43.7 us
  between operations: 17 us -> 14.2 us
  Pallas kernels: 33.7 us -> 36.3 us
  other arithmetic: 3.24 us -> 0.73 us
    ppermute x19, waiting for transfers between devices: 18.4 us -> 33.9 us  [recv(): return lax.ppermute(a, axis, [((i + k) % n, i) for i in range(n)])]
    all_to_all x2 -> x3, blocking collectives: 33.3 us -> 47.8 us  [exchange(): return lax.all_to_all(a, PSG, split_axis=0, concat_axis=0, tiled=True)]
    unnamed x53 -> x18, local copies, waits for them, and re-layouts: 17.1 us -> 5.84 us
    all_to_all x2 -> x1, starting transfers between devices: 10.2 us -> 3.98 us  [exchange(): return lax.all_to_all(a, PSG, split_axis=0, concat_axis=0, tiled=True)]
    ppermute x1, starting transfers between devices: 15.5 us -> 9.3 us  [body(): other = lax.ppermute(part, 'tp', [(0, 1), (1, 0)])]
    ppermute x19, starting transfers between devices: 27.2 us -> 30.4 us  [recv(): return lax.ppermute(a, axis, [((i + k) % n, i) for i in range(n)])]
    slice x8 -> x0, local copies, waits for them, and re-layouts: 3.12 us -> none  [the longest x4 2.14 us: first_of(): return sum((a[(0,) * a.ndim].astype(bf16) for a in arrays)) * 0]
    pallas_call x7, Pallas kernels: 17 us -> 19.3 us  [call(): pl.pallas_call(kernel, out_shape=outs, in_specs=specs, out_specs=jax.tree...]
  transfers between devices with their start and end apart: 23 -> 22, of which waited for: 9 -> 10; matrix products, arithmetic and copies ran while one was open for 7% -> 0% of each run, Pallas kernels for 11% -> 11%
where the time goes in v4:
time: 190 us
  blocking collectives  47.8 us (25%)
  starting transfers between devices  43.7 us (23%)
  waiting for transfers between devices  41.4 us (22%)
  Pallas kernels  36.3 us (19%)
  between operations  14.2 us (7%)
  local copies, waits for them, and re-layouts  5.86 us (3%)
    all_to_all x3, blocking collectives, exchange(): return lax.all_to_all(a, PSG, split_axis=0, concat_axis=0, tiled=True)  47.8 us
    ppermute x19, waiting for transfers between devices, recv(): return lax.ppermute(a, axis, [((i + k) % n, i) for i in range(n)])  33.9 us
    ppermute x19, starting transfers between devices, recv(): return lax.ppermute(a, axis, [((i + k) % n, i) for i in range(n)])  30.4 us
    pallas_call x7, Pallas kernels, call(): pl.pallas_call(kernel, out_shape=outs, in_specs=specs, out_specs=jax.tree...  19.3 us
    ppermute x1, starting transfers between devices, body(): other = lax.ppermute(part, 'tp', [(0, 1), (1, 0)])  9.3 us
    pallas_call x3, Pallas kernels, project(): pl.pallas_call(functools.partial(project_kernel, [len(pieces) for pieces...  6.97 us
    all_to_all x1, waiting for transfers between devices, exchange(): return lax.all_to_all(a, PSG, split_axis=0, concat_axis=0, tiled=True)  5.94 us
    pallas_call x1, Pallas kernels, normalise(): pl.pallas_call(norm_kernel, out_shape=shaped((rows, width), bf16), grid_s...  5.87 us
  transfers between devices with their start and end apart: 22, of which 10 were waited for; matrix products, arithmetic and copies ran while one was open for 0% of the time, Pallas kernels for 11%

profile of v4, /device:TPU:1, one launch (start us, length us, event | category | flops | bytes accessed | tf_op | source)
XLA Modules:
  0.0 190.1 jit_solution(10090995419871616232)
XLA Ops:
  8.1 3.6 %collective-permute-start = (bf16[128,256]{1,0:T(8,128)(2,1)S(1)}, bf16[128,256]{1,0:T(8,128)(2,1)S(1)}, u32[]{:S(2)}, u32[]{:S(2)}) collective-permute-start(bf16[128,256]{1,0:T(8,128)(2,1)S(1)} %constant_dynamic-slice_fusion.refs_0_), channel_id=1, source_target_pairs={{16,0},{32,16},{48,32},{0,48},{17,1},{33,17},{49,33},{1,49},{18,2}... | collective-permute-start | bytes 196616 | tf_op jit(solution)/shard_map/ppermute | solution.py:51
  13.1 3.4 %collective-permute-done.1.refs_2_ = bf16[128,256]{1,0:T(8,128)(2,1)S(1)} collective-permute-done((bf16[128,256]{1,0:T(8,128)(2,1)S(1)}, bf16[128,256]{1,0:T(8,128)(2,1)S(1)}, u32[]{:S(2)}, u32[]{:S(2)}) %collective-permute-start.1) | collective-permute-done | bytes 65568 | tf_op jit(solution)/shard_map/ppermute | solution.py:51
  17.1 5.7 %collective-permute-start.3 = (bf16[512,256]{1,0:T(8,128)(2,1)S(1)}, bf16[512,256]{1,0:T(8,128)(2,1)S(1)}, u32[]{:S(2)}, u32[]{:S(2)}) collective-permute-start(bf16[512,256]{1,0:T(8,128)(2,1)S(1)} %shard_map.98.refs_0_), channel_id=1, source_target_pairs={{2,0},{4,2},{6,4},{8,6},{10,8},{12,10},{14,12},{0,14},{3,1},{5,3},... | collective-permute-start | bytes 786440 | tf_op jit(solution)/shard_map/ppermute | solution.py:51
  26.2 15.2 %all_to_all.20.got_ref = f32[32,8,128]{2,1,0:T(8,128)S(1)} all-to-all(f32[32,8,128]{2,1,0:T(8,128)S(1)} %shard_map.96), channel_id=1, replica_groups=mesh['dp'=4,'y'=4,'z'=8,'tp'=2] {'y','z'}, dimensions={0} | all-to-all | bytes 262144 | tf_op jit(solution)/shard_map/all_to_all | solution.py:55
  41.3 1.2 shard_map.97.refs_3_
  42.6 2.8 %collective-permute-start.11 = (bf16[1536,256]{1,0:T(8,128)(2,1)S(1)}, bf16[1536,256]{1,0:T(8,128)(2,1)S(1)}, u32[]{:S(2)}, u32[]{:S(2)}) collective-permute-start(bf16[1536,256]{1,0:T(8,128)(2,1)S(1)} %shard_map.99.refs_0_), channel_id=1, source_target_pairs={{64,0},{128,64},{192,128},{0,192},{65,1},{129,65},{193,129},{1,193... | collective-permute-start | bytes 2359304 | tf_op jit(solution)/shard_map/ppermute | solution.py:51
  46.1 2.0 %collective-permute-start.5 = (bf16[512,256]{1,0:T(8,128)(2,1)S(1)}, bf16[512,256]{1,0:T(8,128)(2,1)}, u32[]{:S(2)}, u32[]{:S(2)}) collective-permute-start(bf16[512,256]{1,0:T(8,128)(2,1)S(1)} %collective-permute-done.3.refs_1_), channel_id=1, source_target_pairs={{2,0},{4,2},{6,4},{8,6},{10,8},{12,10},{14,12},{0,14},{3,1},{5,3},... | collective-permute-start | bytes 786440 | tf_op jit(solution)/shard_map/ppermute | solution.py:51
  48.1 6.5 %collective-permute-done.6.refs_1_ = bf16[512,256]{1,0:T(8,128)(2,1)S(1)} collective-permute-done((bf16[512,256]{1,0:T(8,128)(2,1)S(1)}, bf16[512,256]{1,0:T(8,128)(2,1)S(1)}, u32[]{:S(2)}, u32[]{:S(2)}) %collective-permute-start.6) | collective-permute-done | bytes 262176 | tf_op jit(solution)/shard_map/ppermute | solution.py:51
  54.6 2.7 %collective-permute-start.7 = (bf16[512,256]{1,0:T(8,128)(2,1)}, bf16[512,256]{1,0:T(8,128)(2,1)S(1)}, u32[]{:S(2)}, u32[]{:S(2)}) collective-permute-start(bf16[512,256]{1,0:T(8,128)(2,1)} %collective-permute-done.5.refs_0_), channel_id=1, source_target_pairs={{2,0},{4,2},{6,4},{8,6},{10,8},{12,10},{14,12},{0,14},{3,1},{5,3},... | collective-permute-start | bytes 786440 | tf_op jit(solution)/shard_map/ppermute | solution.py:51
  57.3 2.0 %collective-permute-done.11.refs_0_ = bf16[1536,256]{1,0:T(8,128)(2,1)S(1)} collective-permute-done((bf16[1536,256]{1,0:T(8,128)(2,1)S(1)}, bf16[1536,256]{1,0:T(8,128)(2,1)S(1)}, u32[]{:S(2)}, u32[]{:S(2)}) %collective-permute-start.11) | collective-permute-done | bytes 786464 | tf_op jit(solution)/shard_map/ppermute | solution.py:51
  60.0 3.4 %collective-permute-start.12 = (bf16[768,256]{1,0:T(8,128)(2,1)}, bf16[768,256]{1,0:T(8,128)(2,1)S(1)}, u32[]{:S(2)}, u32[]{:S(2)}) collective-permute-start(bf16[768,256]{1,0:T(8,128)(2,1)} %shard_map.102), channel_id=1, source_target_pairs={{64,0},{128,64},{192,128},{0,192},{65,1},{129,65},{193,129},{1,193... | collective-permute-start | bytes 1179656 | tf_op jit(solution)/shard_map/ppermute | solution.py:51
  65.1 4.0 %all-to-all-start.1 = ((f32[32,8,128]{2,1,0:T(8,128)}), f32[32,8,128]{2,1,0:T(8,128)S(1)}, u32[]{:S(2)}, u32[]{:S(2)}) async-start(f32[32,8,128]{2,1,0:T(8,128)} %shard_map.97.refs_3_), calls=%async_computation.1 | async-start | bytes 262144 | tf_op jit(solution)/shard_map/all_to_all | solution.py:55
  69.8 1.2 collective-permute-start.10
  71.7 1.4 collective-permute-start.9
  73.1 5.9 %all-to-all-done.1.refs_6_.q_ref = f32[32,8,128]{2,1,0:T(8,128)S(1)} async-done(((f32[32,8,128]{2,1,0:T(8,128)}), f32[32,8,128]{2,1,0:T(8,128)S(1)}, u32[]{:S(2)}, u32[]{:S(2)}) %all-to-all-start.1) | async-done | bytes 131104 | tf_op jit(solution)/shard_map/all_to_all | solution.py:55
  79.1 1.4 collective-permute-done.10.refs_5_
  80.5 1.1 shard_map.104.refs_1_
  81.7 2.7 %collective-permute-start.15 = (bf16[2560,256]{1,0:T(8,128)(2,1)S(1)}, bf16[2560,256]{1,0:T(8,128)(2,1)S(1)}, u32[]{:S(2)}, u32[]{:S(2)}) collective-permute-start(bf16[2560,256]{1,0:T(8,128)(2,1)S(1)} %shard_map.104.refs_1_), channel_id=1, source_target_pairs={{64,0},{128,64},{192,128},{0,192},{65,1},{129,65},{193,129},{1,193... | collective-permute-start | bytes 3932168 | tf_op jit(solution)/shard_map/ppermute | solution.py:51
  84.4 2.8 %copy-done.2 = bf16[1,3,256,4096]{3,2,1,0:T(8,128)(2,1)S(1)} copy-done((bf16[1,3,256,4096]{3,2,1,0:T(8,128)(2,1)S(1)}, bf16[1,3,256,4096]{3,2,1,0:T(8,128)(2,1)}, u32[]{:S(2)}) %copy-start.2) | copy-done | bytes 6291480
  87.2 5.9 %shard_map.95.x_ref.x_hbm = bf16[768,4096]{1,0:T(8,128)(2,1)S(1)} custom-call(s32[6]{0:T(128)S(1)} %pad_add_fusion.pos, bf16[768,4096]{1,0:T(8,128)(2,1)S(1)} %bitcast.7, bf16[1,4096]{1,0:T(2,128)(2,1)S(1)} %broadcast_in_dim.6.gain_ref), custom_call_target="tpu_custom_call" | custom-call | flops 18874368 | bytes 12582912 | tf_op jit(solution)/shard_map/pallas_call | solution.py:129
  93.1 1.8 shard_map.105.refs_1_.refs_0_
  94.9 13.1 %collective-permute-done.16.refs_3_.refs_0_ = bf16[2560,256]{1,0:T(8,128)(2,1)S(1)} collective-permute-done((bf16[2560,256]{1,0:T(8,128)(2,1)S(1)}, bf16[2560,256]{1,0:T(8,128)(2,1)S(1)}, u32[]{:S(2)}, u32[]{:S(2)}) %collective-permute-start.16) | collective-permute-done | bytes 1310752 | tf_op jit(solution)/shard_map/ppermute | solution.py:51
  108.2 2.9 %collective-permute-start.17 = (bf16[1280,256]{1,0:T(8,128)(2,1)S(1)}, bf16[1280,256]{1,0:T(8,128)(2,1)S(1)}, u32[]{:S(2)}, u32[]{:S(2)}) collective-permute-start(bf16[1280,256]{1,0:T(8,128)(2,1)S(1)} %shard_map.107), channel_id=1, source_target_pairs={{64,0},{128,64},{192,128},{0,192},{65,1},{129,65},{193,129},{1,193... | collective-permute-start | bytes 1966088 | tf_op jit(solution)/shard_map/ppermute | solution.py:51
  111.2 3.4 %shard_map.106 = (bf16[768,256]{1,0:T(8,128)(2,1)S(1)}, bf16[768,256]{1,0:T(8,128)(2,1)S(1)}) custom-call(bf16[768,4096]{1,0:T(8,128)(2,1)S(1)} %shard_map.95.x_ref.x_hbm, bf16[1536,256]{1,0:T(8,128)(2,1)S(1)} %collective-permute-done.11.refs_0_, bf16[2560,256]{1,0:T(8,128)(2,1)S(1)} %collective-permute-done.15.refs_1_.refs_0_, ...), custom_call_target="tpu_custom_call" | custom-call | flops 3221225472 | bytes 8781824 | tf_op jit(solution)/shard_map/pallas_call | solution.py:163
  114.6 6.6 %collective-permute-done.18.refs_3_ = bf16[1280,256]{1,0:T(8,128)(2,1)S(1)} collective-permute-done((bf16[1280,256]{1,0:T(8,128)(2,1)S(1)}, bf16[1280,256]{1,0:T(8,128)(2,1)S(1)}, u32[]{:S(2)}, u32[]{:S(2)}) %collective-permute-start.18) | collective-permute-done | bytes 655392 | tf_op jit(solution)/shard_map/ppermute | solution.py:51
  121.2 1.8 shard_map.109.refs_2_
  123.0 1.7 shard_map.110
  124.7 12.9 %shard_map.111 = f32[32,9,128]{2,1,0:T(8,128)S(1)} custom-call(s32[6]{0:T(128)S(1)} %pad_add_fusion.pos, bf16[768,4096]{1,0:T(8,128)(2,1)} %copy-done.1, bf16[512,768]{1,0:T(8,128)(2,1)S(1)} %get-tuple-element.11.high_ref, bf16[512,768]{1,0:T(8,128)(2,1)S(1)} %get-tuple-element.12.low_ref, f32[32,128]{1,0:T(8,128)S(1)} %get-tuple-element.13.stat_ref, ...), custom_call_target="tpu_custom_call" | custom-call | flops 6442450944 | bytes 1048576 | tf_op jit(solution)/shard_map/pallas_call | solution.py:38
  137.6 19.3 %all_to_all.21.got_ref = f32[32,9,128]{2,1,0:T(8,128)S(1)} all-to-all(f32[32,9,128]{2,1,0:T(8,128)S(1)} %shard_map.111), channel_id=1, replica_groups=mesh['dp'=4,'y'=4,'z'=8,'tp'=2] {'y','z'}, dimensions={0} | all-to-all | bytes 294912 | tf_op jit(solution)/shard_map/all_to_all | solution.py:55
  157.8 13.3 %all_to_all.22.ctx_ref = bf16[32,16,128]{2,1,0:T(8,128)(2,1)S(1)} all-to-all(bf16[32,16,128]{2,1,0:T(8,128)(2,1)S(1)} %shard_map.112), channel_id=1, replica_groups=mesh['dp'=4,'y'=4,'z'=8,'tp'=2] {'y','z'}, dimensions={0} | all-to-all | bytes 262144 | tf_op jit(solution)/shard_map/all_to_all | solution.py:55
  171.9 9.3 %collective-permute-start.19 = (f32[40,128]{1,0:T(8,128)S(1)}, f32[40,128]{1,0:T(8,128)S(1)}, u32[]{:S(2)}, u32[]{:S(2)}) collective-permute-start(f32[40,128]{1,0:T(8,128)S(1)} %shard_map.113.own_ref), channel_id=1, source_target_pairs={{0,1},{1,0},{2,3},{3,2},{4,5},{5,4},{6,7},{7,6},{8,9},{9,8},{10,11... | collective-permute-start | bytes 61448 | tf_op jit(solution)/shard_map/ppermute | solution.py:419
  182.1 1.1 shard_map.114
  (57 shorter events, 13.7 us)
Async XLA Ops:
  7.2 1.0 copy-start
  7.2 77.2 %copy-start.8 = (bf16[4096]{0:T(1024)(128)(2,1)S(1)}, bf16[4096]{0:T(1024)(128)(2,1)}, u32[]{:S(2)}) copy-start(bf16[4096]{0:T(1024)(128)(2,1)} %param.10) | copy-start | bytes 24580
  7.2 117.5 %all-gather.2.cloned.1.call-start = ((), (), s32[]{:S(2)}) async-start(), calls=%async_computation.4 | async-start | bytes 8650752 | tf_op jit(solution)/shard_map/all_gather | solution.py:353
  8.1 5.0 %collective-permute-start = (bf16[128,256]{1,0:T(8,128)(2,1)S(1)}, bf16[128,256]{1,0:T(8,128)(2,1)S(1)}, u32[]{:S(2)}, u32[]{:S(2)}) collective-permute-start(bf16[128,256]{1,0:T(8,128)(2,1)S(1)} %constant_dynamic-slice_fusion.refs_0_), channel_id=1, source_target_pairs={{16,0},{32,16},{48,32},{0,48},{17,1},{33,17},{49,33},{1,49},{18,2}... | collective-permute-start | bytes 196616 | tf_op jit(solution)/shard_map/ppermute | solution.py:51
  11.8 4.7 %collective-permute-start.1 = (bf16[128,256]{1,0:T(8,128)(2,1)S(1)}, bf16[128,256]{1,0:T(8,128)(2,1)S(1)}, u32[]{:S(2)}, u32[]{:S(2)}) collective-permute-start(bf16[128,256]{1,0:T(8,128)(2,1)S(1)} %constant_dynamic-slice_fusion.refs_0_), channel_id=1, source_target_pairs={{32,0},{48,16},{0,32},{16,48},{33,1},{49,17},{1,33},{17,49},{34,2}... | collective-permute-start | bytes 196616 | tf_op jit(solution)/shard_map/ppermute | solution.py:51
  12.1 5.0 %collective-permute-start.2 = (bf16[128,256]{1,0:T(8,128)(2,1)S(1)}, bf16[128,256]{1,0:T(8,128)(2,1)S(1)}, u32[]{:S(2)}, u32[]{:S(2)}) collective-permute-start(bf16[128,256]{1,0:T(8,128)(2,1)S(1)} %constant_dynamic-slice_fusion.refs_0_), channel_id=1, source_target_pairs={{48,0},{0,16},{16,32},{32,48},{49,1},{1,17},{17,33},{33,49},{50,2}... | collective-permute-start | bytes 196616 | tf_op jit(solution)/shard_map/ppermute | solution.py:51
  17.1 25.5 %collective-permute-start.3 = (bf16[512,256]{1,0:T(8,128)(2,1)S(1)}, bf16[512,256]{1,0:T(8,128)(2,1)S(1)}, u32[]{:S(2)}, u32[]{:S(2)}) collective-permute-start(bf16[512,256]{1,0:T(8,128)(2,1)S(1)} %shard_map.98.refs_0_), channel_id=1, source_target_pairs={{2,0},{4,2},{6,4},{8,6},{10,8},{12,10},{14,12},{0,14},{3,1},{5,3},... | collective-permute-start | bytes 786440 | tf_op jit(solution)/shard_map/ppermute | solution.py:51
  22.8 19.8 %collective-permute-start.4 = (bf16[512,256]{1,0:T(8,128)(2,1)S(1)}, bf16[512,256]{1,0:T(8,128)(2,1)S(1)}, u32[]{:S(2)}, u32[]{:S(2)}) collective-permute-start(bf16[512,256]{1,0:T(8,128)(2,1)S(1)} %shard_map.98.refs_0_), channel_id=1, source_target_pairs={{14,0},{0,2},{2,4},{4,6},{6,8},{8,10},{10,12},{12,14},{15,1},{1,3}... | collective-permute-start | bytes 786440 | tf_op jit(solution)/shard_map/ppermute | solution.py:51
  23.5 1.0 copy-start.6
  24.5 0.9 copy-start.7
  42.6 16.6 %collective-permute-start.11 = (bf16[1536,256]{1,0:T(8,128)(2,1)S(1)}, bf16[1536,256]{1,0:T(8,128)(2,1)S(1)}, u32[]{:S(2)}, u32[]{:S(2)}) collective-permute-start(bf16[1536,256]{1,0:T(8,128)(2,1)S(1)} %shard_map.99.refs_0_), channel_id=1, source_target_pairs={{64,0},{128,64},{192,128},{0,192},{65,1},{129,65},{193,129},{1,193... | collective-permute-start | bytes 2359304 | tf_op jit(solution)/shard_map/ppermute | solution.py:51
  45.4 18.0 %collective-permute-start.13 = (bf16[1536,256]{1,0:T(8,128)(2,1)S(1)}, bf16[1536,256]{1,0:T(8,128)(2,1)S(1)}, u32[]{:S(2)}, u32[]{:S(2)}) collective-permute-start(bf16[1536,256]{1,0:T(8,128)(2,1)S(1)} %shard_map.99.refs_0_), channel_id=1, source_target_pairs={{192,0},{0,64},{64,128},{128,192},{193,1},{1,65},{65,129},{129,193... | collective-permute-start | bytes 2359304 | tf_op jit(solution)/shard_map/ppermute | solution.py:51
  45.4 9.1 %collective-permute-start.6 = (bf16[512,256]{1,0:T(8,128)(2,1)S(1)}, bf16[512,256]{1,0:T(8,128)(2,1)S(1)}, u32[]{:S(2)}, u32[]{:S(2)}) collective-permute-start(bf16[512,256]{1,0:T(8,128)(2,1)S(1)} %collective-permute-done.4.refs_2_), channel_id=1, source_target_pairs={{14,0},{0,2},{2,4},{4,6},{6,8},{8,10},{10,12},{12,14},{15,1},{1,3}... | collective-permute-start | bytes 786440 | tf_op jit(solution)/shard_map/ppermute | solution.py:51
  46.1 8.4 %collective-permute-start.5 = (bf16[512,256]{1,0:T(8,128)(2,1)S(1)}, bf16[512,256]{1,0:T(8,128)(2,1)}, u32[]{:S(2)}, u32[]{:S(2)}) collective-permute-start(bf16[512,256]{1,0:T(8,128)(2,1)S(1)} %collective-permute-done.3.refs_1_), channel_id=1, source_target_pairs={{2,0},{4,2},{6,4},{8,6},{10,8},{12,10},{14,12},{0,14},{3,1},{5,3},... | collective-permute-start | bytes 786440 | tf_op jit(solution)/shard_map/ppermute | solution.py:51
  54.6 14.6 %collective-permute-start.8 = (bf16[512,256]{1,0:T(8,128)(2,1)S(1)}, bf16[512,256]{1,0:T(8,128)(2,1)S(1)}, u32[]{:S(2)}, u32[]{:S(2)}) collective-permute-start(bf16[512,256]{1,0:T(8,128)(2,1)S(1)} %collective-permute-done.6.refs_1_), channel_id=1, source_target_pairs={{14,0},{0,2},{2,4},{4,6},{6,8},{8,10},{10,12},{12,14},{15,1},{1,3}... | collective-permute-start | bytes 786440 | tf_op jit(solution)/shard_map/ppermute | solution.py:51
  54.6 16.5 %collective-permute-start.7 = (bf16[512,256]{1,0:T(8,128)(2,1)}, bf16[512,256]{1,0:T(8,128)(2,1)S(1)}, u32[]{:S(2)}, u32[]{:S(2)}) collective-permute-start(bf16[512,256]{1,0:T(8,128)(2,1)} %collective-permute-done.5.refs_0_), channel_id=1, source_target_pairs={{2,0},{4,2},{6,4},{8,6},{10,8},{12,10},{14,12},{0,14},{3,1},{5,3},... | collective-permute-start | bytes 786440 | tf_op jit(solution)/shard_map/ppermute | solution.py:51
  60.0 20.4 %collective-permute-start.12 = (bf16[768,256]{1,0:T(8,128)(2,1)}, bf16[768,256]{1,0:T(8,128)(2,1)S(1)}, u32[]{:S(2)}, u32[]{:S(2)}) collective-permute-start(bf16[768,256]{1,0:T(8,128)(2,1)} %shard_map.102), channel_id=1, source_target_pairs={{64,0},{128,64},{192,128},{0,192},{65,1},{129,65},{193,129},{1,193... | collective-permute-start | bytes 1179656 | tf_op jit(solution)/shard_map/ppermute | solution.py:51
  64.2 0.9 copy-start.3
  65.1 15.3 %collective-permute-start.14 = (bf16[768,256]{1,0:T(8,128)(2,1)}, bf16[768,256]{1,0:T(8,128)(2,1)S(1)}, u32[]{:S(2)}, u32[]{:S(2)}) collective-permute-start(bf16[768,256]{1,0:T(8,128)(2,1)} %shard_map.103), channel_id=1, source_target_pairs={{192,0},{0,64},{64,128},{128,192},{193,1},{1,65},{65,129},{129,193... | collective-permute-start | bytes 1179656 | tf_op jit(solution)/shard_map/ppermute | solution.py:51
  65.1 13.9 %all-to-all-start.1 = ((f32[32,8,128]{2,1,0:T(8,128)}), f32[32,8,128]{2,1,0:T(8,128)S(1)}, u32[]{:S(2)}, u32[]{:S(2)}) async-start(f32[32,8,128]{2,1,0:T(8,128)} %shard_map.97.refs_3_), calls=%async_computation.1 | async-start | bytes 262144 | tf_op jit(solution)/shard_map/all_to_all | solution.py:55
  69.8 10.7 %collective-permute-start.10 = (bf16[256,256]{1,0:T(8,128)(2,1)}, bf16[256,256]{1,0:T(8,128)(2,1)}, u32[]{:S(2)}, u32[]{:S(2)}) collective-permute-start(bf16[256,256]{1,0:T(8,128)(2,1)} %shard_map.101), channel_id=1, source_target_pairs={{14,0},{0,2},{2,4},{4,6},{6,8},{8,10},{10,12},{12,14},{15,1},{1,3}... | collective-permute-start | bytes 393224 | tf_op jit(solution)/shard_map/ppermute | solution.py:51
  71.7 8.8 %collective-permute-start.9 = (bf16[256,256]{1,0:T(8,128)(2,1)}, bf16[256,256]{1,0:T(8,128)(2,1)}, u32[]{:S(2)}, u32[]{:S(2)}) collective-permute-start(bf16[256,256]{1,0:T(8,128)(2,1)} %shard_map.100), channel_id=1, source_target_pairs={{2,0},{4,2},{6,4},{8,6},{10,8},{12,10},{14,12},{0,14},{3,1},{5,3},... | collective-permute-start | bytes 393224 | tf_op jit(solution)/shard_map/ppermute | solution.py:51
  81.6 26.4 %collective-permute-start.16 = (bf16[2560,256]{1,0:T(8,128)(2,1)S(1)}, bf16[2560,256]{1,0:T(8,128)(2,1)S(1)}, u32[]{:S(2)}, u32[]{:S(2)}) collective-permute-start(bf16[2560,256]{1,0:T(8,128)(2,1)S(1)} %shard_map.104.refs_1_), channel_id=1, source_target_pairs={{192,0},{0,64},{64,128},{128,192},{193,1},{1,65},{65,129},{129,193... | collective-permute-start | bytes 3932168 | tf_op jit(solution)/shard_map/ppermute | solution.py:51
  81.7 26.5 %collective-permute-start.15 = (bf16[2560,256]{1,0:T(8,128)(2,1)S(1)}, bf16[2560,256]{1,0:T(8,128)(2,1)S(1)}, u32[]{:S(2)}, u32[]{:S(2)}) collective-permute-start(bf16[2560,256]{1,0:T(8,128)(2,1)S(1)} %shard_map.104.refs_1_), channel_id=1, source_target_pairs={{64,0},{128,64},{192,128},{0,192},{65,1},{129,65},{193,129},{1,193... | collective-permute-start | bytes 3932168 | tf_op jit(solution)/shard_map/ppermute | solution.py:51
  84.4 2.8 %copy-start.2 = (bf16[1,3,256,4096]{3,2,1,0:T(8,128)(2,1)S(1)}, bf16[1,3,256,4096]{3,2,1,0:T(8,128)(2,1)}, u32[]{:S(2)}) copy-start(bf16[1,3,256,4096]{3,2,1,0:T(8,128)(2,1)} %param.8) | copy-start | bytes 18874372
  93.1 28.1 %copy-start.1 = (bf16[768,4096]{1,0:T(8,128)(2,1)}, bf16[768,4096]{1,0:T(8,128)(2,1)S(1)}, u32[]{:S(2)}) copy-start(bf16[768,4096]{1,0:T(8,128)(2,1)S(1)} %shard_map.95.x_ref.x_hbm) | copy-start | bytes 18874372
  93.1 18.1 %copy-start.4 = (bf16[1536,256]{1,0:T(8,128)(2,1)S(1)}, bf16[1536,256]{1,0:T(8,128)(2,1)}, u32[]{:S(2)}) copy-start(bf16[1536,256]{1,0:T(8,128)(2,1)} %copy-done.3) | copy-start | bytes 2359300
  108.1 13.1 %collective-permute-start.18 = (bf16[1280,256]{1,0:T(8,128)(2,1)S(1)}, bf16[1280,256]{1,0:T(8,128)(2,1)S(1)}, u32[]{:S(2)}, u32[]{:S(2)}) collective-permute-start(bf16[1280,256]{1,0:T(8,128)(2,1)S(1)} %shard_map.108), channel_id=1, source_target_pairs={{192,0},{0,64},{64,128},{128,192},{193,1},{1,65},{65,129},{129,193... | collective-permute-start | bytes 1966088 | tf_op jit(solution)/shard_map/ppermute | solution.py:51
  108.2 13.0 %collective-permute-start.17 = (bf16[1280,256]{1,0:T(8,128)(2,1)S(1)}, bf16[1280,256]{1,0:T(8,128)(2,1)S(1)}, u32[]{:S(2)}, u32[]{:S(2)}) collective-permute-start(bf16[1280,256]{1,0:T(8,128)(2,1)S(1)} %shard_map.107), channel_id=1, source_target_pairs={{64,0},{128,64},{192,128},{0,192},{65,1},{129,65},{193,129},{1,193... | collective-permute-start | bytes 1966088 | tf_op jit(solution)/shard_map/ppermute | solution.py:51
  124.7 46.5 %copy-start.5 = (bf16[1024,128]{1,0:T(8,128)(2,1)S(1)}, bf16[1024,128]{1,0:T(8,128)(2,1)}, u32[]{:S(2)}) copy-start(bf16[1024,128]{1,0:T(8,128)(2,1)} %w_ref.3) | copy-start | bytes 786436
  171.9 10.1 %collective-permute-start.19 = (f32[40,128]{1,0:T(8,128)S(1)}, f32[40,128]{1,0:T(8,128)S(1)}, u32[]{:S(2)}, u32[]{:S(2)}) collective-permute-start(f32[40,128]{1,0:T(8,128)S(1)} %shard_map.113.own_ref), channel_id=1, source_target_pairs={{0,1},{1,0},{2,3},{3,2},{4,5},{5,4},{6,7},{7,6},{8,9},{9,8},{10,11... | collective-permute-start | bytes 61448 | tf_op jit(solution)/shard_map/ppermute | solution.py:419
Sparse Core Ops, SparseCore 0:
  10.6 104.7 all-gather.1

commit v5 on v4

--- a/solution.py
+++ b/solution.py
@@ -17,7 +17,7 @@
 SIZES = {"dp": NX, "y": NY, "z": NZ}
 VMEM = pl.BlockSpec(memory_space=pltpu.VMEM)
 SMEM = pl.BlockSpec(memory_space=pltpu.SMEM)
-HBM = pl.BlockSpec(memory_space=pltpu.HBM)
+ANY = pl.BlockSpec(memory_space=pl.ANY)
 f32 = jnp.float32
 bf16 = jnp.bfloat16
 
@@ -34,7 +34,7 @@
 
 
 def call(kernel, outs, scratch, *args, mib=8, flops=0, hbm=()):
-    specs = [SMEM] + [HBM if i in hbm else VMEM for i in range(1, len(args))]
+    specs = [SMEM] + [ANY if i in hbm else VMEM for i in range(1, len(args))]
     return pl.pallas_call(
         kernel,
         out_shape=outs,
@@ -68,7 +68,7 @@
     return pl.pallas_call(
         functools.partial(pack_kernel, cuts),
         out_shape=shaped((sum(rows for _, rows in cuts), first.shape[1]), first.dtype),
-        in_specs=[VMEM] * len(pieces) + [pl.BlockSpec(memory_space=pl.ANY)] * len(after),
+        in_specs=[VMEM] * len(pieces) + [ANY] * len(after),
         out_specs=VMEM,
         compiler_params=params(4),
         cost_estimate=pl.CostEstimate(flops=0, bytes_accessed=1 << 20, transcendentals=0),
@@ -87,11 +87,11 @@
     ]
 
 
-def gather(shard, use, q_sum, queries):
+def gather(shard, use, late):
     block = join([shard, recv(shard, "y", 1), recv(shard, "y", 2), recv(shard, "y", -1)])
     half = block.shape[0] // 2
     up1, down1 = recv(block, "z", 1), recv(block, "z", -1)
-    near = join([block, up1, down1], [q_sum])
+    near = join([block, up1, down1])
     near_up, near_down = recv(near, "dp", 1), recv(near, "dp", -1)
     up2, down2 = recv(up1, "z", 1), recv(down1, "z", -1)
     up3, down3 = recv(up2, "z", 1), recv(down2, "z", -1)
@@ -100,11 +100,11 @@
         recv(pack([(up3, 0, half)]), "z", 1),
         recv(pack([(down3, half, half)]), "z", -1),
     ]
-    rest = join([up2, down2, up3, down3, *far], [queries, *near_far])
+    rest = join([up2, down2, up3, down3, *far], near_far)
     rest_up, rest_down = recv(rest, "dp", 1), recv(rest, "dp", -1)
     (own,) = use([[near, rest]])
     rest_far = far_x(rest_up, rest_down, [own])
-    key_up, key_down = use([[near_up, rest_up], [near_down, rest_down]])
+    key_up, key_down = use([[near_up, rest_up], [near_down, rest_down]], late)
     (key_far,) = use([near_far + rest_far])
     return [own, key_up, key_far, key_down]
 
@@ -115,7 +115,7 @@
     return pl.multiple_of(at * LANES, LANES)
 
 
-def norm_kernel(pos, e_ref, gain_ref, out_ref, rows):
+def norm_kernel(pos, e_ref, gain_ref, after_ref, out_ref, rows):
     e = e_ref[...].astype(f32)
     scale = lax.rsqrt(jnp.mean(e * e, axis=-1, keepdims=True) + 1e-06)
     rows[...] = (e * scale * gain_ref[...].astype(f32)).astype(bf16)
@@ -123,7 +123,7 @@
         out_ref[:, i * LANES : (i + 1) * LANES] = rows[:, pl.ds(place(pos, i), LANES)]
 
 
-def normalise(pos, enc, gain, tile):
+def normalise(pos, enc, gain, after, tile):
     rows, width = enc.shape
     block = pl.BlockSpec((tile, width), lambda i, pos: (i, 0))
     return pl.pallas_call(
@@ -132,20 +132,24 @@
         grid_spec=pltpu.PrefetchScalarGridSpec(
             num_scalar_prefetch=1,
             grid=(rows // tile,),
-            in_specs=[block, pl.BlockSpec((1, width), lambda i, pos: (0, 0))],
+            in_specs=[
+                block,
+                pl.BlockSpec((1, width), lambda i, pos: (0, 0)),
+                ANY,
+            ],
             out_specs=block,
             scratch_shapes=[pltpu.VMEM((tile, width), bf16)],
         ),
-        compiler_params=params(12),
+        compiler_params=params(44),
         cost_estimate=pl.CostEstimate(
             flops=6 * rows * width, bytes_accessed=4 * rows * width, transcendentals=0
         ),
-    )(pos, enc, gain)
+    )(pos, enc, gain, after)
 
 
 def project_kernel(counts, x_ref, *refs):
     at_piece = 0
-    for count, out_ref in zip(counts, refs[sum(counts) :]):
+    for count, out_ref in zip(counts, refs[len(refs) - len(counts) :]):
         acc, at = None, 0
         for ref in refs[at_piece : at_piece + count]:
             depth = ref.shape[0]
@@ -156,14 +160,14 @@
         at_piece += count
 
 
-def project(x, lists):
+def project(x, lists, after=()):
     rows, width = x.shape
     cols = lists[0][0].shape[1]
     pieces = [piece for pieces in lists for piece in pieces]
     return pl.pallas_call(
         functools.partial(project_kernel, [len(pieces) for pieces in lists]),
         out_shape=[shaped((rows, cols), bf16)] * len(lists),
-        in_specs=[VMEM] * (1 + len(pieces)),
+        in_specs=[VMEM] * (1 + len(pieces)) + [ANY] * len(after),
         out_specs=[VMEM] * len(lists),
         compiler_params=params(8),
         cost_estimate=pl.CostEstimate(
@@ -171,10 +175,10 @@
             bytes_accessed=2 * (rows * width + width * cols + rows * cols),
             transcendentals=0,
         ),
-    )(x, *pieces)
-
-
-def query_kernel(pos, dec_ref, w_ref, out_ref):
+    )(x, *pieces, *after)
+
+
+def query_kernel(pos, dec_ref, w_ref, after_ref, out_ref):
     at = pl.multiple_of((pos[0] * NZ + pos[1]) * LANES, LANES)
     part = jnp.dot(dec_ref[:, pl.ds(at, LANES)], w_ref[...], preferred_element_type=f32)
     for j in range(out_ref.shape[1]):
@@ -192,8 +196,7 @@
     return row == col
 
 
-def softmax_kernel(plen, pos, q_ref, *refs):
-    keys, (high_ref, low_ref, stat_ref) = refs[:NX], refs[NX:]
+def softmax(plen, pos, q_ref, keys, high_ref, low_ref, stat_ref):
     answers = q_ref.shape[0]
     lane = lax.broadcasted_iota(jnp.int32, (answers, LANES), 1)
     stats = jnp.zeros((answers, LANES), f32)
@@ -239,7 +242,9 @@
     stat_ref[...] = stats
 
 
-def value_kernel(pos, x_hbm, high_ref, low_ref, stat_ref, v_hbm, out_ref, x_buf, buf, acc, x_sems, sems):
+def attend_kernel(plen, pos, q_ref, *refs):
+    keys, refs = refs[:NX], refs[NX:]
+    x_hbm, v_hbm, out_ref, high_ref, low_ref, stat_ref, x_buf, buf, acc, x_sems, sems = refs
     answers, rows, _ = out_ref.shape
     pairs = high_ref.shape[0] // NX
     cols = buf.shape[1] // NX
@@ -261,6 +266,7 @@
         fetch_x(part).start()
         for i in range(part * half, (part + 1) * half):
             fetch(i).start()
+    softmax(plen, pos, q_ref, keys, high_ref, low_ref, stat_ref)
     for part in range(2):
         fetch_x(part).wait()
         for i in range(part * half, (part + 1) * half):
@@ -351,9 +357,7 @@
     pos = jnp.concatenate([jnp.stack([y, z, x]), lengths.reshape(pdev)])
 
     w_values = lax.all_gather(w_value, PSG, axis=0, tiled=True)
-    normed = normalise(
-        pos, enc_states.reshape(slots, width), enc_gain[None], min(slots, 128)
-    )
+    gain = enc_gain[None]
     q_parts = call(
         query_kernel,
         shaped((answers, blocks, LANES)),
@@ -361,29 +365,24 @@
         pos,
         dec_states.reshape(answers, width),
         w_query,
+        gain,
+        hbm=(3,),
     )
     q_sum = call(spread_kernel, shaped(q_parts.shape), [], pos, exchange(q_parts))
     queries = exchange(q_sum)
+    normed = normalise(
+        pos, enc_states.reshape(slots, width), gain, q_sum, min(slots, 128)
+    )
 
     mine = lax.dynamic_slice(w_key, (0, x * quarter), (w_key.shape[0], quarter))
-    keys = gather(mine, functools.partial(project, normed), q_sum, queries)
-    high, low, stat = call(
-        functools.partial(softmax_kernel, plen),
-        [
-            shaped((pairs, slots), bf16),
-            shaped((pairs, slots), bf16),
-            shaped((answers, LANES)),
-        ],
-        [],
-        pos,
-        queries,
-        *keys,
-        flops=2 * pairs * slots * quarter,
-    )
+    keys = gather(mine, functools.partial(project, normed), [queries])
     parts = call(
-        value_kernel,
+        functools.partial(attend_kernel, plen),
         shaped((answers, blocks + 1, LANES)),
         [
+            pltpu.VMEM((pairs, slots), bf16),
+            pltpu.VMEM((pairs, slots), bf16),
+            pltpu.VMEM((answers, LANES), f32),
             pltpu.VMEM((slots, width), bf16),
             pltpu.VMEM((width, columns), bf16),
             pltpu.VMEM((slots, columns), f32),
@@ -391,14 +390,13 @@
             pltpu.SemaphoreType.DMA((len(ORDER),)),
         ],
         pos,
+        queries,
+        *keys,
         normed,
-        high,
-        low,
-        stat,
         w_values,
         mib=52,
         flops=2 * slots * width * columns,
-        hbm=(1, 5),
+        hbm=(2 + NX, 3 + NX),
     )
     rows = 2 * blocks
     merged = call(

time: 190 us -> 184 us (0.968)
  waiting for transfers between devices: 41.4 us -> 25.7 us
  blocking collectives: 47.8 us -> 56.7 us
  Pallas kernels: 36.3 us -> 38.7 us
    ppermute x19, waiting for transfers between devices: 33.9 us -> 24.2 us  [recv(): return lax.ppermute(a, axis, [((i + k) % n, i) for i in range(n)])]
    all_to_all x3 -> x4, blocking collectives: 47.8 us -> 56.7 us  [exchange(): return lax.all_to_all(a, PSG, split_axis=0, concat_axis=0, tiled=True)]
    all_to_all x1 -> x0, waiting for transfers between devices: 5.94 us -> none  [exchange(): return lax.all_to_all(a, PSG, split_axis=0, concat_axis=0, tiled=True)]
    all_to_all x1 -> x0, starting transfers between devices: 3.98 us -> none  [exchange(): return lax.all_to_all(a, PSG, split_axis=0, concat_axis=0, tiled=True)]
    ppermute x1, starting transfers between devices: 9.3 us -> 11.5 us  [body(): other = lax.ppermute(part, 'tp', [(0, 1), (1, 0)])]
    pallas_call x1, Pallas kernels: 5.87 us -> 7.99 us  [normalise(): pl.pallas_call(norm_kernel, out_shape=shaped((rows, width), bf16), grid_s...]
    pallas_call x7 -> x6, Pallas kernels: 19.3 us -> 17.9 us  [call(): pl.pallas_call(kernel, out_shape=outs, in_specs=specs, out_specs=jax.tree...]
    unnamed x18 -> x30, local copies, waits for them, and re-layouts: 5.84 us -> 5.62 us
  transfers between devices with their start and end apart: 22 -> 21, of which waited for: 10 -> 10; matrix products, arithmetic and copies ran while one was open for 0% -> 0% of each run, Pallas kernels for 11% -> 12%
where the time goes in v5:
time: 184 us
  blocking collectives  56.7 us (31%)
  starting transfers between devices  42.5 us (23%)
  Pallas kernels  38.7 us (21%)
  waiting for transfers between devices  25.7 us (14%)
  between operations  14.3 us (8%)
  local copies, waits for them, and re-layouts  5.64 us (3%)
    all_to_all x4, blocking collectives, exchange(): return lax.all_to_all(a, PSG, split_axis=0, concat_axis=0, tiled=True)  56.7 us
    ppermute x19, starting transfers between devices, recv(): return lax.ppermute(a, axis, [((i + k) % n, i) for i in range(n)])  30.9 us
    ppermute x19, waiting for transfers between devices, recv(): return lax.ppermute(a, axis, [((i + k) % n, i) for i in range(n)])  24.2 us
    pallas_call x6, Pallas kernels, call(): pl.pallas_call(kernel, out_shape=outs, in_specs=specs, out_specs=jax.tree...  17.9 us
    ppermute x1, starting transfers between devices, body(): other = lax.ppermute(part, 'tp', [(0, 1), (1, 0)])  11.5 us
    pallas_call x3, Pallas kernels, project(): pl.pallas_call(functools.partial(project_kernel, [len(pieces) for pieces...  8.75 us
    pallas_call x1, Pallas kernels, normalise(): pl.pallas_call(norm_kernel, out_shape=shaped((rows, width), bf16), grid_s...  7.99 us
    unnamed x30, local copies, waits for them, and re-layouts  5.62 us
  transfers between devices with their start and end apart: 21, of which 10 were waited for; matrix products, arithmetic and copies ran while one was open for 0% of the time, Pallas kernels for 12%

profile of v5, /device:TPU:1, one launch (start us, length us, event | category | flops | bytes accessed | tf_op | source)
XLA Modules:
  0.0 183.6 jit_solution(2434540675818279086)
XLA Ops:
  8.1 3.6 %collective-permute-start = (bf16[128,256]{1,0:T(8,128)(2,1)S(1)}, bf16[128,256]{1,0:T(8,128)(2,1)S(1)}, u32[]{:S(2)}, u32[]{:S(2)}) collective-permute-start(bf16[128,256]{1,0:T(8,128)(2,1)S(1)} %constant_dynamic-slice_fusion.refs_0_), channel_id=1, source_target_pairs={{16,0},{32,16},{48,32},{0,48},{17,1},{33,17},{49,33},{1,49},{18,2}... | collective-permute-start | bytes 196616 | tf_op jit(solution)/shard_map/ppermute | solution.py:51
  13.1 3.4 %collective-permute-done.1.refs_2_ = bf16[128,256]{1,0:T(8,128)(2,1)S(1)} collective-permute-done((bf16[128,256]{1,0:T(8,128)(2,1)S(1)}, bf16[128,256]{1,0:T(8,128)(2,1)S(1)}, u32[]{:S(2)}, u32[]{:S(2)}) %collective-permute-start.1) | collective-permute-done | bytes 65568 | tf_op jit(solution)/shard_map/ppermute | solution.py:51
  17.1 5.7 %collective-permute-start.3 = (bf16[512,256]{1,0:T(8,128)(2,1)S(1)}, bf16[512,256]{1,0:T(8,128)(2,1)S(1)}, u32[]{:S(2)}, u32[]{:S(2)}) collective-permute-start(bf16[512,256]{1,0:T(8,128)(2,1)S(1)} %shard_map.98.refs_0_), channel_id=1, source_target_pairs={{2,0},{4,2},{6,4},{8,6},{10,8},{12,10},{14,12},{0,14},{3,1},{5,3},... | collective-permute-start | bytes 786440 | tf_op jit(solution)/shard_map/ppermute | solution.py:51
  22.8 3.3 %collective-permute-done.3.refs_1_ = bf16[512,256]{1,0:T(8,128)(2,1)S(1)} collective-permute-done((bf16[512,256]{1,0:T(8,128)(2,1)S(1)}, bf16[512,256]{1,0:T(8,128)(2,1)S(1)}, u32[]{:S(2)}, u32[]{:S(2)}) %collective-permute-start.3) | collective-permute-done | bytes 262176 | tf_op jit(solution)/shard_map/ppermute | solution.py:51
  26.1 3.1 %collective-permute-done.4.refs_2_ = bf16[512,256]{1,0:T(8,128)(2,1)S(1)} collective-permute-done((bf16[512,256]{1,0:T(8,128)(2,1)S(1)}, bf16[512,256]{1,0:T(8,128)(2,1)S(1)}, u32[]{:S(2)}, u32[]{:S(2)}) %collective-permute-start.4) | collective-permute-done | bytes 262176 | tf_op jit(solution)/shard_map/ppermute | solution.py:51
  29.3 2.6 %collective-permute-start.11 = (bf16[1536,256]{1,0:T(8,128)(2,1)S(1)}, bf16[1536,256]{1,0:T(8,128)(2,1)S(1)}, u32[]{:S(2)}, u32[]{:S(2)}) collective-permute-start(bf16[1536,256]{1,0:T(8,128)(2,1)S(1)} %shard_map.99.refs_0_), channel_id=1, source_target_pairs={{64,0},{128,64},{192,128},{0,192},{65,1},{129,65},{193,129},{1,193... | collective-permute-start | bytes 2359304 | tf_op jit(solution)/shard_map/ppermute | solution.py:51
  31.8 2.7 %collective-permute-start.5 = (bf16[512,256]{1,0:T(8,128)(2,1)S(1)}, bf16[512,256]{1,0:T(8,128)(2,1)S(1)}, u32[]{:S(2)}, u32[]{:S(2)}) collective-permute-start(bf16[512,256]{1,0:T(8,128)(2,1)S(1)} %collective-permute-done.3.refs_1_), channel_id=1, source_target_pairs={{2,0},{4,2},{6,4},{8,6},{10,8},{12,10},{14,12},{0,14},{3,1},{5,3},... | collective-permute-start | bytes 786440 | tf_op jit(solution)/shard_map/ppermute | solution.py:51
  34.5 5.6 %collective-permute-done.6.refs_1_ = bf16[512,256]{1,0:T(8,128)(2,1)S(1)} collective-permute-done((bf16[512,256]{1,0:T(8,128)(2,1)S(1)}, bf16[512,256]{1,0:T(8,128)(2,1)S(1)}, u32[]{:S(2)}, u32[]{:S(2)}) %collective-permute-start.6) | collective-permute-done | bytes 262176 | tf_op jit(solution)/shard_map/ppermute | solution.py:51
  40.1 2.7 %collective-permute-start.7 = (bf16[512,256]{1,0:T(8,128)(2,1)S(1)}, bf16[512,256]{1,0:T(8,128)(2,1)S(1)}, u32[]{:S(2)}, u32[]{:S(2)}) collective-permute-start(bf16[512,256]{1,0:T(8,128)(2,1)S(1)} %collective-permute-done.5.refs_0_), channel_id=1, source_target_pairs={{2,0},{4,2},{6,4},{8,6},{10,8},{12,10},{14,12},{0,14},{3,1},{5,3},... | collective-permute-start | bytes 786440 | tf_op jit(solution)/shard_map/ppermute | solution.py:51
  42.7 1.4 collective-permute-done.11.refs_0_
  44.2 3.6 %collective-permute-start.12 = (bf16[768,256]{1,0:T(8,128)(2,1)S(1)}, bf16[768,256]{1,0:T(8,128)(2,1)S(1)}, u32[]{:S(2)}, u32[]{:S(2)}) collective-permute-start(bf16[768,256]{1,0:T(8,128)(2,1)S(1)} %shard_map.102), channel_id=1, source_target_pairs={{64,0},{128,64},{192,128},{0,192},{65,1},{129,65},{193,129},{1,193... | collective-permute-start | bytes 1179656 | tf_op jit(solution)/shard_map/ppermute | solution.py:51
  47.9 2.6 %collective-permute-done.8.refs_0_.refs_3_ = bf16[512,256]{1,0:T(8,128)(2,1)S(1)} collective-permute-done((bf16[512,256]{1,0:T(8,128)(2,1)S(1)}, bf16[512,256]{1,0:T(8,128)(2,1)S(1)}, u32[]{:S(2)}, u32[]{:S(2)}) %collective-permute-start.8) | collective-permute-done | bytes 262176 | tf_op jit(solution)/shard_map/ppermute | solution.py:51
  50.7 2.7 %collective-permute-start.9 = (bf16[256,256]{1,0:T(8,128)(2,1)S(1)}, bf16[256,256]{1,0:T(8,128)(2,1)S(1)}, u32[]{:S(2)}, u32[]{:S(2)}) collective-permute-start(bf16[256,256]{1,0:T(8,128)(2,1)S(1)} %shard_map.100), channel_id=1, source_target_pairs={{2,0},{4,2},{6,4},{8,6},{10,8},{12,10},{14,12},{0,14},{3,1},{5,3},... | collective-permute-start | bytes 393224 | tf_op jit(solution)/shard_map/ppermute | solution.py:51
  53.4 3.8 %collective-permute-done.10.refs_5_ = bf16[256,256]{1,0:T(8,128)(2,1)S(1)} collective-permute-done((bf16[256,256]{1,0:T(8,128)(2,1)S(1)}, bf16[256,256]{1,0:T(8,128)(2,1)S(1)}, u32[]{:S(2)}, u32[]{:S(2)}) %collective-permute-start.10) | collective-permute-done | bytes 131104 | tf_op jit(solution)/shard_map/ppermute | solution.py:51
  57.3 1.3 collective-permute-start.16
  58.7 2.1 %collective-permute-start.15 = (bf16[2560,256]{1,0:T(8,128)(2,1)S(1)}, bf16[2560,256]{1,0:T(8,128)(2,1)}, u32[]{:S(2)}, u32[]{:S(2)}) collective-permute-start(bf16[2560,256]{1,0:T(8,128)(2,1)S(1)} %shard_map.104.refs_1_), channel_id=1, source_target_pairs={{64,0},{128,64},{192,128},{0,192},{65,1},{129,65},{193,129},{1,193... | collective-permute-start | bytes 3932168 | tf_op jit(solution)/shard_map/ppermute | solution.py:51
  63.5 14.9 %all_to_all.20.got_ref = f32[32,8,128]{2,1,0:T(8,128)S(1)} all-to-all(f32[32,8,128]{2,1,0:T(8,128)S(1)} %shard_map.95), channel_id=1, replica_groups=mesh['dp'=4,'y'=4,'z'=8,'tp'=2] {'y','z'}, dimensions={0} | all-to-all | bytes 262144 | tf_op jit(solution)/shard_map/all_to_all | solution.py:55
  79.0 8.0 %shard_map.97.x_ref.refs_4_ = bf16[768,4096]{1,0:T(8,128)(2,1)S(1)} custom-call(s32[6]{0:T(128)S(1)} %pad_add_fusion.pos, bf16[768,4096]{1,0:T(8,128)(2,1)} %bitcast.8, bf16[1,4096]{1,0:T(2,128)(2,1)S(1)} %broadcast_in_dim.6.after_ref.gain_ref, f32[32,8,128]{2,1,0:T(8,128)S(1)} %shard_map.96.after_ref), custom_call_target="tpu_custom_call" | custom-call | flops 18874368 | bytes 12582912 | tf_op jit(solution)/shard_map/pallas_call | solution.py:129
  87.0 1.8 shard_map.105.refs_1_.refs_0_
  88.8 2.3 %shard_map.108 = bf16[1280,256]{1,0:T(8,128)(2,1)S(1)} custom-call(bf16[2560,256]{1,0:T(8,128)(2,1)} %collective-permute-done.16.refs_3_.refs_0_, bf16[768,256]{1,0:T(8,128)(2,1)S(1)} %shard_map.105.refs_1_.refs_0_), custom_call_target="tpu_custom_call" | custom-call | bytes 1048576 | tf_op jit(solution)/shard_map/pallas_call | solution.py:68
  91.3 1.4 shard_map.107
  92.7 2.7 %collective-permute-start.17 = (bf16[1280,256]{1,0:T(8,128)(2,1)S(1)}, bf16[1280,256]{1,0:T(8,128)(2,1)S(1)}, u32[]{:S(2)}, u32[]{:S(2)}) collective-permute-start(bf16[1280,256]{1,0:T(8,128)(2,1)S(1)} %shard_map.107), channel_id=1, source_target_pairs={{64,0},{128,64},{192,128},{0,192},{65,1},{129,65},{193,129},{1,193... | collective-permute-start | bytes 1966088 | tf_op jit(solution)/shard_map/ppermute | solution.py:51
  95.4 13.7 %all_to_all.21.refs_4_.q_ref = f32[32,8,128]{2,1,0:T(8,128)S(1)} all-to-all(f32[32,8,128]{2,1,0:T(8,128)S(1)} %shard_map.96.after_ref), channel_id=1, replica_groups=mesh['dp'=4,'y'=4,'z'=8,'tp'=2] {'y','z'}, dimensions={0} | all-to-all | bytes 262144 | tf_op jit(solution)/shard_map/all_to_all | solution.py:55
  109.2 5.2 %shard_map.106 = (bf16[768,256]{1,0:T(8,128)(2,1)S(1)}, bf16[768,256]{1,0:T(8,128)(2,1)S(1)}) custom-call(bf16[768,4096]{1,0:T(8,128)(2,1)S(1)} %shard_map.97.x_ref.refs_4_, bf16[1536,256]{1,0:T(8,128)(2,1)S(1)} %copy-done.3, bf16[2560,256]{1,0:T(8,128)(2,1)} %collective-permute-done.15.refs_1_.refs_0_, bf16[1536,256]{1,0:T(8,128)(2,1)S(1)} %copy-done.5, ...), custom_call_target="tpu_custom_call" | custom-call | flops 3221225472 | bytes 8781824 | tf_op jit(solution)/shard_map/pallas_call | solution.py:167
  115.9 1.8 shard_map.109.refs_2_
  117.7 1.0 copy-done.10
  118.7 1.0 copy-done.12
  119.7 13.8 %shard_map.110 = f32[32,9,128]{2,1,0:T(8,128)S(1)} custom-call(s32[6]{0:T(128)S(1)} %pad_add_fusion.pos, f32[32,8,128]{2,1,0:T(8,128)S(1)} %all_to_all.21.refs_4_.q_ref, bf16[768,256]{1,0:T(8,128)(2,1)S(1)} %shard_map.105.refs_1_.refs_0_, bf16[768,256]{1,0:T(8,128)(2,1)S(1)} %copy-done.10, bf16[768,256]{1,0:T(8,128)(2,1)S(1)} %shard_map.109.refs_2_, ...), custom_call_target="tpu_custom_call" | custom-call | flops 6442450944 | bytes 1048576 | tf_op jit(solution)/shard_map/pallas_call | solution.py:38
  133.5 14.7 %all_to_all.22.got_ref = f32[32,9,128]{2,1,0:T(8,128)S(1)} all-to-all(f32[32,9,128]{2,1,0:T(8,128)S(1)} %shard_map.110), channel_id=1, replica_groups=mesh['dp'=4,'y'=4,'z'=8,'tp'=2] {'y','z'}, dimensions={0} | all-to-all | bytes 294912 | tf_op jit(solution)/shard_map/all_to_all | solution.py:55
  149.1 13.3 %all_to_all.23.ctx_ref = bf16[32,16,128]{2,1,0:T(8,128)(2,1)S(1)} all-to-all(bf16[32,16,128]{2,1,0:T(8,128)(2,1)S(1)} %shard_map.111), channel_id=1, replica_groups=mesh['dp'=4,'y'=4,'z'=8,'tp'=2] {'y','z'}, dimensions={0} | all-to-all | bytes 262144 | tf_op jit(solution)/shard_map/all_to_all | solution.py:55
  163.2 11.5 %collective-permute-start.19 = (f32[40,128]{1,0:T(8,128)S(1)}, f32[40,128]{1,0:T(8,128)S(1)}, u32[]{:S(2)}, u32[]{:S(2)}) collective-permute-start(f32[40,128]{1,0:T(8,128)S(1)} %shard_map.112.own_ref), channel_id=1, source_target_pairs={{0,1},{1,0},{2,3},{3,2},{4,5},{5,4},{6,7},{7,6},{8,9},{9,8},{10,11... | collective-permute-start | bytes 61448 | tf_op jit(solution)/shard_map/ppermute | solution.py:417
  175.6 1.1 shard_map.113
  (67 shorter events, 10.8 us)
Async XLA Ops:
  7.2 1.0 copy-start
  7.2 53.5 %copy-start.13 = (bf16[4096]{0:T(1024)(128)(2,1)S(1)}, bf16[4096]{0:T(1024)(128)(2,1)}, u32[]{:S(2)}) copy-start(bf16[4096]{0:T(1024)(128)(2,1)} %param.10) | copy-start | bytes 24580
  7.2 53.5 %copy-start.14 = (s32[1,3]{1,0:T(1,128)S(1)}, s32[1,3]{1,0:T(1,128)}, u32[]{:S(2)}) copy-start(s32[1,3]{1,0:T(1,128)} %param.9) | copy-start | bytes 40
  7.2 110.5 %all-gather.2.cloned.1.call-start = ((), (), s32[]{:S(2)}) async-start(), calls=%async_computation.4 | async-start | bytes 8650752 | tf_op jit(solution)/shard_map/all_gather | solution.py:359
  8.1 5.0 %collective-permute-start = (bf16[128,256]{1,0:T(8,128)(2,1)S(1)}, bf16[128,256]{1,0:T(8,128)(2,1)S(1)}, u32[]{:S(2)}, u32[]{:S(2)}) collective-permute-start(bf16[128,256]{1,0:T(8,128)(2,1)S(1)} %constant_dynamic-slice_fusion.refs_0_), channel_id=1, source_target_pairs={{16,0},{32,16},{48,32},{0,48},{17,1},{33,17},{49,33},{1,49},{18,2}... | collective-permute-start | bytes 196616 | tf_op jit(solution)/shard_map/ppermute | solution.py:51
  11.8 4.7 %collective-permute-start.1 = (bf16[128,256]{1,0:T(8,128)(2,1)S(1)}, bf16[128,256]{1,0:T(8,128)(2,1)S(1)}, u32[]{:S(2)}, u32[]{:S(2)}) collective-permute-start(bf16[128,256]{1,0:T(8,128)(2,1)S(1)} %constant_dynamic-slice_fusion.refs_0_), channel_id=1, source_target_pairs={{32,0},{48,16},{0,32},{16,48},{33,1},{49,17},{1,33},{17,49},{34,2}... | collective-permute-start | bytes 196616 | tf_op jit(solution)/shard_map/ppermute | solution.py:51
  12.1 5.0 %collective-permute-start.2 = (bf16[128,256]{1,0:T(8,128)(2,1)S(1)}, bf16[128,256]{1,0:T(8,128)(2,1)S(1)}, u32[]{:S(2)}, u32[]{:S(2)}) collective-permute-start(bf16[128,256]{1,0:T(8,128)(2,1)S(1)} %constant_dynamic-slice_fusion.refs_0_), channel_id=1, source_target_pairs={{48,0},{0,16},{16,32},{32,48},{49,1},{1,17},{17,33},{33,49},{50,2}... | collective-permute-start | bytes 196616 | tf_op jit(solution)/shard_map/ppermute | solution.py:51
  17.1 9.0 %collective-permute-start.3 = (bf16[512,256]{1,0:T(8,128)(2,1)S(1)}, bf16[512,256]{1,0:T(8,128)(2,1)S(1)}, u32[]{:S(2)}, u32[]{:S(2)}) collective-permute-start(bf16[512,256]{1,0:T(8,128)(2,1)S(1)} %shard_map.98.refs_0_), channel_id=1, source_target_pairs={{2,0},{4,2},{6,4},{8,6},{10,8},{12,10},{14,12},{0,14},{3,1},{5,3},... | collective-permute-start | bytes 786440 | tf_op jit(solution)/shard_map/ppermute | solution.py:51
  22.8 6.4 %collective-permute-start.4 = (bf16[512,256]{1,0:T(8,128)(2,1)S(1)}, bf16[512,256]{1,0:T(8,128)(2,1)S(1)}, u32[]{:S(2)}, u32[]{:S(2)}) collective-permute-start(bf16[512,256]{1,0:T(8,128)(2,1)S(1)} %shard_map.98.refs_0_), channel_id=1, source_target_pairs={{14,0},{0,2},{2,4},{4,6},{6,8},{8,10},{10,12},{12,14},{15,1},{1,3}... | collective-permute-start | bytes 786440 | tf_op jit(solution)/shard_map/ppermute | solution.py:51
  29.3 14.9 %collective-permute-start.11 = (bf16[1536,256]{1,0:T(8,128)(2,1)S(1)}, bf16[1536,256]{1,0:T(8,128)(2,1)S(1)}, u32[]{:S(2)}, u32[]{:S(2)}) collective-permute-start(bf16[1536,256]{1,0:T(8,128)(2,1)S(1)} %shard_map.99.refs_0_), channel_id=1, source_target_pairs={{64,0},{128,64},{192,128},{0,192},{65,1},{129,65},{193,129},{1,193... | collective-permute-start | bytes 2359304 | tf_op jit(solution)/shard_map/ppermute | solution.py:51
  31.8 16.0 %collective-permute-start.13 = (bf16[1536,256]{1,0:T(8,128)(2,1)S(1)}, bf16[1536,256]{1,0:T(8,128)(2,1)S(1)}, u32[]{:S(2)}, u32[]{:S(2)}) collective-permute-start(bf16[1536,256]{1,0:T(8,128)(2,1)S(1)} %shard_map.99.refs_0_), channel_id=1, source_target_pairs={{192,0},{0,64},{64,128},{128,192},{193,1},{1,65},{65,129},{129,193... | collective-permute-start | bytes 2359304 | tf_op jit(solution)/shard_map/ppermute | solution.py:51
  31.8 8.2 %collective-permute-start.6 = (bf16[512,256]{1,0:T(8,128)(2,1)S(1)}, bf16[512,256]{1,0:T(8,128)(2,1)S(1)}, u32[]{:S(2)}, u32[]{:S(2)}) collective-permute-start(bf16[512,256]{1,0:T(8,128)(2,1)S(1)} %collective-permute-done.4.refs_2_), channel_id=1, source_target_pairs={{14,0},{0,2},{2,4},{4,6},{6,8},{8,10},{10,12},{12,14},{15,1},{1,3}... | collective-permute-start | bytes 786440 | tf_op jit(solution)/shard_map/ppermute | solution.py:51
  31.8 8.2 %collective-permute-start.5 = (bf16[512,256]{1,0:T(8,128)(2,1)S(1)}, bf16[512,256]{1,0:T(8,128)(2,1)S(1)}, u32[]{:S(2)}, u32[]{:S(2)}) collective-permute-start(bf16[512,256]{1,0:T(8,128)(2,1)S(1)} %collective-permute-done.3.refs_1_), channel_id=1, source_target_pairs={{2,0},{4,2},{6,4},{8,6},{10,8},{12,10},{14,12},{0,14},{3,1},{5,3},... | collective-permute-start | bytes 786440 | tf_op jit(solution)/shard_map/ppermute | solution.py:51
  40.1 10.5 %collective-permute-start.8 = (bf16[512,256]{1,0:T(8,128)(2,1)S(1)}, bf16[512,256]{1,0:T(8,128)(2,1)S(1)}, u32[]{:S(2)}, u32[]{:S(2)}) collective-permute-start(bf16[512,256]{1,0:T(8,128)(2,1)S(1)} %collective-permute-done.6.refs_1_), channel_id=1, source_target_pairs={{14,0},{0,2},{2,4},{4,6},{6,8},{8,10},{10,12},{12,14},{15,1},{1,3}... | collective-permute-start | bytes 786440 | tf_op jit(solution)/shard_map/ppermute | solution.py:51
  40.1 10.6 %collective-permute-start.7 = (bf16[512,256]{1,0:T(8,128)(2,1)S(1)}, bf16[512,256]{1,0:T(8,128)(2,1)S(1)}, u32[]{:S(2)}, u32[]{:S(2)}) collective-permute-start(bf16[512,256]{1,0:T(8,128)(2,1)S(1)} %collective-permute-done.5.refs_0_), channel_id=1, source_target_pairs={{2,0},{4,2},{6,4},{8,6},{10,8},{12,10},{14,12},{0,14},{3,1},{5,3},... | collective-permute-start | bytes 786440 | tf_op jit(solution)/shard_map/ppermute | solution.py:51
  44.2 13.0 %copy-start.2 = (bf16[1536,256]{1,0:T(8,128)(2,1)}, bf16[1536,256]{1,0:T(8,128)(2,1)S(1)}, u32[]{:S(2)}) copy-start(bf16[1536,256]{1,0:T(8,128)(2,1)S(1)} %collective-permute-done.11.refs_0_) | copy-start | bytes 2359300
  44.2 13.0 %collective-permute-start.12 = (bf16[768,256]{1,0:T(8,128)(2,1)S(1)}, bf16[768,256]{1,0:T(8,128)(2,1)S(1)}, u32[]{:S(2)}, u32[]{:S(2)}) collective-permute-start(bf16[768,256]{1,0:T(8,128)(2,1)S(1)} %shard_map.102), channel_id=1, source_target_pairs={{64,0},{128,64},{192,128},{0,192},{65,1},{129,65},{193,129},{1,193... | collective-permute-start | bytes 1179656 | tf_op jit(solution)/shard_map/ppermute | solution.py:51
  47.8 9.5 %copy-start.4 = (bf16[1536,256]{1,0:T(8,128)(2,1)}, bf16[1536,256]{1,0:T(8,128)(2,1)S(1)}, u32[]{:S(2)}) copy-start(bf16[1536,256]{1,0:T(8,128)(2,1)S(1)} %collective-permute-done.13.refs_0_.refs_2_) | copy-start | bytes 2359300
  47.8 9.4 %collective-permute-start.14 = (bf16[768,256]{1,0:T(8,128)(2,1)S(1)}, bf16[768,256]{1,0:T(8,128)(2,1)S(1)}, u32[]{:S(2)}, u32[]{:S(2)}) collective-permute-start(bf16[768,256]{1,0:T(8,128)(2,1)S(1)} %shard_map.103), channel_id=1, source_target_pairs={{192,0},{0,64},{64,128},{128,192},{193,1},{1,65},{65,129},{129,193... | collective-permute-start | bytes 1179656 | tf_op jit(solution)/shard_map/ppermute | solution.py:51
  50.5 6.7 %collective-permute-start.10 = (bf16[256,256]{1,0:T(8,128)(2,1)S(1)}, bf16[256,256]{1,0:T(8,128)(2,1)S(1)}, u32[]{:S(2)}, u32[]{:S(2)}) collective-permute-start(bf16[256,256]{1,0:T(8,128)(2,1)S(1)} %shard_map.101), channel_id=1, source_target_pairs={{14,0},{0,2},{2,4},{4,6},{6,8},{8,10},{10,12},{12,14},{15,1},{1,3}... | collective-permute-start | bytes 393224 | tf_op jit(solution)/shard_map/ppermute | solution.py:51
  50.7 6.5 %collective-permute-start.9 = (bf16[256,256]{1,0:T(8,128)(2,1)S(1)}, bf16[256,256]{1,0:T(8,128)(2,1)S(1)}, u32[]{:S(2)}, u32[]{:S(2)}) collective-permute-start(bf16[256,256]{1,0:T(8,128)(2,1)S(1)} %shard_map.100), channel_id=1, source_target_pairs={{2,0},{4,2},{6,4},{8,6},{10,8},{12,10},{14,12},{0,14},{3,1},{5,3},... | collective-permute-start | bytes 393224 | tf_op jit(solution)/shard_map/ppermute | solution.py:51
  57.3 31.5 %collective-permute-start.16 = (bf16[2560,256]{1,0:T(8,128)(2,1)S(1)}, bf16[2560,256]{1,0:T(8,128)(2,1)}, u32[]{:S(2)}, u32[]{:S(2)}) collective-permute-start(bf16[2560,256]{1,0:T(8,128)(2,1)S(1)} %shard_map.104.refs_1_), channel_id=1, source_target_pairs={{192,0},{0,64},{64,128},{128,192},{193,1},{1,65},{65,129},{129,193... | collective-permute-start | bytes 3932168 | tf_op jit(solution)/shard_map/ppermute | solution.py:51
  58.7 32.6 %collective-permute-start.15 = (bf16[2560,256]{1,0:T(8,128)(2,1)S(1)}, bf16[2560,256]{1,0:T(8,128)(2,1)}, u32[]{:S(2)}, u32[]{:S(2)}) collective-permute-start(bf16[2560,256]{1,0:T(8,128)(2,1)S(1)} %shard_map.104.refs_1_), channel_id=1, source_target_pairs={{64,0},{128,64},{192,128},{0,192},{65,1},{129,65},{193,129},{1,193... | collective-permute-start | bytes 3932168 | tf_op jit(solution)/shard_map/ppermute | solution.py:51
  87.0 28.8 %copy-start.1 = (bf16[768,4096]{1,0:T(8,128)(2,1)}, bf16[768,4096]{1,0:T(8,128)(2,1)S(1)}, u32[]{:S(2)}) copy-start(bf16[768,4096]{1,0:T(8,128)(2,1)S(1)} %shard_map.97.x_ref.refs_4_) | copy-start | bytes 18874372
  87.0 22.1 %copy-start.3 = (bf16[1536,256]{1,0:T(8,128)(2,1)S(1)}, bf16[1536,256]{1,0:T(8,128)(2,1)}, u32[]{:S(2)}) copy-start(bf16[1536,256]{1,0:T(8,128)(2,1)} %copy-done.2) | copy-start | bytes 2359300
  87.0 22.1 %copy-start.5 = (bf16[1536,256]{1,0:T(8,128)(2,1)S(1)}, bf16[1536,256]{1,0:T(8,128)(2,1)}, u32[]{:S(2)}) copy-start(bf16[1536,256]{1,0:T(8,128)(2,1)} %copy-done.4) | copy-start | bytes 2359300
  91.2 24.7 %collective-permute-start.18 = (bf16[1280,256]{1,0:T(8,128)(2,1)S(1)}, bf16[1280,256]{1,0:T(8,128)(2,1)S(1)}, u32[]{:S(2)}, u32[]{:S(2)}) collective-permute-start(bf16[1280,256]{1,0:T(8,128)(2,1)S(1)} %shard_map.108), channel_id=1, source_target_pairs={{192,0},{0,64},{64,128},{128,192},{193,1},{1,65},{65,129},{129,193... | collective-permute-start | bytes 1966088 | tf_op jit(solution)/shard_map/ppermute | solution.py:51
  92.7 23.1 %collective-permute-start.17 = (bf16[1280,256]{1,0:T(8,128)(2,1)S(1)}, bf16[1280,256]{1,0:T(8,128)(2,1)S(1)}, u32[]{:S(2)}, u32[]{:S(2)}) collective-permute-start(bf16[1280,256]{1,0:T(8,128)(2,1)S(1)} %shard_map.107), channel_id=1, source_target_pairs={{64,0},{128,64},{192,128},{0,192},{65,1},{129,65},{193,129},{1,193... | collective-permute-start | bytes 1966088 | tf_op jit(solution)/shard_map/ppermute | solution.py:51
  117.7 1.0 copy-start.10
  118.7 1.0 copy-start.12
  119.7 42.8 %copy-start.6 = (bf16[1024,128]{1,0:T(8,128)(2,1)S(1)}, bf16[1024,128]{1,0:T(8,128)(2,1)}, u32[]{:S(2)}) copy-start(bf16[1024,128]{1,0:T(8,128)(2,1)} %w_ref.3) | copy-start | bytes 786436
  163.2 12.4 %collective-permute-start.19 = (f32[40,128]{1,0:T(8,128)S(1)}, f32[40,128]{1,0:T(8,128)S(1)}, u32[]{:S(2)}, u32[]{:S(2)}) collective-permute-start(f32[40,128]{1,0:T(8,128)S(1)} %shard_map.112.own_ref), channel_id=1, source_target_pairs={{0,1},{1,0},{2,3},{3,2},{4,5},{5,4},{6,7},{7,6},{8,9},{9,8},{10,11... | collective-permute-start | bytes 61448 | tf_op jit(solution)/shard_map/ppermute | solution.py:417
  (4 other events, 3.4 us)
Sparse Core Ops, SparseCore 0:
  10.6 106.7 all-gather.1

commit v6 on v5

--- a/solution.py
+++ b/solution.py
@@ -87,11 +87,11 @@
     ]
 
 
-def gather(shard, use, late):
+def gather(shard, use, first, second, third):
     block = join([shard, recv(shard, "y", 1), recv(shard, "y", 2), recv(shard, "y", -1)])
     half = block.shape[0] // 2
     up1, down1 = recv(block, "z", 1), recv(block, "z", -1)
-    near = join([block, up1, down1])
+    near = join([block, up1, down1], [first])
     near_up, near_down = recv(near, "dp", 1), recv(near, "dp", -1)
     up2, down2 = recv(up1, "z", 1), recv(down1, "z", -1)
     up3, down3 = recv(up2, "z", 1), recv(down2, "z", -1)
@@ -102,9 +102,10 @@
     ]
     rest = join([up2, down2, up3, down3, *far], near_far)
     rest_up, rest_down = recv(rest, "dp", 1), recv(rest, "dp", -1)
-    (own,) = use([[near, rest]])
+    (own,) = use([[near, rest]], [second])
     rest_far = far_x(rest_up, rest_down, [own])
-    key_up, key_down = use([[near_up, rest_up], [near_down, rest_down]], late)
+    (key_up,) = use([[near_up, rest_up]], [third])
+    (key_down,) = use([[near_down, rest_down]], [third])
     (key_far,) = use([near_far + rest_far])
     return [own, key_up, key_far, key_down]
 
@@ -115,7 +116,7 @@
     return pl.multiple_of(at * LANES, LANES)
 
 
-def norm_kernel(pos, e_ref, gain_ref, after_ref, out_ref, rows):
+def norm_kernel(pos, e_ref, gain_ref, out_ref, rows):
     e = e_ref[...].astype(f32)
     scale = lax.rsqrt(jnp.mean(e * e, axis=-1, keepdims=True) + 1e-06)
     rows[...] = (e * scale * gain_ref[...].astype(f32)).astype(bf16)
@@ -123,7 +124,7 @@
         out_ref[:, i * LANES : (i + 1) * LANES] = rows[:, pl.ds(place(pos, i), LANES)]
 
 
-def normalise(pos, enc, gain, after, tile):
+def normalise(pos, enc, gain, tile):
     rows, width = enc.shape
     block = pl.BlockSpec((tile, width), lambda i, pos: (i, 0))
     return pl.pallas_call(
@@ -135,7 +136,6 @@
             in_specs=[
                 block,
                 pl.BlockSpec((1, width), lambda i, pos: (0, 0)),
-                ANY,
             ],
             out_specs=block,
             scratch_shapes=[pltpu.VMEM((tile, width), bf16)],
@@ -144,7 +144,7 @@
         cost_estimate=pl.CostEstimate(
             flops=6 * rows * width, bytes_accessed=4 * rows * width, transcendentals=0
         ),
-    )(pos, enc, gain, after)
+    )(pos, enc, gain)
 
 
 def project_kernel(counts, x_ref, *refs):
@@ -244,7 +244,7 @@
 
 def attend_kernel(plen, pos, q_ref, *refs):
     keys, refs = refs[:NX], refs[NX:]
-    x_hbm, v_hbm, out_ref, high_ref, low_ref, stat_ref, x_buf, buf, acc, x_sems, sems = refs
+    x_hbm, v_hbm, out_ref, k_buf, high_ref, low_ref, stat_ref, x_buf, buf, acc, k_sems, x_sems, sems = refs
     answers, rows, _ = out_ref.shape
     pairs = high_ref.shape[0] // NX
     cols = buf.shape[1] // NX
@@ -262,11 +262,18 @@
         at = pl.ds(part * half * LANES, half * LANES)
         return pltpu.make_async_copy(x_hbm.at[:, at], x_buf.at[:, at], x_sems.at[part])
 
+    def fetch_key(i):
+        return pltpu.make_async_copy(keys[i], k_buf.at[i], k_sems.at[i])
+
+    for i in range(NX):
+        fetch_key(i).start()
     for part in range(2):
         fetch_x(part).start()
         for i in range(part * half, (part + 1) * half):
             fetch(i).start()
-    softmax(plen, pos, q_ref, keys, high_ref, low_ref, stat_ref)
+    for i in range(NX):
+        fetch_key(i).wait()
+    softmax(plen, pos, q_ref, [k_buf.at[i] for i in range(NX)], high_ref, low_ref, stat_ref)
     for part in range(2):
         fetch_x(part).wait()
         for i in range(part * half, (part + 1) * half):
@@ -371,21 +378,23 @@
     q_sum = call(spread_kernel, shaped(q_parts.shape), [], pos, exchange(q_parts))
     queries = exchange(q_sum)
     normed = normalise(
-        pos, enc_states.reshape(slots, width), gain, q_sum, min(slots, 128)
+        pos, enc_states.reshape(slots, width), gain, min(slots, 128)
     )
 
     mine = lax.dynamic_slice(w_key, (0, x * quarter), (w_key.shape[0], quarter))
-    keys = gather(mine, functools.partial(project, normed), [queries])
+    keys = gather(mine, functools.partial(project, normed), normed, q_sum, queries)
     parts = call(
         functools.partial(attend_kernel, plen),
         shaped((answers, blocks + 1, LANES)),
         [
+            pltpu.VMEM((NX, slots, quarter), bf16),
             pltpu.VMEM((pairs, slots), bf16),
             pltpu.VMEM((pairs, slots), bf16),
             pltpu.VMEM((answers, LANES), f32),
             pltpu.VMEM((slots, width), bf16),
             pltpu.VMEM((width, columns), bf16),
             pltpu.VMEM((slots, columns), f32),
+            pltpu.SemaphoreType.DMA((NX,)),
             pltpu.SemaphoreType.DMA((2,)),
             pltpu.SemaphoreType.DMA((len(ORDER),)),
         ],
@@ -396,7 +405,7 @@
         w_values,
         mib=52,
         flops=2 * slots * width * columns,
-        hbm=(2 + NX, 3 + NX),
+        hbm=tuple(range(2, 4 + NX)),
     )
     rows = 2 * blocks
     merged = call(

time: 184 us -> 175 us (0.951)
  starting transfers between devices: 42.5 us -> 34.3 us
  blocking collectives: 56.7 us -> 62.5 us
  Pallas kernels: 38.7 us -> 33.1 us
  local copies, waits for them, and re-layouts: 5.64 us -> 0.95 us
  waiting for transfers between devices: 25.7 us -> 29 us
    ppermute x1, starting transfers between devices: 11.5 us -> 3.79 us  [body(): other = lax.ppermute(part, 'tp', [(0, 1), (1, 0)])]
    all_to_all x4, blocking collectives: 56.7 us -> 62.5 us  [exchange(): return lax.all_to_all(a, PSG, split_axis=0, concat_axis=0, tiled=True)]
    unnamed x30 -> x10, local copies, waits for them, and re-layouts: 5.62 us -> 0.23 us
    pallas_call x9, Pallas kernels: 3.98 us -> 0.32 us  [pack(): pl.pallas_call(functools.partial(pack_kernel, cuts), out_shape=shaped((su...]
    all_gather x1, waiting for transfers between devices: 0.02 us -> 3.59 us  [body(): w_values = lax.all_gather(w_value, PSG, axis=0, tiled=True)]
    pallas_call x3 -> x4, Pallas kernels: 8.75 us -> 7.14 us  [project(): pl.pallas_call(functools.partial(project_kernel, [len(pieces) for pieces...]
  transfers between devices with their start and end apart: 21 -> 21, of which waited for: 10 -> 11; matrix products, arithmetic and copies ran while one was open for 0% -> 1% of each run, Pallas kernels for 12% -> 10%
where the time goes in v6:
time: 175 us
  blocking collectives  62.5 us (36%)
  starting transfers between devices  34.3 us (20%)
  Pallas kernels  33.1 us (19%)
  waiting for transfers between devices  29 us (17%)
  between operations  14.3 us (8%)
    all_to_all x4, blocking collectives, exchange(): return lax.all_to_all(a, PSG, split_axis=0, concat_axis=0, tiled=True)  62.5 us
    ppermute x19, starting transfers between devices, recv(): return lax.ppermute(a, axis, [((i + k) % n, i) for i in range(n)])  30.5 us
    ppermute x19, waiting for transfers between devices, recv(): return lax.ppermute(a, axis, [((i + k) % n, i) for i in range(n)])  23.9 us
    pallas_call x6, Pallas kernels, call(): pl.pallas_call(kernel, out_shape=outs, in_specs=specs, out_specs=jax.tree...  17.8 us
    pallas_call x1, Pallas kernels, normalise(): pl.pallas_call(norm_kernel, out_shape=shaped((rows, width), bf16), grid_s...  7.9 us
    pallas_call x4, Pallas kernels, project(): pl.pallas_call(functools.partial(project_kernel, [len(pieces) for pieces...  7.14 us
    ppermute x1, starting transfers between devices, body(): other = lax.ppermute(part, 'tp', [(0, 1), (1, 0)])  3.79 us
    all_gather x1, waiting for transfers between devices, body(): w_values = lax.all_gather(w_value, PSG, axis=0, tiled=True)  3.59 us
  transfers between devices with their start and end apart: 21, of which 11 were waited for; matrix products, arithmetic and copies ran while one was open for 1% of the time, Pallas kernels for 10%

profile of v6, /device:TPU:1, one launch (start us, length us, event | category | flops | bytes accessed | tf_op | source)
XLA Modules:
  0.0 174.9 jit_solution(5892998593590299249)
XLA Ops:
  8.1 3.6 %collective-permute-start = (bf16[128,256]{1,0:T(8,128)(2,1)S(1)}, bf16[128,256]{1,0:T(8,128)(2,1)S(1)}, u32[]{:S(2)}, u32[]{:S(2)}) collective-permute-start(bf16[128,256]{1,0:T(8,128)(2,1)S(1)} %constant_dynamic-slice_fusion.refs_0_), channel_id=1, source_target_pairs={{16,0},{32,16},{48,32},{0,48},{17,1},{33,17},{49,33},{1,49},{18,2}... | collective-permute-start | bytes 196616 | tf_op jit(solution)/shard_map/ppermute | solution.py:51
  13.1 3.4 %collective-permute-done.1.refs_2_ = bf16[128,256]{1,0:T(8,128)(2,1)S(1)} collective-permute-done((bf16[128,256]{1,0:T(8,128)(2,1)S(1)}, bf16[128,256]{1,0:T(8,128)(2,1)S(1)}, u32[]{:S(2)}, u32[]{:S(2)}) %collective-permute-start.1) | collective-permute-done | bytes 65568 | tf_op jit(solution)/shard_map/ppermute | solution.py:51
  17.1 5.7 %collective-permute-start.3 = (bf16[512,256]{1,0:T(8,128)(2,1)S(1)}, bf16[512,256]{1,0:T(8,128)(2,1)S(1)}, u32[]{:S(2)}, u32[]{:S(2)}) collective-permute-start(bf16[512,256]{1,0:T(8,128)(2,1)S(1)} %shard_map.98.refs_0_), channel_id=1, source_target_pairs={{2,0},{4,2},{6,4},{8,6},{10,8},{12,10},{14,12},{0,14},{3,1},{5,3},... | collective-permute-start | bytes 786440 | tf_op jit(solution)/shard_map/ppermute | solution.py:51
  24.2 7.9 %shard_map.97.refs_3_.x_ref.refs_4_ = bf16[768,4096]{1,0:T(8,128)(2,1)S(1)} custom-call(s32[6]{0:T(128)S(1)} %pad_add_fusion.pos, bf16[768,4096]{1,0:T(8,128)(2,1)} %bitcast.8, bf16[1,4096]{1,0:T(2,128)(2,1)S(1)} %broadcast_in_dim.6.after_ref.gain_ref), custom_call_target="tpu_custom_call" | custom-call | flops 18874368 | bytes 12582912 | tf_op jit(solution)/shard_map/pallas_call | solution.py:130
  32.2 2.6 %collective-permute-start.11 = (bf16[1536,256]{1,0:T(8,128)(2,1)S(1)}, bf16[1536,256]{1,0:T(8,128)(2,1)S(1)}, u32[]{:S(2)}, u32[]{:S(2)}) collective-permute-start(bf16[1536,256]{1,0:T(8,128)(2,1)S(1)} %shard_map.99.refs_0_), channel_id=1, source_target_pairs={{64,0},{128,64},{192,128},{0,192},{65,1},{129,65},{193,129},{1,193... | collective-permute-start | bytes 2359304 | tf_op jit(solution)/shard_map/ppermute | solution.py:51
  34.8 2.7 %collective-permute-start.5 = (bf16[512,256]{1,0:T(8,128)(2,1)S(1)}, bf16[512,256]{1,0:T(8,128)(2,1)S(1)}, u32[]{:S(2)}, u32[]{:S(2)}) collective-permute-start(bf16[512,256]{1,0:T(8,128)(2,1)S(1)} %collective-permute-done.3.refs_1_), channel_id=1, source_target_pairs={{2,0},{4,2},{6,4},{8,6},{10,8},{12,10},{14,12},{0,14},{3,1},{5,3},... | collective-permute-start | bytes 786440 | tf_op jit(solution)/shard_map/ppermute | solution.py:51
  37.6 8.1 %collective-permute-done.6.refs_1_ = bf16[512,256]{1,0:T(8,128)(2,1)S(1)} collective-permute-done((bf16[512,256]{1,0:T(8,128)(2,1)S(1)}, bf16[512,256]{1,0:T(8,128)(2,1)S(1)}, u32[]{:S(2)}, u32[]{:S(2)}) %collective-permute-start.6) | collective-permute-done | bytes 262176 | tf_op jit(solution)/shard_map/ppermute | solution.py:51
  45.6 2.7 %collective-permute-start.7 = (bf16[512,256]{1,0:T(8,128)(2,1)S(1)}, bf16[512,256]{1,0:T(8,128)(2,1)S(1)}, u32[]{:S(2)}, u32[]{:S(2)}) collective-permute-start(bf16[512,256]{1,0:T(8,128)(2,1)S(1)} %collective-permute-done.5.refs_0_), channel_id=1, source_target_pairs={{2,0},{4,2},{6,4},{8,6},{10,8},{12,10},{14,12},{0,14},{3,1},{5,3},... | collective-permute-start | bytes 786440 | tf_op jit(solution)/shard_map/ppermute | solution.py:51
  48.3 1.0 collective-permute-done.11.refs_0_
  49.3 3.5 %collective-permute-start.12 = (bf16[768,256]{1,0:T(8,128)(2,1)S(1)}, bf16[768,256]{1,0:T(8,128)(2,1)S(1)}, u32[]{:S(2)}, u32[]{:S(2)}) collective-permute-start(bf16[768,256]{1,0:T(8,128)(2,1)S(1)} %shard_map.102), channel_id=1, source_target_pairs={{64,0},{128,64},{192,128},{0,192},{65,1},{129,65},{193,129},{1,193... | collective-permute-start | bytes 1179656 | tf_op jit(solution)/shard_map/ppermute | solution.py:51
  53.0 2.4 %collective-permute-done.8.refs_0_.refs_3_ = bf16[512,256]{1,0:T(8,128)(2,1)S(1)} collective-permute-done((bf16[512,256]{1,0:T(8,128)(2,1)S(1)}, bf16[512,256]{1,0:T(8,128)(2,1)S(1)}, u32[]{:S(2)}, u32[]{:S(2)}) %collective-permute-start.8) | collective-permute-done | bytes 262176 | tf_op jit(solution)/shard_map/ppermute | solution.py:51
  55.5 2.9 %collective-permute-start.9 = (bf16[256,256]{1,0:T(8,128)(2,1)S(1)}, bf16[256,256]{1,0:T(8,128)(2,1)S(1)}, u32[]{:S(2)}, u32[]{:S(2)}) collective-permute-start(bf16[256,256]{1,0:T(8,128)(2,1)S(1)} %shard_map.100), channel_id=1, source_target_pairs={{2,0},{4,2},{6,4},{8,6},{10,8},{12,10},{14,12},{0,14},{3,1},{5,3},... | collective-permute-start | bytes 393224 | tf_op jit(solution)/shard_map/ppermute | solution.py:51
  58.4 2.1 %collective-permute-done.10.refs_5_ = bf16[256,256]{1,0:T(8,128)(2,1)S(1)} collective-permute-done((bf16[256,256]{1,0:T(8,128)(2,1)S(1)}, bf16[256,256]{1,0:T(8,128)(2,1)S(1)}, u32[]{:S(2)}, u32[]{:S(2)}) %collective-permute-start.10) | collective-permute-done | bytes 131104 | tf_op jit(solution)/shard_map/ppermute | solution.py:51
  60.5 0.8 collective-permute-done.14.refs_7_.refs_1_
  61.4 2.7 %collective-permute-start.15 = (bf16[2560,256]{1,0:T(8,128)(2,1)S(1)}, bf16[2560,256]{1,0:T(8,128)(2,1)S(1)}, u32[]{:S(2)}, u32[]{:S(2)}) collective-permute-start(bf16[2560,256]{1,0:T(8,128)(2,1)S(1)} %shard_map.104.refs_1_), channel_id=1, source_target_pairs={{64,0},{128,64},{192,128},{0,192},{65,1},{129,65},{193,129},{1,193... | collective-permute-start | bytes 3932168 | tf_op jit(solution)/shard_map/ppermute | solution.py:51
  64.8 15.9 %all_to_all.20.got_ref = f32[32,8,128]{2,1,0:T(8,128)S(1)} all-to-all(f32[32,8,128]{2,1,0:T(8,128)S(1)} %shard_map.95), channel_id=1, replica_groups=mesh['dp'=4,'y'=4,'z'=8,'tp'=2] {'y','z'}, dimensions={0} | all-to-all | bytes 262144 | tf_op jit(solution)/shard_map/all_to_all | solution.py:55
  81.3 1.8 %shard_map.105.refs_1_.refs_0_ = bf16[768,256]{1,0:T(8,128)(2,1)S(1)} custom-call(bf16[768,4096]{1,0:T(8,128)(2,1)S(1)} %shard_map.97.refs_3_.x_ref.refs_4_, bf16[1536,256]{1,0:T(8,128)(2,1)S(1)} %shard_map.99.refs_0_, bf16[2560,256]{1,0:T(8,128)(2,1)S(1)} %shard_map.104.refs_1_, f32[32,8,128]{2,1,0:T(8,128)S(1)} %shard_map.96.refs_2_), custom_call_target="tpu_custom_call" | custom-call | flops 1610612736 | bytes 8781824 | tf_op jit(solution)/shard_map/pallas_call | solution.py:167
  83.1 5.4 %collective-permute-done.17.refs_0_.refs_1_ = bf16[2560,256]{1,0:T(8,128)(2,1)S(1)} collective-permute-done((bf16[2560,256]{1,0:T(8,128)(2,1)S(1)}, bf16[2560,256]{1,0:T(8,128)(2,1)S(1)}, u32[]{:S(2)}, u32[]{:S(2)}) %collective-permute-start.17) | collective-permute-done | bytes 1310752 | tf_op jit(solution)/shard_map/ppermute | solution.py:51
  88.7 2.7 %collective-permute-start.16 = (bf16[1280,256]{1,0:T(8,128)(2,1)S(1)}, bf16[1280,256]{1,0:T(8,128)(2,1)S(1)}, u32[]{:S(2)}, u32[]{:S(2)}) collective-permute-start(bf16[1280,256]{1,0:T(8,128)(2,1)S(1)} %shard_map.107), channel_id=1, source_target_pairs={{64,0},{128,64},{192,128},{0,192},{65,1},{129,65},{193,129},{1,193... | collective-permute-start | bytes 1966088 | tf_op jit(solution)/shard_map/ppermute | solution.py:51
  91.4 16.8 %all_to_all.21.refs_2_.q_ref = f32[32,8,128]{2,1,0:T(8,128)S(1)} all-to-all(f32[32,8,128]{2,1,0:T(8,128)S(1)} %shard_map.96.refs_2_), channel_id=1, replica_groups=mesh['dp'=4,'y'=4,'z'=8,'tp'=2] {'y','z'}, dimensions={0} | all-to-all | bytes 262144 | tf_op jit(solution)/shard_map/all_to_all | solution.py:55
  108.3 1.8 %shard_map.110.refs_3_ = bf16[768,256]{1,0:T(8,128)(2,1)S(1)} custom-call(bf16[768,4096]{1,0:T(8,128)(2,1)S(1)} %shard_map.97.refs_3_.x_ref.refs_4_, bf16[1536,256]{1,0:T(8,128)(2,1)S(1)} %collective-permute-done.13.refs_0_, bf16[2560,256]{1,0:T(8,128)(2,1)S(1)} %collective-permute-done.17.refs_0_.refs_1_, f32[32,8,128]{2,1,0:T(8,128)S(1)} %all_to_all.21.refs_2_.q_ref), custom_call_target="tpu_custom_call" | custom-call | flops 1610612736 | bytes 8781824 | tf_op jit(solution)/shard_map/pallas_call | solution.py:167
  110.0 1.8 %shard_map.106.refs_1_ = bf16[768,256]{1,0:T(8,128)(2,1)S(1)} custom-call(bf16[768,4096]{1,0:T(8,128)(2,1)S(1)} %shard_map.97.refs_3_.x_ref.refs_4_, bf16[1536,256]{1,0:T(8,128)(2,1)S(1)} %collective-permute-done.11.refs_0_, bf16[2560,256]{1,0:T(8,128)(2,1)S(1)} %collective-permute-done.15.refs_1_.refs_0_, f32[32,8,128]{2,1,0:T(8,128)S(1)} %all_to_all.21.refs_2_.q_ref), custom_call_target="tpu_custom_call" | custom-call | flops 1610612736 | bytes 8781824 | tf_op jit(solution)/shard_map/pallas_call | solution.py:167
  111.9 1.8 %shard_map.109.refs_2_ = bf16[768,256]{1,0:T(8,128)(2,1)S(1)} custom-call(bf16[768,4096]{1,0:T(8,128)(2,1)S(1)} %shard_map.97.refs_3_.x_ref.refs_4_, bf16[768,256]{1,0:T(8,128)(2,1)S(1)} %collective-permute-done.12.refs_6_.refs_0_, bf16[768,256]{1,0:T(8,128)(2,1)S(1)} %collective-permute-done.14.refs_7_.refs_1_, ...), custom_call_target="tpu_custom_call" | custom-call | flops 1610612736 | bytes 8781824 | tf_op jit(solution)/shard_map/pallas_call | solution.py:167
  113.7 3.6 %all-gather.2.cloned.1.call-done.refs_5_ = bf16[4096,1024]{1,0:T(8,128)(2,1)} async-done(((bf16[128,1024]{1,0:T(8,128)(2,1)}), bf16[4096,1024]{1,0:T(8,128)(2,1)}) %all-gather.2.cloned.1.call-update) | async-done | bytes 8388624 | tf_op jit(solution)/shard_map/all_gather | solution.py:366
  117.3 13.6 %shard_map.111 = f32[32,9,128]{2,1,0:T(8,128)S(1)} custom-call(s32[6]{0:T(128)S(1)} %pad_add_fusion.pos, f32[32,8,128]{2,1,0:T(8,128)S(1)} %all_to_all.21.refs_2_.q_ref, bf16[768,256]{1,0:T(8,128)(2,1)S(1)} %shard_map.105.refs_1_.refs_0_, bf16[768,256]{1,0:T(8,128)(2,1)S(1)} %shard_map.106.refs_1_, bf16[768,256]{1,0:T(8,128)(2,1)S(1)} %shard_map.109.refs_2_, ...), custom_call_target="tpu_custom_call" | custom-call | flops 6442450944 | bytes 1048576 | tf_op jit(solution)/shard_map/pallas_call | solution.py:38
  130.9 15.1 %all_to_all.22.got_ref = f32[32,9,128]{2,1,0:T(8,128)S(1)} all-to-all(f32[32,9,128]{2,1,0:T(8,128)S(1)} %shard_map.111), channel_id=1, replica_groups=mesh['dp'=4,'y'=4,'z'=8,'tp'=2] {'y','z'}, dimensions={0} | all-to-all | bytes 294912 | tf_op jit(solution)/shard_map/all_to_all | solution.py:55
  146.0 0.9 shard_map.112
  146.9 14.6 %all_to_all.23.ctx_ref = bf16[32,16,128]{2,1,0:T(8,128)(2,1)S(1)} all-to-all(bf16[32,16,128]{2,1,0:T(8,128)(2,1)S(1)} %shard_map.112), channel_id=1, replica_groups=mesh['dp'=4,'y'=4,'z'=8,'tp'=2] {'y','z'}, dimensions={0} | all-to-all | bytes 262144 | tf_op jit(solution)/shard_map/all_to_all | solution.py:55
  161.6 0.7 shard_map.113.own_ref
  162.3 3.8 %collective-permute-start.19 = (f32[40,128]{1,0:T(8,128)S(1)}, f32[40,128]{1,0:T(8,128)S(1)}, u32[]{:S(2)}, u32[]{:S(2)}) collective-permute-start(f32[40,128]{1,0:T(8,128)S(1)} %shard_map.113.own_ref), channel_id=1, source_target_pairs={{0,1},{1,0},{2,3},{3,2},{4,5},{5,4},{6,7},{7,6},{8,9},{9,8},{10,11... | collective-permute-start | bytes 61448 | tf_op jit(solution)/shard_map/ppermute | solution.py:426
  166.1 0.8 collective-permute-done.19.other_ref
  167.0 1.1 shard_map.114
  (48 shorter events, 6.4 us)
Async XLA Ops:
  7.2 1.0 copy-start
  7.2 110.1 %all-gather.2.cloned.1.call-start = ((), (), s32[]{:S(2)}) async-start(), calls=%async_computation.4 | async-start | bytes 8650752 | tf_op jit(solution)/shard_map/all_gather | solution.py:366
  8.1 5.0 %collective-permute-start = (bf16[128,256]{1,0:T(8,128)(2,1)S(1)}, bf16[128,256]{1,0:T(8,128)(2,1)S(1)}, u32[]{:S(2)}, u32[]{:S(2)}) collective-permute-start(bf16[128,256]{1,0:T(8,128)(2,1)S(1)} %constant_dynamic-slice_fusion.refs_0_), channel_id=1, source_target_pairs={{16,0},{32,16},{48,32},{0,48},{17,1},{33,17},{49,33},{1,49},{18,2}... | collective-permute-start | bytes 196616 | tf_op jit(solution)/shard_map/ppermute | solution.py:51
  11.8 4.7 %collective-permute-start.1 = (bf16[128,256]{1,0:T(8,128)(2,1)S(1)}, bf16[128,256]{1,0:T(8,128)(2,1)S(1)}, u32[]{:S(2)}, u32[]{:S(2)}) collective-permute-start(bf16[128,256]{1,0:T(8,128)(2,1)S(1)} %constant_dynamic-slice_fusion.refs_0_), channel_id=1, source_target_pairs={{32,0},{48,16},{0,32},{16,48},{33,1},{49,17},{1,33},{17,49},{34,2}... | collective-permute-start | bytes 196616 | tf_op jit(solution)/shard_map/ppermute | solution.py:51
  12.1 5.0 %collective-permute-start.2 = (bf16[128,256]{1,0:T(8,128)(2,1)S(1)}, bf16[128,256]{1,0:T(8,128)(2,1)S(1)}, u32[]{:S(2)}, u32[]{:S(2)}) collective-permute-start(bf16[128,256]{1,0:T(8,128)(2,1)S(1)} %constant_dynamic-slice_fusion.refs_0_), channel_id=1, source_target_pairs={{48,0},{0,16},{16,32},{32,48},{49,1},{1,17},{17,33},{33,49},{50,2}... | collective-permute-start | bytes 196616 | tf_op jit(solution)/shard_map/ppermute | solution.py:51
  17.1 15.0 %collective-permute-start.3 = (bf16[512,256]{1,0:T(8,128)(2,1)S(1)}, bf16[512,256]{1,0:T(8,128)(2,1)S(1)}, u32[]{:S(2)}, u32[]{:S(2)}) collective-permute-start(bf16[512,256]{1,0:T(8,128)(2,1)S(1)} %shard_map.98.refs_0_), channel_id=1, source_target_pairs={{2,0},{4,2},{6,4},{8,6},{10,8},{12,10},{14,12},{0,14},{3,1},{5,3},... | collective-permute-start | bytes 786440 | tf_op jit(solution)/shard_map/ppermute | solution.py:51
  22.8 9.4 %collective-permute-start.4 = (bf16[512,256]{1,0:T(8,128)(2,1)S(1)}, bf16[512,256]{1,0:T(8,128)(2,1)S(1)}, u32[]{:S(2)}, u32[]{:S(2)}) collective-permute-start(bf16[512,256]{1,0:T(8,128)(2,1)S(1)} %shard_map.98.refs_0_), channel_id=1, source_target_pairs={{14,0},{0,2},{2,4},{4,6},{6,8},{8,10},{10,12},{12,14},{15,1},{1,3}... | collective-permute-start | bytes 786440 | tf_op jit(solution)/shard_map/ppermute | solution.py:51
  32.1 79.7 %copy-start.1 = (bf16[768,4096]{1,0:T(8,128)(2,1)}, bf16[768,4096]{1,0:T(8,128)(2,1)S(1)}, u32[]{:S(2)}) copy-start(bf16[768,4096]{1,0:T(8,128)(2,1)S(1)} %shard_map.97.refs_3_.x_ref.refs_4_) | copy-start | bytes 18874372
  32.1 31.9 %copy-start.3 = (bf16[1,32,4096]{2,1,0:T(8,128)(2,1)S(1)}, bf16[1,32,4096]{2,1,0:T(8,128)(2,1)}, u32[]{:S(2)}) copy-start(bf16[1,32,4096]{2,1,0:T(8,128)(2,1)} %param.11) | copy-start | bytes 786436
  32.2 31.9 %copy-start.4 = (bf16[128,1024]{1,0:T(8,128)(2,1)S(1)}, bf16[128,1024]{1,0:T(8,128)(2,1)}, u32[]{:S(2)}) copy-start(bf16[128,1024]{1,0:T(8,128)(2,1)} %w_ref.2) | copy-start | bytes 786436
  32.2 17.0 %collective-permute-start.11 = (bf16[1536,256]{1,0:T(8,128)(2,1)S(1)}, bf16[1536,256]{1,0:T(8,128)(2,1)S(1)}, u32[]{:S(2)}, u32[]{:S(2)}) collective-permute-start(bf16[1536,256]{1,0:T(8,128)(2,1)S(1)} %shard_map.99.refs_0_), channel_id=1, source_target_pairs={{64,0},{128,64},{192,128},{0,192},{65,1},{129,65},{193,129},{1,193... | collective-permute-start | bytes 2359304 | tf_op jit(solution)/shard_map/ppermute | solution.py:51
  34.8 18.0 %collective-permute-start.13 = (bf16[1536,256]{1,0:T(8,128)(2,1)S(1)}, bf16[1536,256]{1,0:T(8,128)(2,1)S(1)}, u32[]{:S(2)}, u32[]{:S(2)}) collective-permute-start(bf16[1536,256]{1,0:T(8,128)(2,1)S(1)} %shard_map.99.refs_0_), channel_id=1, source_target_pairs={{192,0},{0,64},{64,128},{128,192},{193,1},{1,65},{65,129},{129,193... | collective-permute-start | bytes 2359304 | tf_op jit(solution)/shard_map/ppermute | solution.py:51
  34.8 10.8 %collective-permute-start.6 = (bf16[512,256]{1,0:T(8,128)(2,1)S(1)}, bf16[512,256]{1,0:T(8,128)(2,1)S(1)}, u32[]{:S(2)}, u32[]{:S(2)}) collective-permute-start(bf16[512,256]{1,0:T(8,128)(2,1)S(1)} %collective-permute-done.4.refs_2_), channel_id=1, source_target_pairs={{14,0},{0,2},{2,4},{4,6},{6,8},{8,10},{10,12},{12,14},{15,1},{1,3}... | collective-permute-start | bytes 786440 | tf_op jit(solution)/shard_map/ppermute | solution.py:51
  34.8 10.8 %collective-permute-start.5 = (bf16[512,256]{1,0:T(8,128)(2,1)S(1)}, bf16[512,256]{1,0:T(8,128)(2,1)S(1)}, u32[]{:S(2)}, u32[]{:S(2)}) collective-permute-start(bf16[512,256]{1,0:T(8,128)(2,1)S(1)} %collective-permute-done.3.refs_1_), channel_id=1, source_target_pairs={{2,0},{4,2},{6,4},{8,6},{10,8},{12,10},{14,12},{0,14},{3,1},{5,3},... | collective-permute-start | bytes 786440 | tf_op jit(solution)/shard_map/ppermute | solution.py:51
  45.6 9.7 %collective-permute-start.8 = (bf16[512,256]{1,0:T(8,128)(2,1)S(1)}, bf16[512,256]{1,0:T(8,128)(2,1)S(1)}, u32[]{:S(2)}, u32[]{:S(2)}) collective-permute-start(bf16[512,256]{1,0:T(8,128)(2,1)S(1)} %collective-permute-done.6.refs_1_), channel_id=1, source_target_pairs={{14,0},{0,2},{2,4},{4,6},{6,8},{8,10},{10,12},{12,14},{15,1},{1,3}... | collective-permute-start | bytes 786440 | tf_op jit(solution)/shard_map/ppermute | solution.py:51
  45.6 9.8 %collective-permute-start.7 = (bf16[512,256]{1,0:T(8,128)(2,1)S(1)}, bf16[512,256]{1,0:T(8,128)(2,1)S(1)}, u32[]{:S(2)}, u32[]{:S(2)}) collective-permute-start(bf16[512,256]{1,0:T(8,128)(2,1)S(1)} %collective-permute-done.5.refs_0_), channel_id=1, source_target_pairs={{2,0},{4,2},{6,4},{8,6},{10,8},{12,10},{14,12},{0,14},{3,1},{5,3},... | collective-permute-start | bytes 786440 | tf_op jit(solution)/shard_map/ppermute | solution.py:51
  49.3 11.1 %collective-permute-start.12 = (bf16[768,256]{1,0:T(8,128)(2,1)S(1)}, bf16[768,256]{1,0:T(8,128)(2,1)S(1)}, u32[]{:S(2)}, u32[]{:S(2)}) collective-permute-start(bf16[768,256]{1,0:T(8,128)(2,1)S(1)} %shard_map.102), channel_id=1, source_target_pairs={{64,0},{128,64},{192,128},{0,192},{65,1},{129,65},{193,129},{1,193... | collective-permute-start | bytes 1179656 | tf_op jit(solution)/shard_map/ppermute | solution.py:51
  52.9 8.3 %collective-permute-start.14 = (bf16[768,256]{1,0:T(8,128)(2,1)S(1)}, bf16[768,256]{1,0:T(8,128)(2,1)S(1)}, u32[]{:S(2)}, u32[]{:S(2)}) collective-permute-start(bf16[768,256]{1,0:T(8,128)(2,1)S(1)} %shard_map.103), channel_id=1, source_target_pairs={{192,0},{0,64},{64,128},{128,192},{193,1},{1,65},{65,129},{129,193... | collective-permute-start | bytes 1179656 | tf_op jit(solution)/shard_map/ppermute | solution.py:51
  55.3 5.1 %collective-permute-start.10 = (bf16[256,256]{1,0:T(8,128)(2,1)S(1)}, bf16[256,256]{1,0:T(8,128)(2,1)S(1)}, u32[]{:S(2)}, u32[]{:S(2)}) collective-permute-start(bf16[256,256]{1,0:T(8,128)(2,1)S(1)} %shard_map.101), channel_id=1, source_target_pairs={{14,0},{0,2},{2,4},{4,6},{6,8},{8,10},{10,12},{12,14},{15,1},{1,3}... | collective-permute-start | bytes 393224 | tf_op jit(solution)/shard_map/ppermute | solution.py:51
  55.5 5.0 %collective-permute-start.9 = (bf16[256,256]{1,0:T(8,128)(2,1)S(1)}, bf16[256,256]{1,0:T(8,128)(2,1)S(1)}, u32[]{:S(2)}, u32[]{:S(2)}) collective-permute-start(bf16[256,256]{1,0:T(8,128)(2,1)S(1)} %shard_map.100), channel_id=1, source_target_pairs={{2,0},{4,2},{6,4},{8,6},{10,8},{12,10},{14,12},{0,14},{3,1},{5,3},... | collective-permute-start | bytes 393224 | tf_op jit(solution)/shard_map/ppermute | solution.py:51
  61.3 27.2 %collective-permute-start.17 = (bf16[2560,256]{1,0:T(8,128)(2,1)S(1)}, bf16[2560,256]{1,0:T(8,128)(2,1)S(1)}, u32[]{:S(2)}, u32[]{:S(2)}) collective-permute-start(bf16[2560,256]{1,0:T(8,128)(2,1)S(1)} %shard_map.104.refs_1_), channel_id=1, source_target_pairs={{192,0},{0,64},{64,128},{128,192},{193,1},{1,65},{65,129},{129,193... | collective-permute-start | bytes 3932168 | tf_op jit(solution)/shard_map/ppermute | solution.py:51
  61.4 27.2 %collective-permute-start.15 = (bf16[2560,256]{1,0:T(8,128)(2,1)S(1)}, bf16[2560,256]{1,0:T(8,128)(2,1)S(1)}, u32[]{:S(2)}, u32[]{:S(2)}) collective-permute-start(bf16[2560,256]{1,0:T(8,128)(2,1)S(1)} %shard_map.104.refs_1_), channel_id=1, source_target_pairs={{64,0},{128,64},{192,128},{0,192},{65,1},{129,65},{193,129},{1,193... | collective-permute-start | bytes 3932168 | tf_op jit(solution)/shard_map/ppermute | solution.py:51
  88.5 23.3 %collective-permute-start.18 = (bf16[1280,256]{1,0:T(8,128)(2,1)S(1)}, bf16[1280,256]{1,0:T(8,128)(2,1)S(1)}, u32[]{:S(2)}, u32[]{:S(2)}) collective-permute-start(bf16[1280,256]{1,0:T(8,128)(2,1)S(1)} %shard_map.108), channel_id=1, source_target_pairs={{192,0},{0,64},{64,128},{128,192},{193,1},{1,65},{65,129},{129,193... | collective-permute-start | bytes 1966088 | tf_op jit(solution)/shard_map/ppermute | solution.py:51
  88.7 23.2 %collective-permute-start.16 = (bf16[1280,256]{1,0:T(8,128)(2,1)S(1)}, bf16[1280,256]{1,0:T(8,128)(2,1)S(1)}, u32[]{:S(2)}, u32[]{:S(2)}) collective-permute-start(bf16[1280,256]{1,0:T(8,128)(2,1)S(1)} %shard_map.107), channel_id=1, source_target_pairs={{64,0},{128,64},{192,128},{0,192},{65,1},{129,65},{193,129},{1,193... | collective-permute-start | bytes 1966088 | tf_op jit(solution)/shard_map/ppermute | solution.py:51
  113.7 47.9 %copy-start.2 = (bf16[1024,128]{1,0:T(8,128)(2,1)S(1)}, bf16[1024,128]{1,0:T(8,128)(2,1)}, u32[]{:S(2)}) copy-start(bf16[1024,128]{1,0:T(8,128)(2,1)} %w_ref.3) | copy-start | bytes 786436
  162.3 4.6 %collective-permute-start.19 = (f32[40,128]{1,0:T(8,128)S(1)}, f32[40,128]{1,0:T(8,128)S(1)}, u32[]{:S(2)}, u32[]{:S(2)}) collective-permute-start(f32[40,128]{1,0:T(8,128)S(1)} %shard_map.113.own_ref), channel_id=1, source_target_pairs={{0,1},{1,0},{2,3},{3,2},{4,5},{5,4},{6,7},{7,6},{8,9},{9,8},{10,11... | collective-permute-start | bytes 61448 | tf_op jit(solution)/shard_map/ppermute | solution.py:426
Sparse Core Ops, SparseCore 0:
  10.6 106.6 all-gather.1

commit v7 on v6

--- a/solution.py
+++ b/solution.py
@@ -13,6 +13,7 @@
 NY = 4
 NZ = 8
 LANES = 128
+PARTS = 4
 PSG = ("y", "z")
 SIZES = {"dp": NX, "y": NY, "z": NZ}
 VMEM = pl.BlockSpec(memory_space=pltpu.VMEM)
@@ -249,7 +250,7 @@
     pairs = high_ref.shape[0] // NX
     cols = buf.shape[1] // NX
     blocks = cols // LANES
-    half = len(ORDER) // 2
+    per = len(ORDER) // PARTS
 
     def fetch(i):
         return pltpu.make_async_copy(
@@ -259,7 +260,7 @@
         )
 
     def fetch_x(part):
-        at = pl.ds(part * half * LANES, half * LANES)
+        at = pl.ds(part * per * LANES, per * LANES)
         return pltpu.make_async_copy(x_hbm.at[:, at], x_buf.at[:, at], x_sems.at[part])
 
     def fetch_key(i):
@@ -267,18 +268,18 @@
 
     for i in range(NX):
         fetch_key(i).start()
-    for part in range(2):
+    for part in range(PARTS):
         fetch_x(part).start()
-        for i in range(part * half, (part + 1) * half):
+        for i in range(part * per, (part + 1) * per):
             fetch(i).start()
     for i in range(NX):
         fetch_key(i).wait()
     softmax(plen, pos, q_ref, [k_buf.at[i] for i in range(NX)], high_ref, low_ref, stat_ref)
-    for part in range(2):
+    for part in range(PARTS):
         fetch_x(part).wait()
-        for i in range(part * half, (part + 1) * half):
+        for i in range(part * per, (part + 1) * per):
             fetch(i).wait()
-        at = slice(part * half * LANES, (part + 1) * half * LANES)
+        at = slice(part * per * LANES, (part + 1) * per * LANES)
         for g in range(NX):
             col = slice(g * cols, (g + 1) * cols)
             v = jnp.dot(x_buf[:, at], buf[at, col], preferred_element_type=f32)
@@ -395,7 +396,7 @@
             pltpu.VMEM((width, columns), bf16),
             pltpu.VMEM((slots, columns), f32),
             pltpu.SemaphoreType.DMA((NX,)),
-            pltpu.SemaphoreType.DMA((2,)),
+            pltpu.SemaphoreType.DMA((PARTS,)),
             pltpu.SemaphoreType.DMA((len(ORDER),)),
         ],
         pos,

time: 175 us -> 175 us (level)
  no operation moved by 1% of the time
where the time goes in v7:
time: 175 us
  blocking collectives  62.5 us (36%)
  starting transfers between devices  34.3 us (20%)
  Pallas kernels  32.9 us (19%)
  waiting for transfers between devices  29 us (17%)
  between operations  14.3 us (8%)
    all_to_all x4, blocking collectives, exchange(): return lax.all_to_all(a, PSG, split_axis=0, concat_axis=0, tiled=True)  62.5 us
    ppermute x19, starting transfers between devices, recv(): return lax.ppermute(a, axis, [((i + k) % n, i) for i in range(n)])  30.5 us
    ppermute x19, waiting for transfers between devices, recv(): return lax.ppermute(a, axis, [((i + k) % n, i) for i in range(n)])  23.9 us
    pallas_call x6, Pallas kernels, call(): pl.pallas_call(kernel, out_shape=outs, in_specs=specs, out_specs=jax.tree...  17.5 us
    pallas_call x1, Pallas kernels, normalise(): pl.pallas_call(norm_kernel, out_shape=shaped((rows, width), bf16), grid_s...  7.9 us
    pallas_call x4, Pallas kernels, project(): pl.pallas_call(functools.partial(project_kernel, [len(pieces) for pieces...  7.14 us
    ppermute x1, starting transfers between devices, body(): other = lax.ppermute(part, 'tp', [(0, 1), (1, 0)])  3.8 us
    all_gather x1, waiting for transfers between devices, body(): w_values = lax.all_gather(w_value, PSG, axis=0, tiled=True)  3.59 us
  transfers between devices with their start and end apart: 21, of which 11 were waited for; matrix products, arithmetic and copies ran while one was open for 1% of the time, Pallas kernels for 10%

profile of v7, /device:TPU:1, one launch (start us, length us, event | category | flops | bytes accessed | tf_op | source)
XLA Modules:
  0.0 174.7 jit_solution(8689401133581292212)
XLA Ops:
  8.1 3.6 %collective-permute-start = (bf16[128,256]{1,0:T(8,128)(2,1)S(1)}, bf16[128,256]{1,0:T(8,128)(2,1)S(1)}, u32[]{:S(2)}, u32[]{:S(2)}) collective-permute-start(bf16[128,256]{1,0:T(8,128)(2,1)S(1)} %constant_dynamic-slice_fusion.refs_0_), channel_id=1, source_target_pairs={{16,0},{32,16},{48,32},{0,48},{17,1},{33,17},{49,33},{1,49},{18,2}... | collective-permute-start | bytes 196616 | tf_op jit(solution)/shard_map/ppermute | solution.py:52
  13.1 3.4 %collective-permute-done.1.refs_2_ = bf16[128,256]{1,0:T(8,128)(2,1)S(1)} collective-permute-done((bf16[128,256]{1,0:T(8,128)(2,1)S(1)}, bf16[128,256]{1,0:T(8,128)(2,1)S(1)}, u32[]{:S(2)}, u32[]{:S(2)}) %collective-permute-start.1) | collective-permute-done | bytes 65568 | tf_op jit(solution)/shard_map/ppermute | solution.py:52
  17.1 5.7 %collective-permute-start.3 = (bf16[512,256]{1,0:T(8,128)(2,1)S(1)}, bf16[512,256]{1,0:T(8,128)(2,1)S(1)}, u32[]{:S(2)}, u32[]{:S(2)}) collective-permute-start(bf16[512,256]{1,0:T(8,128)(2,1)S(1)} %shard_map.98.refs_0_), channel_id=1, source_target_pairs={{2,0},{4,2},{6,4},{8,6},{10,8},{12,10},{14,12},{0,14},{3,1},{5,3},... | collective-permute-start | bytes 786440 | tf_op jit(solution)/shard_map/ppermute | solution.py:52
  24.2 7.9 %shard_map.97.refs_3_.x_ref.refs_4_ = bf16[768,4096]{1,0:T(8,128)(2,1)S(1)} custom-call(s32[6]{0:T(128)S(1)} %pad_add_fusion.pos, bf16[768,4096]{1,0:T(8,128)(2,1)} %bitcast.8, bf16[1,4096]{1,0:T(2,128)(2,1)S(1)} %broadcast_in_dim.6.after_ref.gain_ref), custom_call_target="tpu_custom_call" | custom-call | flops 18874368 | bytes 12582912 | tf_op jit(solution)/shard_map/pallas_call | solution.py:131
  32.2 2.6 %collective-permute-start.11 = (bf16[1536,256]{1,0:T(8,128)(2,1)S(1)}, bf16[1536,256]{1,0:T(8,128)(2,1)S(1)}, u32[]{:S(2)}, u32[]{:S(2)}) collective-permute-start(bf16[1536,256]{1,0:T(8,128)(2,1)S(1)} %shard_map.99.refs_0_), channel_id=1, source_target_pairs={{64,0},{128,64},{192,128},{0,192},{65,1},{129,65},{193,129},{1,193... | collective-permute-start | bytes 2359304 | tf_op jit(solution)/shard_map/ppermute | solution.py:52
  34.8 2.7 %collective-permute-start.5 = (bf16[512,256]{1,0:T(8,128)(2,1)S(1)}, bf16[512,256]{1,0:T(8,128)(2,1)S(1)}, u32[]{:S(2)}, u32[]{:S(2)}) collective-permute-start(bf16[512,256]{1,0:T(8,128)(2,1)S(1)} %collective-permute-done.3.refs_1_), channel_id=1, source_target_pairs={{2,0},{4,2},{6,4},{8,6},{10,8},{12,10},{14,12},{0,14},{3,1},{5,3},... | collective-permute-start | bytes 786440 | tf_op jit(solution)/shard_map/ppermute | solution.py:52
  37.6 8.1 %collective-permute-done.6.refs_1_ = bf16[512,256]{1,0:T(8,128)(2,1)S(1)} collective-permute-done((bf16[512,256]{1,0:T(8,128)(2,1)S(1)}, bf16[512,256]{1,0:T(8,128)(2,1)S(1)}, u32[]{:S(2)}, u32[]{:S(2)}) %collective-permute-start.6) | collective-permute-done | bytes 262176 | tf_op jit(solution)/shard_map/ppermute | solution.py:52
  45.6 2.7 %collective-permute-start.7 = (bf16[512,256]{1,0:T(8,128)(2,1)S(1)}, bf16[512,256]{1,0:T(8,128)(2,1)S(1)}, u32[]{:S(2)}, u32[]{:S(2)}) collective-permute-start(bf16[512,256]{1,0:T(8,128)(2,1)S(1)} %collective-permute-done.5.refs_0_), channel_id=1, source_target_pairs={{2,0},{4,2},{6,4},{8,6},{10,8},{12,10},{14,12},{0,14},{3,1},{5,3},... | collective-permute-start | bytes 786440 | tf_op jit(solution)/shard_map/ppermute | solution.py:52
  48.3 1.0 collective-permute-done.11.refs_0_
  49.3 3.5 %collective-permute-start.12 = (bf16[768,256]{1,0:T(8,128)(2,1)S(1)}, bf16[768,256]{1,0:T(8,128)(2,1)S(1)}, u32[]{:S(2)}, u32[]{:S(2)}) collective-permute-start(bf16[768,256]{1,0:T(8,128)(2,1)S(1)} %shard_map.102), channel_id=1, source_target_pairs={{64,0},{128,64},{192,128},{0,192},{65,1},{129,65},{193,129},{1,193... | collective-permute-start | bytes 1179656 | tf_op jit(solution)/shard_map/ppermute | solution.py:52
  53.0 2.4 %collective-permute-done.8.refs_0_.refs_3_ = bf16[512,256]{1,0:T(8,128)(2,1)S(1)} collective-permute-done((bf16[512,256]{1,0:T(8,128)(2,1)S(1)}, bf16[512,256]{1,0:T(8,128)(2,1)S(1)}, u32[]{:S(2)}, u32[]{:S(2)}) %collective-permute-start.8) | collective-permute-done | bytes 262176 | tf_op jit(solution)/shard_map/ppermute | solution.py:52
  55.5 2.9 %collective-permute-start.9 = (bf16[256,256]{1,0:T(8,128)(2,1)S(1)}, bf16[256,256]{1,0:T(8,128)(2,1)S(1)}, u32[]{:S(2)}, u32[]{:S(2)}) collective-permute-start(bf16[256,256]{1,0:T(8,128)(2,1)S(1)} %shard_map.100), channel_id=1, source_target_pairs={{2,0},{4,2},{6,4},{8,6},{10,8},{12,10},{14,12},{0,14},{3,1},{5,3},... | collective-permute-start | bytes 393224 | tf_op jit(solution)/shard_map/ppermute | solution.py:52
  58.4 2.1 %collective-permute-done.10.refs_5_ = bf16[256,256]{1,0:T(8,128)(2,1)S(1)} collective-permute-done((bf16[256,256]{1,0:T(8,128)(2,1)S(1)}, bf16[256,256]{1,0:T(8,128)(2,1)S(1)}, u32[]{:S(2)}, u32[]{:S(2)}) %collective-permute-start.10) | collective-permute-done | bytes 131104 | tf_op jit(solution)/shard_map/ppermute | solution.py:52
  60.5 0.8 collective-permute-done.14.refs_7_.refs_1_
  61.4 2.7 %collective-permute-start.15 = (bf16[2560,256]{1,0:T(8,128)(2,1)S(1)}, bf16[2560,256]{1,0:T(8,128)(2,1)S(1)}, u32[]{:S(2)}, u32[]{:S(2)}) collective-permute-start(bf16[2560,256]{1,0:T(8,128)(2,1)S(1)} %shard_map.104.refs_1_), channel_id=1, source_target_pairs={{64,0},{128,64},{192,128},{0,192},{65,1},{129,65},{193,129},{1,193... | collective-permute-start | bytes 3932168 | tf_op jit(solution)/shard_map/ppermute | solution.py:52
  64.8 15.9 %all_to_all.20.got_ref = f32[32,8,128]{2,1,0:T(8,128)S(1)} all-to-all(f32[32,8,128]{2,1,0:T(8,128)S(1)} %shard_map.95), channel_id=1, replica_groups=mesh['dp'=4,'y'=4,'z'=8,'tp'=2] {'y','z'}, dimensions={0} | all-to-all | bytes 262144 | tf_op jit(solution)/shard_map/all_to_all | solution.py:56
  81.3 1.8 %shard_map.105.refs_1_.refs_0_ = bf16[768,256]{1,0:T(8,128)(2,1)S(1)} custom-call(bf16[768,4096]{1,0:T(8,128)(2,1)S(1)} %shard_map.97.refs_3_.x_ref.refs_4_, bf16[1536,256]{1,0:T(8,128)(2,1)S(1)} %shard_map.99.refs_0_, bf16[2560,256]{1,0:T(8,128)(2,1)S(1)} %shard_map.104.refs_1_, f32[32,8,128]{2,1,0:T(8,128)S(1)} %shard_map.96.refs_2_), custom_call_target="tpu_custom_call" | custom-call | flops 1610612736 | bytes 8781824 | tf_op jit(solution)/shard_map/pallas_call | solution.py:168
  83.1 5.4 %collective-permute-done.17.refs_0_.refs_1_ = bf16[2560,256]{1,0:T(8,128)(2,1)S(1)} collective-permute-done((bf16[2560,256]{1,0:T(8,128)(2,1)S(1)}, bf16[2560,256]{1,0:T(8,128)(2,1)S(1)}, u32[]{:S(2)}, u32[]{:S(2)}) %collective-permute-start.17) | collective-permute-done | bytes 1310752 | tf_op jit(solution)/shard_map/ppermute | solution.py:52
  88.7 2.7 %collective-permute-start.16 = (bf16[1280,256]{1,0:T(8,128)(2,1)S(1)}, bf16[1280,256]{1,0:T(8,128)(2,1)S(1)}, u32[]{:S(2)}, u32[]{:S(2)}) collective-permute-start(bf16[1280,256]{1,0:T(8,128)(2,1)S(1)} %shard_map.107), channel_id=1, source_target_pairs={{64,0},{128,64},{192,128},{0,192},{65,1},{129,65},{193,129},{1,193... | collective-permute-start | bytes 1966088 | tf_op jit(solution)/shard_map/ppermute | solution.py:52
  91.4 16.8 %all_to_all.21.refs_2_.q_ref = f32[32,8,128]{2,1,0:T(8,128)S(1)} all-to-all(f32[32,8,128]{2,1,0:T(8,128)S(1)} %shard_map.96.refs_2_), channel_id=1, replica_groups=mesh['dp'=4,'y'=4,'z'=8,'tp'=2] {'y','z'}, dimensions={0} | all-to-all | bytes 262144 | tf_op jit(solution)/shard_map/all_to_all | solution.py:56
  108.3 1.8 %shard_map.110.refs_3_ = bf16[768,256]{1,0:T(8,128)(2,1)S(1)} custom-call(bf16[768,4096]{1,0:T(8,128)(2,1)S(1)} %shard_map.97.refs_3_.x_ref.refs_4_, bf16[1536,256]{1,0:T(8,128)(2,1)S(1)} %collective-permute-done.13.refs_0_, bf16[2560,256]{1,0:T(8,128)(2,1)S(1)} %collective-permute-done.17.refs_0_.refs_1_, f32[32,8,128]{2,1,0:T(8,128)S(1)} %all_to_all.21.refs_2_.q_ref), custom_call_target="tpu_custom_call" | custom-call | flops 1610612736 | bytes 8781824 | tf_op jit(solution)/shard_map/pallas_call | solution.py:168
  110.0 1.8 %shard_map.106.refs_1_ = bf16[768,256]{1,0:T(8,128)(2,1)S(1)} custom-call(bf16[768,4096]{1,0:T(8,128)(2,1)S(1)} %shard_map.97.refs_3_.x_ref.refs_4_, bf16[1536,256]{1,0:T(8,128)(2,1)S(1)} %collective-permute-done.11.refs_0_, bf16[2560,256]{1,0:T(8,128)(2,1)S(1)} %collective-permute-done.15.refs_1_.refs_0_, f32[32,8,128]{2,1,0:T(8,128)S(1)} %all_to_all.21.refs_2_.q_ref), custom_call_target="tpu_custom_call" | custom-call | flops 1610612736 | bytes 8781824 | tf_op jit(solution)/shard_map/pallas_call | solution.py:168
  111.9 1.8 %shard_map.109.refs_2_ = bf16[768,256]{1,0:T(8,128)(2,1)S(1)} custom-call(bf16[768,4096]{1,0:T(8,128)(2,1)S(1)} %shard_map.97.refs_3_.x_ref.refs_4_, bf16[768,256]{1,0:T(8,128)(2,1)S(1)} %collective-permute-done.12.refs_6_.refs_0_, bf16[768,256]{1,0:T(8,128)(2,1)S(1)} %collective-permute-done.14.refs_7_.refs_1_, ...), custom_call_target="tpu_custom_call" | custom-call | flops 1610612736 | bytes 8781824 | tf_op jit(solution)/shard_map/pallas_call | solution.py:168
  113.7 3.6 %all-gather.2.cloned.1.call-done.refs_5_ = bf16[4096,1024]{1,0:T(8,128)(2,1)} async-done(((bf16[128,1024]{1,0:T(8,128)(2,1)}), bf16[4096,1024]{1,0:T(8,128)(2,1)}) %all-gather.2.cloned.1.call-update) | async-done | bytes 8388624 | tf_op jit(solution)/shard_map/all_gather | solution.py:367
  117.3 13.4 %shard_map.111 = f32[32,9,128]{2,1,0:T(8,128)S(1)} custom-call(s32[6]{0:T(128)S(1)} %pad_add_fusion.pos, f32[32,8,128]{2,1,0:T(8,128)S(1)} %all_to_all.21.refs_2_.q_ref, bf16[768,256]{1,0:T(8,128)(2,1)S(1)} %shard_map.105.refs_1_.refs_0_, bf16[768,256]{1,0:T(8,128)(2,1)S(1)} %shard_map.106.refs_1_, bf16[768,256]{1,0:T(8,128)(2,1)S(1)} %shard_map.109.refs_2_, ...), custom_call_target="tpu_custom_call" | custom-call | flops 6442450944 | bytes 1048576 | tf_op jit(solution)/shard_map/pallas_call | solution.py:39
  130.6 15.1 %all_to_all.22.got_ref = f32[32,9,128]{2,1,0:T(8,128)S(1)} all-to-all(f32[32,9,128]{2,1,0:T(8,128)S(1)} %shard_map.111), channel_id=1, replica_groups=mesh['dp'=4,'y'=4,'z'=8,'tp'=2] {'y','z'}, dimensions={0} | all-to-all | bytes 294912 | tf_op jit(solution)/shard_map/all_to_all | solution.py:56
  145.7 0.9 shard_map.112
  146.6 14.6 %all_to_all.23.ctx_ref = bf16[32,16,128]{2,1,0:T(8,128)(2,1)S(1)} all-to-all(bf16[32,16,128]{2,1,0:T(8,128)(2,1)S(1)} %shard_map.112), channel_id=1, replica_groups=mesh['dp'=4,'y'=4,'z'=8,'tp'=2] {'y','z'}, dimensions={0} | all-to-all | bytes 262144 | tf_op jit(solution)/shard_map/all_to_all | solution.py:56
  161.3 0.7 shard_map.113.own_ref
  162.0 3.8 %collective-permute-start.19 = (f32[40,128]{1,0:T(8,128)S(1)}, f32[40,128]{1,0:T(8,128)S(1)}, u32[]{:S(2)}, u32[]{:S(2)}) collective-permute-start(f32[40,128]{1,0:T(8,128)S(1)} %shard_map.113.own_ref), channel_id=1, source_target_pairs={{0,1},{1,0},{2,3},{3,2},{4,5},{5,4},{6,7},{7,6},{8,9},{9,8},{10,11... | collective-permute-start | bytes 61448 | tf_op jit(solution)/shard_map/ppermute | solution.py:427
  165.8 0.8 collective-permute-done.19.other_ref
  166.7 1.1 shard_map.114
  (48 shorter events, 6.4 us)
Async XLA Ops:
  7.2 1.0 copy-start
  7.2 110.1 %all-gather.2.cloned.1.call-start = ((), (), s32[]{:S(2)}) async-start(), calls=%async_computation.4 | async-start | bytes 8650752 | tf_op jit(solution)/shard_map/all_gather | solution.py:367
  8.1 5.0 %collective-permute-start = (bf16[128,256]{1,0:T(8,128)(2,1)S(1)}, bf16[128,256]{1,0:T(8,128)(2,1)S(1)}, u32[]{:S(2)}, u32[]{:S(2)}) collective-permute-start(bf16[128,256]{1,0:T(8,128)(2,1)S(1)} %constant_dynamic-slice_fusion.refs_0_), channel_id=1, source_target_pairs={{16,0},{32,16},{48,32},{0,48},{17,1},{33,17},{49,33},{1,49},{18,2}... | collective-permute-start | bytes 196616 | tf_op jit(solution)/shard_map/ppermute | solution.py:52
  11.8 4.7 %collective-permute-start.1 = (bf16[128,256]{1,0:T(8,128)(2,1)S(1)}, bf16[128,256]{1,0:T(8,128)(2,1)S(1)}, u32[]{:S(2)}, u32[]{:S(2)}) collective-permute-start(bf16[128,256]{1,0:T(8,128)(2,1)S(1)} %constant_dynamic-slice_fusion.refs_0_), channel_id=1, source_target_pairs={{32,0},{48,16},{0,32},{16,48},{33,1},{49,17},{1,33},{17,49},{34,2}... | collective-permute-start | bytes 196616 | tf_op jit(solution)/shard_map/ppermute | solution.py:52
  12.1 5.0 %collective-permute-start.2 = (bf16[128,256]{1,0:T(8,128)(2,1)S(1)}, bf16[128,256]{1,0:T(8,128)(2,1)S(1)}, u32[]{:S(2)}, u32[]{:S(2)}) collective-permute-start(bf16[128,256]{1,0:T(8,128)(2,1)S(1)} %constant_dynamic-slice_fusion.refs_0_), channel_id=1, source_target_pairs={{48,0},{0,16},{16,32},{32,48},{49,1},{1,17},{17,33},{33,49},{50,2}... | collective-permute-start | bytes 196616 | tf_op jit(solution)/shard_map/ppermute | solution.py:52
  17.1 15.0 %collective-permute-start.3 = (bf16[512,256]{1,0:T(8,128)(2,1)S(1)}, bf16[512,256]{1,0:T(8,128)(2,1)S(1)}, u32[]{:S(2)}, u32[]{:S(2)}) collective-permute-start(bf16[512,256]{1,0:T(8,128)(2,1)S(1)} %shard_map.98.refs_0_), channel_id=1, source_target_pairs={{2,0},{4,2},{6,4},{8,6},{10,8},{12,10},{14,12},{0,14},{3,1},{5,3},... | collective-permute-start | bytes 786440 | tf_op jit(solution)/shard_map/ppermute | solution.py:52
  22.8 9.4 %collective-permute-start.4 = (bf16[512,256]{1,0:T(8,128)(2,1)S(1)}, bf16[512,256]{1,0:T(8,128)(2,1)S(1)}, u32[]{:S(2)}, u32[]{:S(2)}) collective-permute-start(bf16[512,256]{1,0:T(8,128)(2,1)S(1)} %shard_map.98.refs_0_), channel_id=1, source_target_pairs={{14,0},{0,2},{2,4},{4,6},{6,8},{8,10},{10,12},{12,14},{15,1},{1,3}... | collective-permute-start | bytes 786440 | tf_op jit(solution)/shard_map/ppermute | solution.py:52
  32.1 79.7 %copy-start.1 = (bf16[768,4096]{1,0:T(8,128)(2,1)}, bf16[768,4096]{1,0:T(8,128)(2,1)S(1)}, u32[]{:S(2)}) copy-start(bf16[768,4096]{1,0:T(8,128)(2,1)S(1)} %shard_map.97.refs_3_.x_ref.refs_4_) | copy-start | bytes 18874372
  32.1 31.9 %copy-start.3 = (bf16[1,32,4096]{2,1,0:T(8,128)(2,1)S(1)}, bf16[1,32,4096]{2,1,0:T(8,128)(2,1)}, u32[]{:S(2)}) copy-start(bf16[1,32,4096]{2,1,0:T(8,128)(2,1)} %param.11) | copy-start | bytes 786436
  32.2 31.9 %copy-start.4 = (bf16[128,1024]{1,0:T(8,128)(2,1)S(1)}, bf16[128,1024]{1,0:T(8,128)(2,1)}, u32[]{:S(2)}) copy-start(bf16[128,1024]{1,0:T(8,128)(2,1)} %w_ref.2) | copy-start | bytes 786436
  32.2 17.0 %collective-permute-start.11 = (bf16[1536,256]{1,0:T(8,128)(2,1)S(1)}, bf16[1536,256]{1,0:T(8,128)(2,1)S(1)}, u32[]{:S(2)}, u32[]{:S(2)}) collective-permute-start(bf16[1536,256]{1,0:T(8,128)(2,1)S(1)} %shard_map.99.refs_0_), channel_id=1, source_target_pairs={{64,0},{128,64},{192,128},{0,192},{65,1},{129,65},{193,129},{1,193... | collective-permute-start | bytes 2359304 | tf_op jit(solution)/shard_map/ppermute | solution.py:52
  34.8 18.0 %collective-permute-start.13 = (bf16[1536,256]{1,0:T(8,128)(2,1)S(1)}, bf16[1536,256]{1,0:T(8,128)(2,1)S(1)}, u32[]{:S(2)}, u32[]{:S(2)}) collective-permute-start(bf16[1536,256]{1,0:T(8,128)(2,1)S(1)} %shard_map.99.refs_0_), channel_id=1, source_target_pairs={{192,0},{0,64},{64,128},{128,192},{193,1},{1,65},{65,129},{129,193... | collective-permute-start | bytes 2359304 | tf_op jit(solution)/shard_map/ppermute | solution.py:52
  34.8 10.8 %collective-permute-start.6 = (bf16[512,256]{1,0:T(8,128)(2,1)S(1)}, bf16[512,256]{1,0:T(8,128)(2,1)S(1)}, u32[]{:S(2)}, u32[]{:S(2)}) collective-permute-start(bf16[512,256]{1,0:T(8,128)(2,1)S(1)} %collective-permute-done.4.refs_2_), channel_id=1, source_target_pairs={{14,0},{0,2},{2,4},{4,6},{6,8},{8,10},{10,12},{12,14},{15,1},{1,3}... | collective-permute-start | bytes 786440 | tf_op jit(solution)/shard_map/ppermute | solution.py:52
  34.8 10.8 %collective-permute-start.5 = (bf16[512,256]{1,0:T(8,128)(2,1)S(1)}, bf16[512,256]{1,0:T(8,128)(2,1)S(1)}, u32[]{:S(2)}, u32[]{:S(2)}) collective-permute-start(bf16[512,256]{1,0:T(8,128)(2,1)S(1)} %collective-permute-done.3.refs_1_), channel_id=1, source_target_pairs={{2,0},{4,2},{6,4},{8,6},{10,8},{12,10},{14,12},{0,14},{3,1},{5,3},... | collective-permute-start | bytes 786440 | tf_op jit(solution)/shard_map/ppermute | solution.py:52
  45.6 9.7 %collective-permute-start.8 = (bf16[512,256]{1,0:T(8,128)(2,1)S(1)}, bf16[512,256]{1,0:T(8,128)(2,1)S(1)}, u32[]{:S(2)}, u32[]{:S(2)}) collective-permute-start(bf16[512,256]{1,0:T(8,128)(2,1)S(1)} %collective-permute-done.6.refs_1_), channel_id=1, source_target_pairs={{14,0},{0,2},{2,4},{4,6},{6,8},{8,10},{10,12},{12,14},{15,1},{1,3}... | collective-permute-start | bytes 786440 | tf_op jit(solution)/shard_map/ppermute | solution.py:52
  45.6 9.8 %collective-permute-start.7 = (bf16[512,256]{1,0:T(8,128)(2,1)S(1)}, bf16[512,256]{1,0:T(8,128)(2,1)S(1)}, u32[]{:S(2)}, u32[]{:S(2)}) collective-permute-start(bf16[512,256]{1,0:T(8,128)(2,1)S(1)} %collective-permute-done.5.refs_0_), channel_id=1, source_target_pairs={{2,0},{4,2},{6,4},{8,6},{10,8},{12,10},{14,12},{0,14},{3,1},{5,3},... | collective-permute-start | bytes 786440 | tf_op jit(solution)/shard_map/ppermute | solution.py:52
  49.3 11.1 %collective-permute-start.12 = (bf16[768,256]{1,0:T(8,128)(2,1)S(1)}, bf16[768,256]{1,0:T(8,128)(2,1)S(1)}, u32[]{:S(2)}, u32[]{:S(2)}) collective-permute-start(bf16[768,256]{1,0:T(8,128)(2,1)S(1)} %shard_map.102), channel_id=1, source_target_pairs={{64,0},{128,64},{192,128},{0,192},{65,1},{129,65},{193,129},{1,193... | collective-permute-start | bytes 1179656 | tf_op jit(solution)/shard_map/ppermute | solution.py:52
  52.9 8.3 %collective-permute-start.14 = (bf16[768,256]{1,0:T(8,128)(2,1)S(1)}, bf16[768,256]{1,0:T(8,128)(2,1)S(1)}, u32[]{:S(2)}, u32[]{:S(2)}) collective-permute-start(bf16[768,256]{1,0:T(8,128)(2,1)S(1)} %shard_map.103), channel_id=1, source_target_pairs={{192,0},{0,64},{64,128},{128,192},{193,1},{1,65},{65,129},{129,193... | collective-permute-start | bytes 1179656 | tf_op jit(solution)/shard_map/ppermute | solution.py:52
  55.3 5.1 %collective-permute-start.10 = (bf16[256,256]{1,0:T(8,128)(2,1)S(1)}, bf16[256,256]{1,0:T(8,128)(2,1)S(1)}, u32[]{:S(2)}, u32[]{:S(2)}) collective-permute-start(bf16[256,256]{1,0:T(8,128)(2,1)S(1)} %shard_map.101), channel_id=1, source_target_pairs={{14,0},{0,2},{2,4},{4,6},{6,8},{8,10},{10,12},{12,14},{15,1},{1,3}... | collective-permute-start | bytes 393224 | tf_op jit(solution)/shard_map/ppermute | solution.py:52
  55.5 5.0 %collective-permute-start.9 = (bf16[256,256]{1,0:T(8,128)(2,1)S(1)}, bf16[256,256]{1,0:T(8,128)(2,1)S(1)}, u32[]{:S(2)}, u32[]{:S(2)}) collective-permute-start(bf16[256,256]{1,0:T(8,128)(2,1)S(1)} %shard_map.100), channel_id=1, source_target_pairs={{2,0},{4,2},{6,4},{8,6},{10,8},{12,10},{14,12},{0,14},{3,1},{5,3},... | collective-permute-start | bytes 393224 | tf_op jit(solution)/shard_map/ppermute | solution.py:52
  61.3 27.2 %collective-permute-start.17 = (bf16[2560,256]{1,0:T(8,128)(2,1)S(1)}, bf16[2560,256]{1,0:T(8,128)(2,1)S(1)}, u32[]{:S(2)}, u32[]{:S(2)}) collective-permute-start(bf16[2560,256]{1,0:T(8,128)(2,1)S(1)} %shard_map.104.refs_1_), channel_id=1, source_target_pairs={{192,0},{0,64},{64,128},{128,192},{193,1},{1,65},{65,129},{129,193... | collective-permute-start | bytes 3932168 | tf_op jit(solution)/shard_map/ppermute | solution.py:52
  61.4 27.2 %collective-permute-start.15 = (bf16[2560,256]{1,0:T(8,128)(2,1)S(1)}, bf16[2560,256]{1,0:T(8,128)(2,1)S(1)}, u32[]{:S(2)}, u32[]{:S(2)}) collective-permute-start(bf16[2560,256]{1,0:T(8,128)(2,1)S(1)} %shard_map.104.refs_1_), channel_id=1, source_target_pairs={{64,0},{128,64},{192,128},{0,192},{65,1},{129,65},{193,129},{1,193... | collective-permute-start | bytes 3932168 | tf_op jit(solution)/shard_map/ppermute | solution.py:52
  88.5 23.3 %collective-permute-start.18 = (bf16[1280,256]{1,0:T(8,128)(2,1)S(1)}, bf16[1280,256]{1,0:T(8,128)(2,1)S(1)}, u32[]{:S(2)}, u32[]{:S(2)}) collective-permute-start(bf16[1280,256]{1,0:T(8,128)(2,1)S(1)} %shard_map.108), channel_id=1, source_target_pairs={{192,0},{0,64},{64,128},{128,192},{193,1},{1,65},{65,129},{129,193... | collective-permute-start | bytes 1966088 | tf_op jit(solution)/shard_map/ppermute | solution.py:52
  88.7 23.2 %collective-permute-start.16 = (bf16[1280,256]{1,0:T(8,128)(2,1)S(1)}, bf16[1280,256]{1,0:T(8,128)(2,1)S(1)}, u32[]{:S(2)}, u32[]{:S(2)}) collective-permute-start(bf16[1280,256]{1,0:T(8,128)(2,1)S(1)} %shard_map.107), channel_id=1, source_target_pairs={{64,0},{128,64},{192,128},{0,192},{65,1},{129,65},{193,129},{1,193... | collective-permute-start | bytes 1966088 | tf_op jit(solution)/shard_map/ppermute | solution.py:52
  113.7 47.6 %copy-start.2 = (bf16[1024,128]{1,0:T(8,128)(2,1)S(1)}, bf16[1024,128]{1,0:T(8,128)(2,1)}, u32[]{:S(2)}) copy-start(bf16[1024,128]{1,0:T(8,128)(2,1)} %w_ref.3) | copy-start | bytes 786436
  162.0 4.6 %collective-permute-start.19 = (f32[40,128]{1,0:T(8,128)S(1)}, f32[40,128]{1,0:T(8,128)S(1)}, u32[]{:S(2)}, u32[]{:S(2)}) collective-permute-start(f32[40,128]{1,0:T(8,128)S(1)} %shard_map.113.own_ref), channel_id=1, source_target_pairs={{0,1},{1,0},{2,3},{3,2},{4,5},{5,4},{6,7},{7,6},{8,9},{9,8},{10,11... | collective-permute-start | bytes 61448 | tf_op jit(solution)/shard_map/ppermute | solution.py:427
Sparse Core Ops, SparseCore 0:
  10.6 106.6 all-gather.1

commit v8 on v7

--- a/solution.py
+++ b/solution.py
@@ -288,8 +288,9 @@
         quarter = lax.rem(pos[2] + dx, NX)
         v = acc[:, pl.ds(pl.multiple_of(quarter * cols, cols), cols)].astype(bf16)
         at = slice(dx * pairs, (dx + 1) * pairs)
-        numer = jnp.dot(high_ref[at, :], v, preferred_element_type=f32)
-        numer += jnp.dot(low_ref[at, :], v, preferred_element_type=f32)
+        both = jnp.concatenate([high_ref[at, :], low_ref[at, :]], axis=0)
+        sums = jnp.dot(both, v, preferred_element_type=f32)
+        numer = sums[:pairs, :] + sums[pairs:, :]
         numer = jnp.where(same_head(pairs, cols, answers), numer, 0.0)
         total = numer[0:answers, :]
         for h in range(1, pairs // answers):

time: 175 us -> 175 us (level)
  no operation moved by 1% of the time
where the time goes in v8:
time: 175 us
  blocking collectives  62.5 us (36%)
  starting transfers between devices  34.3 us (20%)
  Pallas kernels  32.8 us (19%)
  waiting for transfers between devices  29 us (17%)
  between operations  14.3 us (8%)
    all_to_all x4, blocking collectives, exchange(): return lax.all_to_all(a, PSG, split_axis=0, concat_axis=0, tiled=True)  62.5 us
    ppermute x19, starting transfers between devices, recv(): return lax.ppermute(a, axis, [((i + k) % n, i) for i in range(n)])  30.5 us
    ppermute x19, waiting for transfers between devices, recv(): return lax.ppermute(a, axis, [((i + k) % n, i) for i in range(n)])  23.9 us
    pallas_call x6, Pallas kernels, call(): pl.pallas_call(kernel, out_shape=outs, in_specs=specs, out_specs=jax.tree...  17.4 us
    pallas_call x1, Pallas kernels, normalise(): pl.pallas_call(norm_kernel, out_shape=shaped((rows, width), bf16), grid_s...  7.9 us
    pallas_call x4, Pallas kernels, project(): pl.pallas_call(functools.partial(project_kernel, [len(pieces) for pieces...  7.14 us
    ppermute x1, starting transfers between devices, body(): other = lax.ppermute(part, 'tp', [(0, 1), (1, 0)])  3.8 us
    all_gather x1, waiting for transfers between devices, body(): w_values = lax.all_gather(w_value, PSG, axis=0, tiled=True)  3.59 us
  transfers between devices with their start and end apart: 21, of which 11 were waited for; matrix products, arithmetic and copies ran while one was open for 1% of the time, Pallas kernels for 10%

profile of v8, /device:TPU:1, one launch (start us, length us, event | category | flops | bytes accessed | tf_op | source)
XLA Modules:
  0.0 174.6 jit_solution(3097997279525376406)
XLA Ops:
  8.1 3.6 %collective-permute-start = (bf16[128,256]{1,0:T(8,128)(2,1)S(1)}, bf16[128,256]{1,0:T(8,128)(2,1)S(1)}, u32[]{:S(2)}, u32[]{:S(2)}) collective-permute-start(bf16[128,256]{1,0:T(8,128)(2,1)S(1)} %constant_dynamic-slice_fusion.refs_0_), channel_id=1, source_target_pairs={{16,0},{32,16},{48,32},{0,48},{17,1},{33,17},{49,33},{1,49},{18,2}... | collective-permute-start | bytes 196616 | tf_op jit(solution)/shard_map/ppermute | solution.py:52
  13.1 3.4 %collective-permute-done.1.refs_2_ = bf16[128,256]{1,0:T(8,128)(2,1)S(1)} collective-permute-done((bf16[128,256]{1,0:T(8,128)(2,1)S(1)}, bf16[128,256]{1,0:T(8,128)(2,1)S(1)}, u32[]{:S(2)}, u32[]{:S(2)}) %collective-permute-start.1) | collective-permute-done | bytes 65568 | tf_op jit(solution)/shard_map/ppermute | solution.py:52
  17.1 5.7 %collective-permute-start.3 = (bf16[512,256]{1,0:T(8,128)(2,1)S(1)}, bf16[512,256]{1,0:T(8,128)(2,1)S(1)}, u32[]{:S(2)}, u32[]{:S(2)}) collective-permute-start(bf16[512,256]{1,0:T(8,128)(2,1)S(1)} %shard_map.98.refs_0_), channel_id=1, source_target_pairs={{2,0},{4,2},{6,4},{8,6},{10,8},{12,10},{14,12},{0,14},{3,1},{5,3},... | collective-permute-start | bytes 786440 | tf_op jit(solution)/shard_map/ppermute | solution.py:52
  24.2 7.9 %shard_map.97.refs_3_.x_ref.refs_4_ = bf16[768,4096]{1,0:T(8,128)(2,1)S(1)} custom-call(s32[6]{0:T(128)S(1)} %pad_add_fusion.pos, bf16[768,4096]{1,0:T(8,128)(2,1)} %bitcast.8, bf16[1,4096]{1,0:T(2,128)(2,1)S(1)} %broadcast_in_dim.6.after_ref.gain_ref), custom_call_target="tpu_custom_call" | custom-call | flops 18874368 | bytes 12582912 | tf_op jit(solution)/shard_map/pallas_call | solution.py:131
  32.2 2.6 %collective-permute-start.11 = (bf16[1536,256]{1,0:T(8,128)(2,1)S(1)}, bf16[1536,256]{1,0:T(8,128)(2,1)S(1)}, u32[]{:S(2)}, u32[]{:S(2)}) collective-permute-start(bf16[1536,256]{1,0:T(8,128)(2,1)S(1)} %shard_map.99.refs_0_), channel_id=1, source_target_pairs={{64,0},{128,64},{192,128},{0,192},{65,1},{129,65},{193,129},{1,193... | collective-permute-start | bytes 2359304 | tf_op jit(solution)/shard_map/ppermute | solution.py:52
  34.8 2.7 %collective-permute-start.5 = (bf16[512,256]{1,0:T(8,128)(2,1)S(1)}, bf16[512,256]{1,0:T(8,128)(2,1)S(1)}, u32[]{:S(2)}, u32[]{:S(2)}) collective-permute-start(bf16[512,256]{1,0:T(8,128)(2,1)S(1)} %collective-permute-done.3.refs_1_), channel_id=1, source_target_pairs={{2,0},{4,2},{6,4},{8,6},{10,8},{12,10},{14,12},{0,14},{3,1},{5,3},... | collective-permute-start | bytes 786440 | tf_op jit(solution)/shard_map/ppermute | solution.py:52
  37.6 8.1 %collective-permute-done.6.refs_1_ = bf16[512,256]{1,0:T(8,128)(2,1)S(1)} collective-permute-done((bf16[512,256]{1,0:T(8,128)(2,1)S(1)}, bf16[512,256]{1,0:T(8,128)(2,1)S(1)}, u32[]{:S(2)}, u32[]{:S(2)}) %collective-permute-start.6) | collective-permute-done | bytes 262176 | tf_op jit(solution)/shard_map/ppermute | solution.py:52
  45.6 2.7 %collective-permute-start.7 = (bf16[512,256]{1,0:T(8,128)(2,1)S(1)}, bf16[512,256]{1,0:T(8,128)(2,1)S(1)}, u32[]{:S(2)}, u32[]{:S(2)}) collective-permute-start(bf16[512,256]{1,0:T(8,128)(2,1)S(1)} %collective-permute-done.5.refs_0_), channel_id=1, source_target_pairs={{2,0},{4,2},{6,4},{8,6},{10,8},{12,10},{14,12},{0,14},{3,1},{5,3},... | collective-permute-start | bytes 786440 | tf_op jit(solution)/shard_map/ppermute | solution.py:52
  48.3 1.0 collective-permute-done.11.refs_0_
  49.3 3.5 %collective-permute-start.12 = (bf16[768,256]{1,0:T(8,128)(2,1)S(1)}, bf16[768,256]{1,0:T(8,128)(2,1)S(1)}, u32[]{:S(2)}, u32[]{:S(2)}) collective-permute-start(bf16[768,256]{1,0:T(8,128)(2,1)S(1)} %shard_map.102), channel_id=1, source_target_pairs={{64,0},{128,64},{192,128},{0,192},{65,1},{129,65},{193,129},{1,193... | collective-permute-start | bytes 1179656 | tf_op jit(solution)/shard_map/ppermute | solution.py:52
  53.0 2.4 %collective-permute-done.8.refs_0_.refs_3_ = bf16[512,256]{1,0:T(8,128)(2,1)S(1)} collective-permute-done((bf16[512,256]{1,0:T(8,128)(2,1)S(1)}, bf16[512,256]{1,0:T(8,128)(2,1)S(1)}, u32[]{:S(2)}, u32[]{:S(2)}) %collective-permute-start.8) | collective-permute-done | bytes 262176 | tf_op jit(solution)/shard_map/ppermute | solution.py:52
  55.5 2.9 %collective-permute-start.9 = (bf16[256,256]{1,0:T(8,128)(2,1)S(1)}, bf16[256,256]{1,0:T(8,128)(2,1)S(1)}, u32[]{:S(2)}, u32[]{:S(2)}) collective-permute-start(bf16[256,256]{1,0:T(8,128)(2,1)S(1)} %shard_map.100), channel_id=1, source_target_pairs={{2,0},{4,2},{6,4},{8,6},{10,8},{12,10},{14,12},{0,14},{3,1},{5,3},... | collective-permute-start | bytes 393224 | tf_op jit(solution)/shard_map/ppermute | solution.py:52
  58.4 2.1 %collective-permute-done.10.refs_5_ = bf16[256,256]{1,0:T(8,128)(2,1)S(1)} collective-permute-done((bf16[256,256]{1,0:T(8,128)(2,1)S(1)}, bf16[256,256]{1,0:T(8,128)(2,1)S(1)}, u32[]{:S(2)}, u32[]{:S(2)}) %collective-permute-start.10) | collective-permute-done | bytes 131104 | tf_op jit(solution)/shard_map/ppermute | solution.py:52
  60.5 0.8 collective-permute-done.14.refs_7_.refs_1_
  61.4 2.7 %collective-permute-start.15 = (bf16[2560,256]{1,0:T(8,128)(2,1)S(1)}, bf16[2560,256]{1,0:T(8,128)(2,1)S(1)}, u32[]{:S(2)}, u32[]{:S(2)}) collective-permute-start(bf16[2560,256]{1,0:T(8,128)(2,1)S(1)} %shard_map.104.refs_1_), channel_id=1, source_target_pairs={{64,0},{128,64},{192,128},{0,192},{65,1},{129,65},{193,129},{1,193... | collective-permute-start | bytes 3932168 | tf_op jit(solution)/shard_map/ppermute | solution.py:52
  64.8 15.9 %all_to_all.20.got_ref = f32[32,8,128]{2,1,0:T(8,128)S(1)} all-to-all(f32[32,8,128]{2,1,0:T(8,128)S(1)} %shard_map.95), channel_id=1, replica_groups=mesh['dp'=4,'y'=4,'z'=8,'tp'=2] {'y','z'}, dimensions={0} | all-to-all | bytes 262144 | tf_op jit(solution)/shard_map/all_to_all | solution.py:56
  81.3 1.8 %shard_map.105.refs_1_.refs_0_ = bf16[768,256]{1,0:T(8,128)(2,1)S(1)} custom-call(bf16[768,4096]{1,0:T(8,128)(2,1)S(1)} %shard_map.97.refs_3_.x_ref.refs_4_, bf16[1536,256]{1,0:T(8,128)(2,1)S(1)} %shard_map.99.refs_0_, bf16[2560,256]{1,0:T(8,128)(2,1)S(1)} %shard_map.104.refs_1_, f32[32,8,128]{2,1,0:T(8,128)S(1)} %shard_map.96.refs_2_), custom_call_target="tpu_custom_call" | custom-call | flops 1610612736 | bytes 8781824 | tf_op jit(solution)/shard_map/pallas_call | solution.py:168
  83.1 5.4 %collective-permute-done.17.refs_0_.refs_1_ = bf16[2560,256]{1,0:T(8,128)(2,1)S(1)} collective-permute-done((bf16[2560,256]{1,0:T(8,128)(2,1)S(1)}, bf16[2560,256]{1,0:T(8,128)(2,1)S(1)}, u32[]{:S(2)}, u32[]{:S(2)}) %collective-permute-start.17) | collective-permute-done | bytes 1310752 | tf_op jit(solution)/shard_map/ppermute | solution.py:52
  88.7 2.7 %collective-permute-start.16 = (bf16[1280,256]{1,0:T(8,128)(2,1)S(1)}, bf16[1280,256]{1,0:T(8,128)(2,1)S(1)}, u32[]{:S(2)}, u32[]{:S(2)}) collective-permute-start(bf16[1280,256]{1,0:T(8,128)(2,1)S(1)} %shard_map.107), channel_id=1, source_target_pairs={{64,0},{128,64},{192,128},{0,192},{65,1},{129,65},{193,129},{1,193... | collective-permute-start | bytes 1966088 | tf_op jit(solution)/shard_map/ppermute | solution.py:52
  91.4 16.8 %all_to_all.21.refs_2_.q_ref = f32[32,8,128]{2,1,0:T(8,128)S(1)} all-to-all(f32[32,8,128]{2,1,0:T(8,128)S(1)} %shard_map.96.refs_2_), channel_id=1, replica_groups=mesh['dp'=4,'y'=4,'z'=8,'tp'=2] {'y','z'}, dimensions={0} | all-to-all | bytes 262144 | tf_op jit(solution)/shard_map/all_to_all | solution.py:56
  108.3 1.8 %shard_map.110.refs_3_ = bf16[768,256]{1,0:T(8,128)(2,1)S(1)} custom-call(bf16[768,4096]{1,0:T(8,128)(2,1)S(1)} %shard_map.97.refs_3_.x_ref.refs_4_, bf16[1536,256]{1,0:T(8,128)(2,1)S(1)} %collective-permute-done.13.refs_0_, bf16[2560,256]{1,0:T(8,128)(2,1)S(1)} %collective-permute-done.17.refs_0_.refs_1_, f32[32,8,128]{2,1,0:T(8,128)S(1)} %all_to_all.21.refs_2_.q_ref), custom_call_target="tpu_custom_call" | custom-call | flops 1610612736 | bytes 8781824 | tf_op jit(solution)/shard_map/pallas_call | solution.py:168
  110.0 1.8 %shard_map.106.refs_1_ = bf16[768,256]{1,0:T(8,128)(2,1)S(1)} custom-call(bf16[768,4096]{1,0:T(8,128)(2,1)S(1)} %shard_map.97.refs_3_.x_ref.refs_4_, bf16[1536,256]{1,0:T(8,128)(2,1)S(1)} %collective-permute-done.11.refs_0_, bf16[2560,256]{1,0:T(8,128)(2,1)S(1)} %collective-permute-done.15.refs_1_.refs_0_, f32[32,8,128]{2,1,0:T(8,128)S(1)} %all_to_all.21.refs_2_.q_ref), custom_call_target="tpu_custom_call" | custom-call | flops 1610612736 | bytes 8781824 | tf_op jit(solution)/shard_map/pallas_call | solution.py:168
  111.9 1.8 %shard_map.109.refs_2_ = bf16[768,256]{1,0:T(8,128)(2,1)S(1)} custom-call(bf16[768,4096]{1,0:T(8,128)(2,1)S(1)} %shard_map.97.refs_3_.x_ref.refs_4_, bf16[768,256]{1,0:T(8,128)(2,1)S(1)} %collective-permute-done.12.refs_6_.refs_0_, bf16[768,256]{1,0:T(8,128)(2,1)S(1)} %collective-permute-done.14.refs_7_.refs_1_, ...), custom_call_target="tpu_custom_call" | custom-call | flops 1610612736 | bytes 8781824 | tf_op jit(solution)/shard_map/pallas_call | solution.py:168
  113.7 3.6 %all-gather.2.cloned.1.call-done.refs_5_ = bf16[4096,1024]{1,0:T(8,128)(2,1)} async-done(((bf16[128,1024]{1,0:T(8,128)(2,1)}), bf16[4096,1024]{1,0:T(8,128)(2,1)}) %all-gather.2.cloned.1.call-update) | async-done | bytes 8388624 | tf_op jit(solution)/shard_map/all_gather | solution.py:368
  117.3 13.3 %shard_map.111 = f32[32,9,128]{2,1,0:T(8,128)S(1)} custom-call(s32[6]{0:T(128)S(1)} %pad_add_fusion.pos, f32[32,8,128]{2,1,0:T(8,128)S(1)} %all_to_all.21.refs_2_.q_ref, bf16[768,256]{1,0:T(8,128)(2,1)S(1)} %shard_map.105.refs_1_.refs_0_, bf16[768,256]{1,0:T(8,128)(2,1)S(1)} %shard_map.106.refs_1_, bf16[768,256]{1,0:T(8,128)(2,1)S(1)} %shard_map.109.refs_2_, ...), custom_call_target="tpu_custom_call" | custom-call | flops 6442450944 | bytes 1048576 | tf_op jit(solution)/shard_map/pallas_call | solution.py:39
  130.6 15.1 %all_to_all.22.got_ref = f32[32,9,128]{2,1,0:T(8,128)S(1)} all-to-all(f32[32,9,128]{2,1,0:T(8,128)S(1)} %shard_map.111), channel_id=1, replica_groups=mesh['dp'=4,'y'=4,'z'=8,'tp'=2] {'y','z'}, dimensions={0} | all-to-all | bytes 294912 | tf_op jit(solution)/shard_map/all_to_all | solution.py:56
  145.7 0.9 shard_map.112
  146.6 14.6 %all_to_all.23.ctx_ref = bf16[32,16,128]{2,1,0:T(8,128)(2,1)S(1)} all-to-all(bf16[32,16,128]{2,1,0:T(8,128)(2,1)S(1)} %shard_map.112), channel_id=1, replica_groups=mesh['dp'=4,'y'=4,'z'=8,'tp'=2] {'y','z'}, dimensions={0} | all-to-all | bytes 262144 | tf_op jit(solution)/shard_map/all_to_all | solution.py:56
  161.2 0.7 shard_map.113.own_ref
  162.0 3.8 %collective-permute-start.19 = (f32[40,128]{1,0:T(8,128)S(1)}, f32[40,128]{1,0:T(8,128)S(1)}, u32[]{:S(2)}, u32[]{:S(2)}) collective-permute-start(f32[40,128]{1,0:T(8,128)S(1)} %shard_map.113.own_ref), channel_id=1, source_target_pairs={{0,1},{1,0},{2,3},{3,2},{4,5},{5,4},{6,7},{7,6},{8,9},{9,8},{10,11... | collective-permute-start | bytes 61448 | tf_op jit(solution)/shard_map/ppermute | solution.py:428
  165.8 0.8 collective-permute-done.19.other_ref
  166.6 1.1 shard_map.114
  (48 shorter events, 6.4 us)
Async XLA Ops:
  7.2 1.0 copy-start
  7.2 110.1 %all-gather.2.cloned.1.call-start = ((), (), s32[]{:S(2)}) async-start(), calls=%async_computation.4 | async-start | bytes 8650752 | tf_op jit(solution)/shard_map/all_gather | solution.py:368
  8.1 5.0 %collective-permute-start = (bf16[128,256]{1,0:T(8,128)(2,1)S(1)}, bf16[128,256]{1,0:T(8,128)(2,1)S(1)}, u32[]{:S(2)}, u32[]{:S(2)}) collective-permute-start(bf16[128,256]{1,0:T(8,128)(2,1)S(1)} %constant_dynamic-slice_fusion.refs_0_), channel_id=1, source_target_pairs={{16,0},{32,16},{48,32},{0,48},{17,1},{33,17},{49,33},{1,49},{18,2}... | collective-permute-start | bytes 196616 | tf_op jit(solution)/shard_map/ppermute | solution.py:52
  11.8 4.7 %collective-permute-start.1 = (bf16[128,256]{1,0:T(8,128)(2,1)S(1)}, bf16[128,256]{1,0:T(8,128)(2,1)S(1)}, u32[]{:S(2)}, u32[]{:S(2)}) collective-permute-start(bf16[128,256]{1,0:T(8,128)(2,1)S(1)} %constant_dynamic-slice_fusion.refs_0_), channel_id=1, source_target_pairs={{32,0},{48,16},{0,32},{16,48},{33,1},{49,17},{1,33},{17,49},{34,2}... | collective-permute-start | bytes 196616 | tf_op jit(solution)/shard_map/ppermute | solution.py:52
  12.1 5.0 %collective-permute-start.2 = (bf16[128,256]{1,0:T(8,128)(2,1)S(1)}, bf16[128,256]{1,0:T(8,128)(2,1)S(1)}, u32[]{:S(2)}, u32[]{:S(2)}) collective-permute-start(bf16[128,256]{1,0:T(8,128)(2,1)S(1)} %constant_dynamic-slice_fusion.refs_0_), channel_id=1, source_target_pairs={{48,0},{0,16},{16,32},{32,48},{49,1},{1,17},{17,33},{33,49},{50,2}... | collective-permute-start | bytes 196616 | tf_op jit(solution)/shard_map/ppermute | solution.py:52
  17.1 15.0 %collective-permute-start.3 = (bf16[512,256]{1,0:T(8,128)(2,1)S(1)}, bf16[512,256]{1,0:T(8,128)(2,1)S(1)}, u32[]{:S(2)}, u32[]{:S(2)}) collective-permute-start(bf16[512,256]{1,0:T(8,128)(2,1)S(1)} %shard_map.98.refs_0_), channel_id=1, source_target_pairs={{2,0},{4,2},{6,4},{8,6},{10,8},{12,10},{14,12},{0,14},{3,1},{5,3},... | collective-permute-start | bytes 786440 | tf_op jit(solution)/shard_map/ppermute | solution.py:52
  22.8 9.4 %collective-permute-start.4 = (bf16[512,256]{1,0:T(8,128)(2,1)S(1)}, bf16[512,256]{1,0:T(8,128)(2,1)S(1)}, u32[]{:S(2)}, u32[]{:S(2)}) collective-permute-start(bf16[512,256]{1,0:T(8,128)(2,1)S(1)} %shard_map.98.refs_0_), channel_id=1, source_target_pairs={{14,0},{0,2},{2,4},{4,6},{6,8},{8,10},{10,12},{12,14},{15,1},{1,3}... | collective-permute-start | bytes 786440 | tf_op jit(solution)/shard_map/ppermute | solution.py:52
  32.1 79.7 %copy-start.1 = (bf16[768,4096]{1,0:T(8,128)(2,1)}, bf16[768,4096]{1,0:T(8,128)(2,1)S(1)}, u32[]{:S(2)}) copy-start(bf16[768,4096]{1,0:T(8,128)(2,1)S(1)} %shard_map.97.refs_3_.x_ref.refs_4_) | copy-start | bytes 18874372
  32.1 31.9 %copy-start.3 = (bf16[1,32,4096]{2,1,0:T(8,128)(2,1)S(1)}, bf16[1,32,4096]{2,1,0:T(8,128)(2,1)}, u32[]{:S(2)}) copy-start(bf16[1,32,4096]{2,1,0:T(8,128)(2,1)} %param.11) | copy-start | bytes 786436
  32.2 31.9 %copy-start.4 = (bf16[128,1024]{1,0:T(8,128)(2,1)S(1)}, bf16[128,1024]{1,0:T(8,128)(2,1)}, u32[]{:S(2)}) copy-start(bf16[128,1024]{1,0:T(8,128)(2,1)} %w_ref.2) | copy-start | bytes 786436
  32.2 17.0 %collective-permute-start.11 = (bf16[1536,256]{1,0:T(8,128)(2,1)S(1)}, bf16[1536,256]{1,0:T(8,128)(2,1)S(1)}, u32[]{:S(2)}, u32[]{:S(2)}) collective-permute-start(bf16[1536,256]{1,0:T(8,128)(2,1)S(1)} %shard_map.99.refs_0_), channel_id=1, source_target_pairs={{64,0},{128,64},{192,128},{0,192},{65,1},{129,65},{193,129},{1,193... | collective-permute-start | bytes 2359304 | tf_op jit(solution)/shard_map/ppermute | solution.py:52
  34.8 18.0 %collective-permute-start.13 = (bf16[1536,256]{1,0:T(8,128)(2,1)S(1)}, bf16[1536,256]{1,0:T(8,128)(2,1)S(1)}, u32[]{:S(2)}, u32[]{:S(2)}) collective-permute-start(bf16[1536,256]{1,0:T(8,128)(2,1)S(1)} %shard_map.99.refs_0_), channel_id=1, source_target_pairs={{192,0},{0,64},{64,128},{128,192},{193,1},{1,65},{65,129},{129,193... | collective-permute-start | bytes 2359304 | tf_op jit(solution)/shard_map/ppermute | solution.py:52
  34.8 10.8 %collective-permute-start.6 = (bf16[512,256]{1,0:T(8,128)(2,1)S(1)}, bf16[512,256]{1,0:T(8,128)(2,1)S(1)}, u32[]{:S(2)}, u32[]{:S(2)}) collective-permute-start(bf16[512,256]{1,0:T(8,128)(2,1)S(1)} %collective-permute-done.4.refs_2_), channel_id=1, source_target_pairs={{14,0},{0,2},{2,4},{4,6},{6,8},{8,10},{10,12},{12,14},{15,1},{1,3}... | collective-permute-start | bytes 786440 | tf_op jit(solution)/shard_map/ppermute | solution.py:52
  34.8 10.8 %collective-permute-start.5 = (bf16[512,256]{1,0:T(8,128)(2,1)S(1)}, bf16[512,256]{1,0:T(8,128)(2,1)S(1)}, u32[]{:S(2)}, u32[]{:S(2)}) collective-permute-start(bf16[512,256]{1,0:T(8,128)(2,1)S(1)} %collective-permute-done.3.refs_1_), channel_id=1, source_target_pairs={{2,0},{4,2},{6,4},{8,6},{10,8},{12,10},{14,12},{0,14},{3,1},{5,3},... | collective-permute-start | bytes 786440 | tf_op jit(solution)/shard_map/ppermute | solution.py:52
  45.6 9.7 %collective-permute-start.8 = (bf16[512,256]{1,0:T(8,128)(2,1)S(1)}, bf16[512,256]{1,0:T(8,128)(2,1)S(1)}, u32[]{:S(2)}, u32[]{:S(2)}) collective-permute-start(bf16[512,256]{1,0:T(8,128)(2,1)S(1)} %collective-permute-done.6.refs_1_), channel_id=1, source_target_pairs={{14,0},{0,2},{2,4},{4,6},{6,8},{8,10},{10,12},{12,14},{15,1},{1,3}... | collective-permute-start | bytes 786440 | tf_op jit(solution)/shard_map/ppermute | solution.py:52
  45.6 9.8 %collective-permute-start.7 = (bf16[512,256]{1,0:T(8,128)(2,1)S(1)}, bf16[512,256]{1,0:T(8,128)(2,1)S(1)}, u32[]{:S(2)}, u32[]{:S(2)}) collective-permute-start(bf16[512,256]{1,0:T(8,128)(2,1)S(1)} %collective-permute-done.5.refs_0_), channel_id=1, source_target_pairs={{2,0},{4,2},{6,4},{8,6},{10,8},{12,10},{14,12},{0,14},{3,1},{5,3},... | collective-permute-start | bytes 786440 | tf_op jit(solution)/shard_map/ppermute | solution.py:52
  49.3 11.1 %collective-permute-start.12 = (bf16[768,256]{1,0:T(8,128)(2,1)S(1)}, bf16[768,256]{1,0:T(8,128)(2,1)S(1)}, u32[]{:S(2)}, u32[]{:S(2)}) collective-permute-start(bf16[768,256]{1,0:T(8,128)(2,1)S(1)} %shard_map.102), channel_id=1, source_target_pairs={{64,0},{128,64},{192,128},{0,192},{65,1},{129,65},{193,129},{1,193... | collective-permute-start | bytes 1179656 | tf_op jit(solution)/shard_map/ppermute | solution.py:52
  52.9 8.3 %collective-permute-start.14 = (bf16[768,256]{1,0:T(8,128)(2,1)S(1)}, bf16[768,256]{1,0:T(8,128)(2,1)S(1)}, u32[]{:S(2)}, u32[]{:S(2)}) collective-permute-start(bf16[768,256]{1,0:T(8,128)(2,1)S(1)} %shard_map.103), channel_id=1, source_target_pairs={{192,0},{0,64},{64,128},{128,192},{193,1},{1,65},{65,129},{129,193... | collective-permute-start | bytes 1179656 | tf_op jit(solution)/shard_map/ppermute | solution.py:52
  55.3 5.1 %collective-permute-start.10 = (bf16[256,256]{1,0:T(8,128)(2,1)S(1)}, bf16[256,256]{1,0:T(8,128)(2,1)S(1)}, u32[]{:S(2)}, u32[]{:S(2)}) collective-permute-start(bf16[256,256]{1,0:T(8,128)(2,1)S(1)} %shard_map.101), channel_id=1, source_target_pairs={{14,0},{0,2},{2,4},{4,6},{6,8},{8,10},{10,12},{12,14},{15,1},{1,3}... | collective-permute-start | bytes 393224 | tf_op jit(solution)/shard_map/ppermute | solution.py:52
  55.5 5.0 %collective-permute-start.9 = (bf16[256,256]{1,0:T(8,128)(2,1)S(1)}, bf16[256,256]{1,0:T(8,128)(2,1)S(1)}, u32[]{:S(2)}, u32[]{:S(2)}) collective-permute-start(bf16[256,256]{1,0:T(8,128)(2,1)S(1)} %shard_map.100), channel_id=1, source_target_pairs={{2,0},{4,2},{6,4},{8,6},{10,8},{12,10},{14,12},{0,14},{3,1},{5,3},... | collective-permute-start | bytes 393224 | tf_op jit(solution)/shard_map/ppermute | solution.py:52
  61.3 27.2 %collective-permute-start.17 = (bf16[2560,256]{1,0:T(8,128)(2,1)S(1)}, bf16[2560,256]{1,0:T(8,128)(2,1)S(1)}, u32[]{:S(2)}, u32[]{:S(2)}) collective-permute-start(bf16[2560,256]{1,0:T(8,128)(2,1)S(1)} %shard_map.104.refs_1_), channel_id=1, source_target_pairs={{192,0},{0,64},{64,128},{128,192},{193,1},{1,65},{65,129},{129,193... | collective-permute-start | bytes 3932168 | tf_op jit(solution)/shard_map/ppermute | solution.py:52
  61.4 27.2 %collective-permute-start.15 = (bf16[2560,256]{1,0:T(8,128)(2,1)S(1)}, bf16[2560,256]{1,0:T(8,128)(2,1)S(1)}, u32[]{:S(2)}, u32[]{:S(2)}) collective-permute-start(bf16[2560,256]{1,0:T(8,128)(2,1)S(1)} %shard_map.104.refs_1_), channel_id=1, source_target_pairs={{64,0},{128,64},{192,128},{0,192},{65,1},{129,65},{193,129},{1,193... | collective-permute-start | bytes 3932168 | tf_op jit(solution)/shard_map/ppermute | solution.py:52
  88.5 23.3 %collective-permute-start.18 = (bf16[1280,256]{1,0:T(8,128)(2,1)S(1)}, bf16[1280,256]{1,0:T(8,128)(2,1)S(1)}, u32[]{:S(2)}, u32[]{:S(2)}) collective-permute-start(bf16[1280,256]{1,0:T(8,128)(2,1)S(1)} %shard_map.108), channel_id=1, source_target_pairs={{192,0},{0,64},{64,128},{128,192},{193,1},{1,65},{65,129},{129,193... | collective-permute-start | bytes 1966088 | tf_op jit(solution)/shard_map/ppermute | solution.py:52
  88.7 23.2 %collective-permute-start.16 = (bf16[1280,256]{1,0:T(8,128)(2,1)S(1)}, bf16[1280,256]{1,0:T(8,128)(2,1)S(1)}, u32[]{:S(2)}, u32[]{:S(2)}) collective-permute-start(bf16[1280,256]{1,0:T(8,128)(2,1)S(1)} %shard_map.107), channel_id=1, source_target_pairs={{64,0},{128,64},{192,128},{0,192},{65,1},{129,65},{193,129},{1,193... | collective-permute-start | bytes 1966088 | tf_op jit(solution)/shard_map/ppermute | solution.py:52
  113.7 47.6 %copy-start.2 = (bf16[1024,128]{1,0:T(8,128)(2,1)S(1)}, bf16[1024,128]{1,0:T(8,128)(2,1)}, u32[]{:S(2)}) copy-start(bf16[1024,128]{1,0:T(8,128)(2,1)} %w_ref.3) | copy-start | bytes 786436
  162.0 4.6 %collective-permute-start.19 = (f32[40,128]{1,0:T(8,128)S(1)}, f32[40,128]{1,0:T(8,128)S(1)}, u32[]{:S(2)}, u32[]{:S(2)}) collective-permute-start(f32[40,128]{1,0:T(8,128)S(1)} %shard_map.113.own_ref), channel_id=1, source_target_pairs={{0,1},{1,0},{2,3},{3,2},{4,5},{5,4},{6,7},{7,6},{8,9},{9,8},{10,11... | collective-permute-start | bytes 61448 | tf_op jit(solution)/shard_map/ppermute | solution.py:428
Sparse Core Ops, SparseCore 0:
  10.6 106.6 all-gather.1
